TPU v7x, 256 devices: a whole 4x4x8 slice. The times are simulated.
256 devices in a mesh: group: 16 (over z, core), tp: 16 (over y, x).
Axes of the slice: x: 4, y: 4, z: 8, core: 2. Of those that a mesh axis runs over, the one named last changes fastest.
Arguments:
- hidden: bfloat16 [2, 2048, 8192], P(None, 'group'), may hold values from -6 to 6
- w_query: bfloat16 [8192, 4096], P(None, 'tp'), may hold values from -0.0625 to 0.0625
- w_key: bfloat16 [8192, 512], P(None, 'tp'), may hold values from -0.0625 to 0.0625
- w_value: bfloat16 [8192, 512], P(None, 'tp'), may hold values from -0.0625 to 0.0625
- w_out: bfloat16 [4096, 8192], P('tp'), may hold values from -0.09375 to 0.09375
- key_cache: bfloat16 [2048, 512, 512], P(('group', 'tp')), may hold values from -80 to 80
- value_cache: bfloat16 [2048, 512, 512], P(('group', 'tp')), may hold values from -6 to 6
- lengths: int32 [2048], P(('group', 'tp')), may hold values from 1 to 510, as said below
- row_slot: int32 [2, 2048], P(None, 'group'), may hold values from 0 to 12, as said below
- evict_slot: int32 [2, 192], replicated, may hold values from 0 to 12, as said below
- evict_adapter: int32 [2, 192], replicated, may hold values from 0 to 191, as said below
- owner: int32 [192], replicated, may hold values from 0 to 191, as said below
- pool_a_in: bfloat16 [192, 48, 8192], P('group', None, 'tp'), may hold values from -0.0625 to 0.0625
- pool_b_q: bfloat16 [192, 16, 4096], P('group', None, 'tp'), may hold values from -1.5 to 1.5
- pool_b_k: bfloat16 [192, 16, 512], P('group', None, 'tp'), may hold values from -1.5 to 1.5
- pool_b_v: bfloat16 [192, 16, 512], P('group', None, 'tp'), may hold values from -1.5 to 1.5
- pool_a_o: bfloat16 [192, 16, 4096], P('group', None, 'tp'), may hold values from -0.09375 to 0.09375
- pool_b_o: bfloat16 [192, 16, 8192], P('group', None, 'tp'), may hold values from -1.5 to 1.5
- slot_a_in: bfloat16 [208, 48, 8192], P('group', None, 'tp'), may hold values from -0.0625 to 0.0625
- slot_b_q: bfloat16 [208, 16, 4096], P('group', None, 'tp'), may hold values from -1.5 to 1.5
- slot_b_k: bfloat16 [208, 16, 512], P('group', None, 'tp'), may hold values from -1.5 to 1.5
- slot_b_v: bfloat16 [208, 16, 512], P('group', None, 'tp'), may hold values from -1.5 to 1.5
- slot_a_o: bfloat16 [208, 16, 4096], P('group', None, 'tp'), may hold values from -0.09375 to 0.09375
- slot_b_o: bfloat16 [208, 16, 8192], P('group', None, 'tp'), may hold values from -1.5 to 1.5
Outputs:
- attn_out: bfloat16 [2, 2048, 8192], P(None, 'group', 'tp')
Inputs may be any that keep to these rules, and one draw needn't show every extreme that they name: `lengths`: one row of each replica has exactly 510. `row_slot`: at each step every one of a replica's 13 slots is used by some row of that replica. `evict_slot`: the 12 slots one replica refills in a step are distinct. `evict_adapter`: the adapters one replica loads in a step are distinct; at most 2 of them have pool positions held by any one replica (position p is held by replica p // 12), and exactly 2 for some replica, at every replica and step. `owner`: A permutation.
All inputs are finite; a program needn't handle non-finite values.
Results may differ from a plain program's by a relative error of at most 0.013.
Values may be sent and summed in bfloat16 or wider, within the bound.
No kernel may reach another device: no remote copies, remote signals or barrier semaphores. Data moves between devices by JAX's collectives and lax.ppermute only.
A program may use at most 128 MiB of HBM per device.

v0:
```python
import math

import jax
import jax.numpy as jnp
from jax import lax
from jax.sharding import PartitionSpec as P

QH = 32
KH = 4
HD = 128
CAP = 2


low_rank_scale = 0.5


def select_rows(onehot, pieces):
    picked = []
    for piece in pieces:
        flat = piece.reshape(piece.shape[0], -1)
        mixed = jnp.dot(onehot, flat, preferred_element_type=jnp.float32)
        picked.append(mixed.astype(jnp.bfloat16).reshape((onehot.shape[0],) + piece.shape[1:]))
    return tuple(picked)


def locate(wanted, owner):
    table = jnp.arange(owner.shape[0], dtype=jnp.int32)
    match = wanted[..., None] == table
    return jnp.sum(jnp.where(match, owner, 0), axis=-1)


def project(tokens, weight, shrunk, adapter_output):
    base_contribution = jnp.dot(tokens, weight, preferred_element_type=jnp.float32)
    adapter_delta = jnp.einsum(
        "rk,rkc->rc", shrunk, adapter_output, preferred_element_type=jnp.float32
    )
    return (base_contribution + low_rank_scale * adapter_delta).astype(jnp.bfloat16)


def shards(
    hidden,
    w_query,
    w_key,
    w_value,
    w_out,
    key_cache,
    value_cache,
    lengths,
    row_slot,
    evict_slot,
    evict_adapter,
    owner,
    pool_a_in,
    pool_b_q,
    pool_b_k,
    pool_b_v,
    pool_a_o,
    pool_b_o,
    slot_a_in,
    slot_b_q,
    slot_b_k,
    slot_b_v,
    slot_a_o,
    slot_b_o,
):
    group_count = lax.axis_size("group")
    my_group = lax.axis_index("group")
    my_part = lax.axis_index("tp")
    step_count = hidden.shape[0]
    held_count = pool_a_in.shape[0]
    slot_count = slot_a_in.shape[0]
    load_count = evict_slot.shape[1] // group_count
    rank_size = pool_b_q.shape[1]
    in_width = pool_a_in.shape[2]
    out_width = pool_b_o.shape[2]
    local_rows = key_cache.shape[0]
    cache_length = key_cache.shape[1]
    score_scale = 1.0 / math.sqrt(HD)
    pool_arrays = (pool_a_in, pool_b_q, pool_b_k, pool_b_v, pool_a_o, pool_b_o)
    stored = (slot_a_in, slot_b_q, slot_b_k, slot_b_v, slot_a_o, slot_b_o)
    position = locate(evict_adapter, owner)
    source = (position // held_count).reshape(step_count, group_count, load_count)
    local_index = (position % held_count).reshape(step_count, group_count, load_count)
    load_order = jnp.arange(load_count)
    earlier = load_order[:, None] < load_order[None, :]
    same_source = source[:, :, :, None] == source[:, :, None, :]
    load_rank = jnp.sum(same_source & earlier, axis=2)

    def send_table(step):
        from_me = source[step] == my_group
        hits = (
            from_me[:, :, None, None]
            & (load_rank[step][:, :, None, None] == jnp.arange(CAP)[:, None])
            & (local_index[step][:, :, None, None] == jnp.arange(held_count))
        )
        return jnp.sum(hits, axis=1).astype(jnp.bfloat16)

    def outgoing(step_list):
        table = jnp.concatenate([send_table(step) for step in step_list], axis=1)
        table = table.reshape(group_count * len(step_list) * CAP, held_count)
        return select_rows(table, pool_arrays)

    cached_keys = key_cache
    cached_values = value_cache
    positions = jnp.arange(cache_length, dtype=jnp.int32)
    step_outputs = []
    for step in range(step_count):
        sent_now = outgoing([step])
        arrived_now = (
            lax.all_to_all(sent_now[0], "group", split_axis=0, concat_axis=0, tiled=True),
            lax.all_to_all(sent_now[1], "group", split_axis=0, concat_axis=0, tiled=True),
            lax.all_to_all(sent_now[2], "group", split_axis=0, concat_axis=0, tiled=True),
            lax.all_to_all(sent_now[3], "group", split_axis=0, concat_axis=0, tiled=True),
            lax.all_to_all(sent_now[4], "group", split_axis=0, concat_axis=0, tiled=True),
            lax.all_to_all(sent_now[5], "group", split_axis=0, concat_axis=0, tiled=True),
        )
        my_source = lax.dynamic_index_in_dim(source[step], my_group, 0, keepdims=False)
        my_rank = lax.dynamic_index_in_dim(load_rank[step], my_group, 0, keepdims=False)
        wanted_row = my_source * (1 * CAP) + 0 * CAP + my_rank
        onehot = (wanted_row[:, None] == jnp.arange(group_count * 1 * CAP)).astype(jnp.bfloat16)
        loaded = select_rows(onehot, arrived_now)
        targets = lax.dynamic_slice_in_dim(evict_slot[step], my_group * load_count, load_count, 0)
        placing = targets[None, :] == jnp.arange(slot_count)[:, None]
        replaced = select_rows(placing.astype(jnp.bfloat16), loaded)
        refilled = jnp.any(placing, axis=1)
        stored = tuple(
            (
                jnp.where(refilled.reshape((slot_count,) + (1,) * (older.ndim - 1)), newer, older)
                for newer, older in zip(replaced, stored)
            )
        )
        users = (row_slot[step][:, None] == jnp.arange(slot_count)).astype(jnp.bfloat16)
        a_in, b_q, b_k, b_v, a_o, b_o = select_rows(users, stored)
        tokens = hidden[step]
        tokens_part = lax.dynamic_slice_in_dim(tokens, my_part * in_width, in_width, 1)
        partial_in = jnp.einsum("rd,rkd->rk", tokens_part, a_in, preferred_element_type=jnp.float32)
        shrunk = lax.psum(partial_in, "tp").astype(jnp.bfloat16)
        query = project(tokens, w_query, shrunk[:, :rank_size], b_q)
        key_new = project(tokens, w_key, shrunk[:, rank_size : 2 * rank_size], b_k)
        value_new = project(tokens, w_value, shrunk[:, 2 * rank_size :], b_v)
        query_rows, key_rows, value_rows = (
            lax.all_to_all(query, "tp", split_axis=0, concat_axis=1, tiled=True),
            lax.all_to_all(key_new, "tp", split_axis=0, concat_axis=1, tiled=True),
            lax.all_to_all(value_new, "tp", split_axis=0, concat_axis=1, tiled=True),
        )
        spot = lengths + step
        fresh = (positions[None, :] == spot[:, None])[:, :, None]
        cached_keys = jnp.where(fresh, key_rows[:, None, :], cached_keys)
        cached_values = jnp.where(fresh, value_rows[:, None, :], cached_values)
        query_heads = query_rows.reshape(local_rows, KH, QH // KH, HD)
        key_heads = cached_keys.reshape(local_rows, cache_length, KH, HD)
        value_heads = cached_values.reshape(local_rows, cache_length, KH, HD).astype(jnp.float32)
        scores = (
            jnp.einsum(
                "rkgc,rlkc->rkgl", query_heads, key_heads, preferred_element_type=jnp.float32
            )
            * score_scale
        )
        visible = (positions[None, :] <= spot[:, None])[:, None, None, :]
        scores = jnp.where(visible, scores, -jnp.inf)
        highest = jnp.max(scores, axis=-1, keepdims=True)
        weights = jnp.exp(scores - highest)
        totals = jnp.sum(weights, axis=-1, keepdims=True)
        mixed = jnp.einsum("rkgl,rlkc->rkgc", weights, value_heads)
        attended = (mixed / totals).reshape(local_rows, QH * HD).astype(jnp.bfloat16)
        head_rows = lax.all_to_all(attended, "tp", split_axis=1, concat_axis=0, tiled=True)
        base_output = jnp.dot(head_rows, w_out, preferred_element_type=jnp.float32)
        shrink_part = jnp.einsum("rc,rkc->rk", head_rows, a_o, preferred_element_type=jnp.float32)
        summed_out, shrunk_out = lax.psum((base_output, shrink_part), "tp")
        local_column_share = lax.dynamic_slice_in_dim(summed_out, my_part * out_width, out_width, 1)
        adapter_output = jnp.einsum(
            "rk,rkc->rc", shrunk_out.astype(jnp.bfloat16), b_o, preferred_element_type=jnp.float32
        )
        step_outputs.append(
            (local_column_share + low_rank_scale * adapter_output).astype(jnp.bfloat16)
        )
    return jnp.stack(step_outputs)


def solution(mesh):
    placed = (
        P(None, "group", None),
        P(None, "tp"),
        P(None, "tp"),
        P(None, "tp"),
        P("tp", None),
        P(("group", "tp"), None, None),
        P(("group", "tp"), None, None),
        P(("group", "tp")),
        P(None, "group"),
        P(),
        P(),
        P(),
        P("group", None, "tp"),
        P("group", None, "tp"),
        P("group", None, "tp"),
        P("group", None, "tp"),
        P("group", None, "tp"),
        P("group", None, "tp"),
        P("group", None, "tp"),
        P("group", None, "tp"),
        P("group", None, "tp"),
        P("group", None, "tp"),
        P("group", None, "tp"),
        P("group", None, "tp"),
    )
    return jax.shard_map(
        shards, mesh=mesh, in_specs=placed, out_specs=P(None, "group", "tp"), check_vma=False
    )
```

profile of v0, /device:TPU:32, one launch (start us, length us, event | category | flops | bytes accessed | tf_op | source)
XLA Modules:
  0.0 576.1 jit_solution(18405698610719454795)
XLA Ops:
  11.1 8.6 %all-to-all-start.3 = ((bf16[16,2,512]{2,1,0:T(2,128)(2,1)}), bf16[16,2,512]{2,1,0:T(2,128)(2,1)S(1)}, u32[]{:S(2)}, u32[]{:S(2)}) async-start(bf16[16,2,512]{2,1,0:T(2,128)(2,1)} %reshape.695), calls=%async_computation.3 | async-start | bytes 65536 | tf_op jit(solution)/shard_map/all_to_all | solution.py:112
  31.8 5.3 all-to-all-done.5
  37.1 4.8 all-to-all-start.13
  48.3 4.8 all-to-all-start.15
  54.0 5.4 all-to-all-done.15
  59.4 4.8 all-to-all-start.8
  65.3 8.7 %all-to-all-done.8 = bf16[32,16,256]{2,1,0:T(8,128)(2,1)S(1)} async-done(((bf16[32,16,256]{2,1,0:T(8,128)(2,1)}), bf16[32,16,256]{2,1,0:T(8,128)(2,1)S(1)}, u32[]{:S(2)}, u32[]{:S(2)}) %all-to-all-start.8) | async-done | bytes 262176 | tf_op jit(solution)/shard_map/all_to_all | solution.py:114
  74.0 4.9 all-to-all-start.1
  79.8 8.9 %all-to-all-done.1 = bf16[32,16,256]{2,1,0:T(8,128)(2,1)S(1)} async-done(((bf16[32,16,256]{2,1,0:T(8,128)(2,1)}), bf16[32,16,256]{2,1,0:T(8,128)(2,1)S(1)}, u32[]{:S(2)}, u32[]{:S(2)}) %all-to-all-start.1) | async-done | bytes 262176 | tf_op jit(solution)/shard_map/all_to_all | solution.py:111
  88.8 4.9 all-to-all-start.11
  94.6 9.0 %all-to-all-done.11 = bf16[32,16,256]{2,1,0:T(8,128)(2,1)S(1)} async-done(((bf16[32,16,256]{2,1,0:T(8,128)(2,1)}), bf16[32,16,256]{2,1,0:T(8,128)(2,1)S(1)}, u32[]{:S(2)}, u32[]{:S(2)}) %all-to-all-start.11) | async-done | bytes 262176 | tf_op jit(solution)/shard_map/all_to_all | solution.py:111
  103.6 5.0 all-to-all-start.18
  119.1 5.1 all-to-all-start
  137.7 22.6 %all-to-all-done = bf16[32,48,512]{2,1,0:T(8,128)(2,1)S(1)} async-done(((bf16[32,48,512]{2,1,0:T(8,128)(2,1)}), bf16[32,48,512]{2,1,0:T(8,128)(2,1)S(1)}, u32[]{:S(2)}, u32[]{:S(2)}) %all-to-all-start) | async-done | bytes 1572896 | tf_op jit(solution)/shard_map/all_to_all | solution.py:110
  160.3 7.0 %all-to-all-start.10 = ((bf16[32,48,512]{2,1,0:T(8,128)(2,1)}), bf16[32,48,512]{2,1,0:T(8,128)(2,1)}, u32[]{:S(2)}, u32[]{:S(2)}) async-start(bf16[32,48,512]{2,1,0:T(8,128)(2,1)} %bitcast.377), calls=%async_computation.10 | async-start | bytes 3145728 | tf_op jit(solution)/shard_map/all_to_all | solution.py:110
  189.5 13.8 %all-to-all-done.10 = bf16[32,48,512]{2,1,0:T(8,128)(2,1)} async-done(((bf16[32,48,512]{2,1,0:T(8,128)(2,1)}), bf16[32,48,512]{2,1,0:T(8,128)(2,1)}, u32[]{:S(2)}, u32[]{:S(2)}) %all-to-all-start.10) | async-done | bytes 1572896 | tf_op jit(solution)/shard_map/all_to_all | solution.py:110
  224.2 76.2 %all-reduce.1 = (bf16[128,48]{1,0:T(8,128)(2,1)S(1)}, bf16[128,48]{1,0:T(8,128)(2,1)S(1)}) all-reduce(f32[128,48]{1,0:T(8,128)} %bitcast.481, f32[128,48]{1,0:T(8,128)} %bitcast.483), channel_id=1, replica_groups=mesh['group'=16,'tp'=16] {'tp'}, use_global_device_ids=true, to_apply=%region_11.12 | all-reduce | flops 12288 | bytes 73728 | tf_op jit(solution)/shard_map/psum | solution.py:137
  319.6 7.2 %all-to-all-start.4 = ((bf16[16,2,128]{2,1,0:T(2,128)(2,1)}), bf16[16,2,128]{2,1,0:T(2,128)(2,1)S(1)}, u32[]{:S(2)}, u32[]{:S(2)}) async-start(bf16[16,2,128]{2,1,0:T(2,128)(2,1)} %reshape.699), calls=%async_computation.4 | async-start | bytes 16384 | tf_op jit(solution)/shard_map/all_to_all | solution.py:143
  338.9 6.2 %all-to-all-done.16 = bf16[16,2,128]{2,1,0:T(2,128)(2,1)S(1)} async-done(((bf16[16,2,128]{2,1,0:T(2,128)(2,1)}), bf16[16,2,128]{2,1,0:T(2,128)(2,1)S(1)}, u32[]{:S(2)}, u32[]{:S(2)}) %all-to-all-start.16) | async-done | bytes 8224 | tf_op jit(solution)/shard_map/all_to_all | solution.py:144
  356.0 5.0 all-to-all-start.2
  361.2 9.7 %fusion.13 = (bf16[8,64,4,8,128]{4,3,2,1,0:T(8,128)(2,1)}, bf16[8,64,4,8,128]{4,3,2,1,0:T(8,128)(2,1)}, bf16[8,64,4,8,128]{4,3,2,1,0:T(8,128)(2,1)}, bf16[8,64,4,8,128]{4,3,2,1,0:T(8,128)(2,1)}) fusion(bf16[8,512,512]{2,1,0:T(8,128)(2,1)} %param.30, pred[8,512]{1,0:T(8,128)(4,1)S(1)} %copy-done.32, bf16[8,512]{1,0:T(8,128)(2,1)S(1)} %broadcast_in_dim.189, ...), kind=kLoop, calls=%fused_computation.49 | loop fusion | flops 8388608 | bytes 25206784
  370.9 7.2 %all-to-all-start.12 = ((bf16[16,8,256]{2,1,0:T(8,128)(2,1)}), bf16[16,8,256]{2,1,0:T(8,128)(2,1)S(1)}, u32[]{:S(2)}, u32[]{:S(2)}) async-start(bf16[16,8,256]{2,1,0:T(8,128)(2,1)} %fusion.65), calls=%async_computation.12 | async-start | bytes 131072 | tf_op jit(solution)/shard_map/all_to_all | solution.py:142
  385.8 4.9 all-to-all-start.7
  398.4 4.9 all-to-all-start.17
  403.4 4.9 fusion.115
  411.0 4.8 fusion.113
  418.3 6.6 %all-to-all-start.9 = ((bf16[32,16,512]{2,1,0:T(8,128)(2,1)}), bf16[32,16,512]{2,1,0:T(8,128)(2,1)S(1)}, u32[]{:S(2)}, u32[]{:S(2)}) async-start(bf16[32,16,512]{2,1,0:T(8,128)(2,1)} %bitcast.118), calls=%async_computation.9 | async-start | bytes 1048576 | tf_op jit(solution)/shard_map/all_to_all | solution.py:115
  426.1 13.1 %all-to-all-done.9 = bf16[32,16,512]{2,1,0:T(8,128)(2,1)S(1)} async-done(((bf16[32,16,512]{2,1,0:T(8,128)(2,1)}), bf16[32,16,512]{2,1,0:T(8,128)(2,1)S(1)}, u32[]{:S(2)}, u32[]{:S(2)}) %all-to-all-start.9) | async-done | bytes 524320 | tf_op jit(solution)/shard_map/all_to_all | solution.py:115
  439.2 6.1 %all-to-all-start.19 = ((bf16[32,16,512]{2,1,0:T(8,128)(2,1)}), bf16[32,16,512]{2,1,0:T(8,128)(2,1)S(1)}, u32[]{:S(2)}, u32[]{:S(2)}) async-start(bf16[32,16,512]{2,1,0:T(8,128)(2,1)} %bitcast.167), calls=%async_computation.19 | async-start | bytes 1048576 | tf_op jit(solution)/shard_map/all_to_all | solution.py:115
  449.8 10.1 %all-to-all-done.19 = bf16[32,16,512]{2,1,0:T(8,128)(2,1)S(1)} async-done(((bf16[32,16,512]{2,1,0:T(8,128)(2,1)}), bf16[32,16,512]{2,1,0:T(8,128)(2,1)S(1)}, u32[]{:S(2)}, u32[]{:S(2)}) %all-to-all-start.19) | async-done | bytes 524320 | tf_op jit(solution)/shard_map/all_to_all | solution.py:115
  466.5 73.7 %all-reduce = (bf16[128,16]{1,0:T(8,128)(2,1)S(1)}, bf16[128,16]{1,0:T(8,128)(2,1)S(1)}) all-reduce(f32[128,16]{1,0:T(8,128)S(1)} %bitcast.484, f32[128,16]{1,0:T(8,128)S(1)} %bitcast.482), channel_id=1, replica_groups=mesh['group'=16,'tp'=16] {'tp'}, use_global_device_ids=true, to_apply=%region_15.16 | all-reduce | flops 4096 | bytes 24576 | tf_op jit(solution)/shard_map/psum | solution.py:169
  542.7 23.7 %all-reduce.5.cloned.1.call-done = (f32[128,8192]{1,0:T(8,128)}, f32[128,8192]{1,0:T(8,128)}) async-done(((f32[128,8192]{1,0:T(8,128)}, f32[128,8192]{1,0:T(8,128)}), (f32[128,8192]{1,0:T(8,128)}, f32[128,8192]{1,0:T(8,128)})) %all-reduce.5.cloned.1.call-update) | async-done | bytes 8388624 | tf_op jit(solution)/shard_map/psum | solution.py:169
  (366 shorter events, 172.8 us)
Async XLA Ops:
  6.5 295.0 %copy-start = (bf16[8192,32]{0,1:T(8,128)(2,1)S(1)}, bf16[8192,32]{0,1:T(8,128)(2,1)}, u32[]{:S(2)}) copy-start(bf16[8192,32]{0,1:T(8,128)(2,1)} %param.26) | copy-start | bytes 1572868
  6.5 57.7 %copy-start.27 = (bf16[12,16,256]{2,1,0:T(8,128)(2,1)S(1)}, bf16[12,16,256]{2,1,0:T(8,128)(2,1)}, u32[]{:S(2)}) copy-start(bf16[12,16,256]{2,1,0:T(8,128)(2,1)} %param.37) | copy-start | bytes 294916
  8.2 65.8 %copy-start.28 = (s32[1,16,12]{1,0,2:T(1,128)}, s32[1,16,12]{1,0,2:T(1,128)S(1)}, u32[]{:S(2)}) copy-start(s32[1,16,12]{1,0,2:T(1,128)S(1)} %get-tuple-element.42) | copy-start | bytes 2308
  11.1 14.9 %all-to-all-start.3 = ((bf16[16,2,512]{2,1,0:T(2,128)(2,1)}), bf16[16,2,512]{2,1,0:T(2,128)(2,1)S(1)}, u32[]{:S(2)}, u32[]{:S(2)}) async-start(bf16[16,2,512]{2,1,0:T(2,128)(2,1)} %reshape.695), calls=%async_computation.3 | async-start | bytes 65536 | tf_op jit(solution)/shard_map/all_to_all | solution.py:112
  26.0 11.1 %all-to-all-start.5 = ((bf16[16,2,512]{2,1,0:T(2,128)(2,1)}), bf16[16,2,512]{2,1,0:T(2,128)(2,1)S(1)}, u32[]{:S(2)}, u32[]{:S(2)}) async-start(bf16[16,2,512]{2,1,0:T(2,128)(2,1)} %reshape.687), calls=%async_computation.5 | async-start | bytes 65536 | tf_op jit(solution)/shard_map/all_to_all | solution.py:113
  37.1 11.2 %all-to-all-start.13 = ((bf16[16,2,512]{2,1,0:T(2,128)(2,1)}), bf16[16,2,512]{2,1,0:T(2,128)(2,1)S(1)}, u32[]{:S(2)}, u32[]{:S(2)}) async-start(bf16[16,2,512]{2,1,0:T(2,128)(2,1)} %reshape.693), calls=%async_computation.13 | async-start | bytes 65536 | tf_op jit(solution)/shard_map/all_to_all | solution.py:112
  48.2 65.1 %copy-start.22 = (bf16[16,2,512]{2,1,0:T(2,128)(2,1)}, bf16[16,2,512]{2,1,0:T(2,128)(2,1)S(1)}, u32[]{:S(2)}) copy-start(bf16[16,2,512]{2,1,0:T(2,128)(2,1)S(1)} %all-to-all-done.13) | copy-start | bytes 98308
  48.3 11.1 %all-to-all-start.15 = ((bf16[16,2,512]{2,1,0:T(2,128)(2,1)}), bf16[16,2,512]{2,1,0:T(2,128)(2,1)S(1)}, u32[]{:S(2)}, u32[]{:S(2)}) async-start(bf16[16,2,512]{2,1,0:T(2,128)(2,1)} %reshape.685), calls=%async_computation.15 | async-start | bytes 65536 | tf_op jit(solution)/shard_map/all_to_all | solution.py:113
  59.4 14.6 %all-to-all-start.8 = ((bf16[32,16,256]{2,1,0:T(8,128)(2,1)}), bf16[32,16,256]{2,1,0:T(8,128)(2,1)S(1)}, u32[]{:S(2)}, u32[]{:S(2)}) async-start(bf16[32,16,256]{2,1,0:T(8,128)(2,1)} %bitcast.103), calls=%async_computation.8 | async-start | bytes 524288 | tf_op jit(solution)/shard_map/all_to_all | solution.py:114
  74.0 14.8 %all-to-all-start.1 = ((bf16[32,16,256]{2,1,0:T(8,128)(2,1)}), bf16[32,16,256]{2,1,0:T(8,128)(2,1)S(1)}, u32[]{:S(2)}, u32[]{:S(2)}) async-start(bf16[32,16,256]{2,1,0:T(8,128)(2,1)} %bitcast.87), calls=%async_computation.1 | async-start | bytes 524288 | tf_op jit(solution)/shard_map/all_to_all | solution.py:111
  88.8 14.8 %all-to-all-start.11 = ((bf16[32,16,256]{2,1,0:T(8,128)(2,1)}), bf16[32,16,256]{2,1,0:T(8,128)(2,1)S(1)}, u32[]{:S(2)}, u32[]{:S(2)}) async-start(bf16[32,16,256]{2,1,0:T(8,128)(2,1)} %bitcast.142), calls=%async_computation.11 | async-start | bytes 524288 | tf_op jit(solution)/shard_map/all_to_all | solution.py:111
  103.6 14.8 %all-to-all-start.18 = ((bf16[32,16,256]{2,1,0:T(8,128)(2,1)}), bf16[32,16,256]{2,1,0:T(8,128)(2,1)S(1)}, u32[]{:S(2)}, u32[]{:S(2)}) async-start(bf16[32,16,256]{2,1,0:T(8,128)(2,1)} %bitcast.155), calls=%async_computation.18 | async-start | bytes 524288 | tf_op jit(solution)/shard_map/all_to_all | solution.py:114
  119.1 41.2 %all-to-all-start = ((bf16[32,48,512]{2,1,0:T(8,128)(2,1)}), bf16[32,48,512]{2,1,0:T(8,128)(2,1)S(1)}, u32[]{:S(2)}, u32[]{:S(2)}) async-start(bf16[32,48,512]{2,1,0:T(8,128)(2,1)} %bitcast.378), calls=%async_computation | async-start | bytes 3145728 | tf_op jit(solution)/shard_map/all_to_all | solution.py:110
  130.0 30.3 %copy-start.36 = (s32[12]{0:T(128)}, s32[12]{0:T(128)S(1)}, u32[]{:S(2)}) copy-start(s32[12]{0:T(128)S(1)} %get-tuple-element.68) | copy-start | bytes 148
  130.2 39.7 %copy-start.48 = (pred[13]{0:T(512)(128)(4,1)}, pred[13]{0:T(512)(128)(4,1)S(1)}, u32[]{:S(2)}) copy-start(pred[13]{0:T(512)(128)(4,1)S(1)} %fusion.137) | copy-start | bytes 43
  130.3 39.6 %copy-start.52 = (pred[13]{0:T(512)(128)(4,1)}, pred[13]{0:T(512)(128)(4,1)S(1)}, u32[]{:S(2)}) copy-start(pred[13]{0:T(512)(128)(4,1)S(1)} %fusion.138) | copy-start | bytes 43
  136.9 40.4 %copy-start.10 = (bf16[32,16,256]{2,1,0:T(8,128)(2,1)S(1)}, bf16[32,16,256]{2,1,0:T(8,128)(2,1)}, u32[]{:S(2)}) copy-start(bf16[32,16,256]{2,1,0:T(8,128)(2,1)} %copy-done.9) | copy-start | bytes 786436
  160.3 43.0 %all-to-all-start.10 = ((bf16[32,48,512]{2,1,0:T(8,128)(2,1)}), bf16[32,48,512]{2,1,0:T(8,128)(2,1)}, u32[]{:S(2)}, u32[]{:S(2)}) async-start(bf16[32,48,512]{2,1,0:T(8,128)(2,1)} %bitcast.377), calls=%async_computation.10 | async-start | bytes 3145728 | tf_op jit(solution)/shard_map/all_to_all | solution.py:110
  224.2 87.8 %copy-start.16 = (bf16[128,512]{0,1:T(8,128)(2,1)S(1)}, bf16[128,512]{0,1:T(8,128)(2,1)}, u32[]{:S(2)}) copy-start(bf16[128,512]{0,1:T(8,128)(2,1)} %copy.100) | copy-start | bytes 393220
  224.2 87.9 %copy-start.58 = (bf16[8192,32]{0,1:T(8,128)(2,1)S(1)}, bf16[8192,32]{0,1:T(8,128)(2,1)}, u32[]{:S(2)}) copy-start(bf16[8192,32]{0,1:T(8,128)(2,1)} %param.27) | copy-start | bytes 1572868
  304.9 14.7 %all-to-all-start.14 = ((bf16[16,2,128]{2,1,0:T(2,128)(2,1)}), bf16[16,2,128]{2,1,0:T(2,128)(2,1)S(1)}, u32[]{:S(2)}, u32[]{:S(2)}) async-start(bf16[16,2,128]{2,1,0:T(2,128)(2,1)} %reshape.697), calls=%async_computation.14 | async-start | bytes 16384 | tf_op jit(solution)/shard_map/all_to_all | solution.py:143
  319.6 14.7 %all-to-all-start.4 = ((bf16[16,2,128]{2,1,0:T(2,128)(2,1)}), bf16[16,2,128]{2,1,0:T(2,128)(2,1)S(1)}, u32[]{:S(2)}, u32[]{:S(2)}) async-start(bf16[16,2,128]{2,1,0:T(2,128)(2,1)} %reshape.699), calls=%async_computation.4 | async-start | bytes 16384 | tf_op jit(solution)/shard_map/all_to_all | solution.py:143
  334.3 10.8 %all-to-all-start.16 = ((bf16[16,2,128]{2,1,0:T(2,128)(2,1)}), bf16[16,2,128]{2,1,0:T(2,128)(2,1)S(1)}, u32[]{:S(2)}, u32[]{:S(2)}) async-start(bf16[16,2,128]{2,1,0:T(2,128)(2,1)} %reshape.689), calls=%async_computation.16 | async-start | bytes 16384 | tf_op jit(solution)/shard_map/all_to_all | solution.py:144
  345.1 10.8 %all-to-all-start.6 = ((bf16[16,2,128]{2,1,0:T(2,128)(2,1)}), bf16[16,2,128]{2,1,0:T(2,128)(2,1)S(1)}, u32[]{:S(2)}, u32[]{:S(2)}) async-start(bf16[16,2,128]{2,1,0:T(2,128)(2,1)} %reshape.691), calls=%async_computation.6 | async-start | bytes 16384 | tf_op jit(solution)/shard_map/all_to_all | solution.py:144
  356.0 14.9 %all-to-all-start.2 = ((bf16[16,8,256]{2,1,0:T(8,128)(2,1)}), bf16[16,8,256]{2,1,0:T(8,128)(2,1)S(1)}, u32[]{:S(2)}, u32[]{:S(2)}) async-start(bf16[16,8,256]{2,1,0:T(8,128)(2,1)} %fusion.62), calls=%async_computation.2 | async-start | bytes 131072 | tf_op jit(solution)/shard_map/all_to_all | solution.py:142
  370.9 14.9 %all-to-all-start.12 = ((bf16[16,8,256]{2,1,0:T(8,128)(2,1)}), bf16[16,8,256]{2,1,0:T(8,128)(2,1)S(1)}, u32[]{:S(2)}, u32[]{:S(2)}) async-start(bf16[16,8,256]{2,1,0:T(8,128)(2,1)} %fusion.65), calls=%async_computation.12 | async-start | bytes 131072 | tf_op jit(solution)/shard_map/all_to_all | solution.py:142
  385.8 12.6 %all-to-all-start.7 = ((bf16[8,16,256]{2,0,1:T(8,128)(2,1)}), bf16[8,16,256]{2,0,1:T(8,128)(2,1)S(1)}, u32[]{:S(2)}, u32[]{:S(2)}) async-start(bf16[8,16,256]{2,0,1:T(8,128)(2,1)} %copy.91), calls=%async_computation.7 | async-start | bytes 131072 | tf_op jit(solution)/shard_map/all_to_all | solution.py:166
  398.4 12.6 %all-to-all-start.17 = ((bf16[8,16,256]{2,0,1:T(8,128)(2,1)}), bf16[8,16,256]{2,0,1:T(8,128)(2,1)S(1)}, u32[]{:S(2)}, u32[]{:S(2)}) async-start(bf16[8,16,256]{2,0,1:T(8,128)(2,1)} %copy.104), calls=%async_computation.17 | async-start | bytes 131072 | tf_op jit(solution)/shard_map/all_to_all | solution.py:166
  403.4 163.0 %all-reduce.5.cloned.1.call-start = ((), (), s32[]{:S(2)}) async-start(), calls=%async_computation.20 | async-start | bytes 16777216 | tf_op jit(solution)/shard_map/psum | solution.py:169
  418.3 21.0 %all-to-all-start.9 = ((bf16[32,16,512]{2,1,0:T(8,128)(2,1)}), bf16[32,16,512]{2,1,0:T(8,128)(2,1)S(1)}, u32[]{:S(2)}, u32[]{:S(2)}) async-start(bf16[32,16,512]{2,1,0:T(8,128)(2,1)} %bitcast.118), calls=%async_computation.9 | async-start | bytes 1048576 | tf_op jit(solution)/shard_map/all_to_all | solution.py:115
  439.2 20.7 %all-to-all-start.19 = ((bf16[32,16,512]{2,1,0:T(8,128)(2,1)}), bf16[32,16,512]{2,1,0:T(8,128)(2,1)S(1)}, u32[]{:S(2)}, u32[]{:S(2)}) async-start(bf16[32,16,512]{2,1,0:T(8,128)(2,1)} %bitcast.167), calls=%async_computation.19 | async-start | bytes 1048576 | tf_op jit(solution)/shard_map/all_to_all | solution.py:115
  465.8 103.3 %copy-start.1 = (bf16[8192,32]{0,1:T(8,128)(2,1)S(1)}, bf16[8192,32]{0,1:T(8,128)(2,1)}, u32[]{:S(2)}) copy-start(bf16[8192,32]{0,1:T(8,128)(2,1)} %param.26) | copy-start | bytes 1572868
  (48 other events, 497.2 us)
Sparse Core Ops, SparseCore 0:
  416.0 150.2 all-reduce.4
where the time goes:
time: 587 us; the launch traced here: 576 us
  waiting for transfers between devices  151 us (26%)
  blocking collectives  150 us (26%)
  starting transfers between devices  107 us (18%)
  matrix products  66.5 us (11%)
  local copies, waits for them, and re-layouts  61.6 us (10%)
  other arithmetic  24.4 us (4%)
  between operations  15.1 us (3%)
    psum x1, blocking collectives, shards(): shrunk = lax.psum(partial_in, 'tp').astype(jnp.bfloat16)  76.2 us
    psum x1, blocking collectives, shards(): summed_out, shrunk_out = lax.psum((base_output, shrink_part), 'tp')  73.7 us
    unnamed x195, local copies, waits for them, and re-layouts  42.2 us
    all_to_all x2, waiting for transfers between devices, shards(): lax.all_to_all(sent_now[0], 'group', split_axis=0, concat_axis=0, tiled=T...  36.5 us
    psum x1, waiting for transfers between devices, shards(): summed_out, shrunk_out = lax.psum((base_output, shrink_part), 'tp')  23.7 us
    all_to_all x2, waiting for transfers between devices, shards(): lax.all_to_all(sent_now[5], 'group', split_axis=0, concat_axis=0, tiled=T...  23.2 us
    dot_general x36, matrix products, select_rows(): mixed = jnp.dot(onehot, flat, preferred_element_type=jnp.float32)  20.8 us
    all_to_all x2, waiting for transfers between devices, shards(): lax.all_to_all(sent_now[1], 'group', split_axis=0, concat_axis=0, tiled=T...  17.9 us
  transfers between devices with their start and end apart: 21, of which 19 were waited for; matrix products, arithmetic and copies ran while one was open for 20% of the time, Pallas kernels for 0%

commit v1 on v0

v1 whole, which is shorter than its diff:
```python
import math

import jax
import jax.numpy as jnp
from jax import lax
from jax.experimental import pallas as pl
from jax.experimental.pallas import tpu as pltpu
from jax.sharding import PartitionSpec as P

QH = 32
KH = 4
HD = 128
STEPS = 2
ROWS = 128
RANK = 16
LOADS = 12
SLOTS = 13
HELD = 12
N = 16
ALL_ROWS = STEPS * ROWS
LOCAL = ROWS // N
MINE = STEPS * LOCAL
ENTRIES = 1 + STEPS * LOADS
IN_RANK = 3 * RANK
PER_DOT = 5
QF = 256
KF = 32
IN_PART = 512
OUT_PART = 512
FEATURES = QH * HD
LENGTH = 512
KW = KH * HD
BF16 = jnp.bfloat16
F32 = jnp.float32
low_rank_scale = 0.5


def vmem():
    return pl.BlockSpec(memory_space=pltpu.VMEM)


def hbm():
    return pl.BlockSpec(memory_space=pl.ANY)


def smem():
    return pl.BlockSpec(memory_space=pltpu.SMEM)


def params():
    return pltpu.CompilerParams(vmem_limit_bytes=40 * 1024 * 1024)


def cost(flops, nbytes):
    return pl.CostEstimate(flops=flops, bytes_accessed=nbytes, transcendentals=0)


def shrink_kernel(index, pool, slot, tokens, entry, out, maps, arrived):
    copies = []
    for i in range(ENTRIES):
        origin = slot.at[index[0]] if i == 0 else pool.at[index[i]]
        copy = pltpu.make_async_copy(origin, maps.at[pl.ds(i * IN_RANK, IN_RANK)], arrived.at[i])
        copy.start()
        copies.append(copy)
    used = entry[...]
    total = jnp.zeros((IN_RANK, ALL_ROWS), F32)
    for first in range(0, ENTRIES, PER_DOT):
        for i in range(first, first + PER_DOT):
            copies[i].wait()
        block = maps[pl.ds(first * IN_RANK, PER_DOT * IN_RANK), :]
        product = lax.dot_general(
            block, tokens[...], (((1,), (1,)), ((), ())), preferred_element_type=F32
        )
        for k in range(PER_DOT):
            piece = product[k * IN_RANK : (k + 1) * IN_RANK]
            total = total + jnp.where(used == first + k, piece, 0.0)
    out[...] = total.astype(BF16)


def expand(shrunk, entry):
    loads = STEPS * LOADS
    load = lax.broadcasted_iota(jnp.int32, (loads, ALL_ROWS), 0) + 1
    chosen = load == entry
    blocks = [jnp.where(chosen, shrunk[r : r + 1, :], 0.0) for r in range(RANK)]
    kept = jnp.where(entry == 0, shrunk, 0.0)
    return jnp.concatenate(blocks + [kept], axis=0).astype(BF16)


def contract(left, right):
    return lax.dot_general(left, right, (((0,), (0,)), ((), ())), preferred_element_type=F32)


def project_kernel(parts, entry, base_q, base_kv, up_q, up_kv, out):
    shrunk = jnp.sum(parts[...].astype(F32), axis=0).astype(BF16).astype(F32)
    used = entry[...]
    wide_q = expand(shrunk[:RANK], used)
    wide_k = expand(shrunk[RANK : 2 * RANK], used)
    wide_v = expand(shrunk[2 * RANK :], used)
    query = base_q[...] + low_rank_scale * contract(wide_q, up_q[...])
    delta_k = contract(wide_k, up_kv[...])
    delta_v = contract(wide_v, up_kv[...])
    column = lax.broadcasted_iota(jnp.int32, delta_k.shape, 1)
    delta = jnp.where(column < KF, delta_k, delta_v)
    fresh = base_kv[...] + low_rank_scale * delta
    for t in range(N):
        for s in range(STEPS):
            low = s * ROWS + t * LOCAL
            out[t, s * LOCAL : (s + 1) * LOCAL, :QF] = query[low : low + LOCAL]
            out[t, s * LOCAL : (s + 1) * LOCAL, QF:] = fresh[low : low + LOCAL]


def attend_kernel(lengths, queries, keys_new, values_new, keys, values, out):
    row = pl.program_id(0)
    length = lengths[row]
    position = lax.broadcasted_iota(jnp.int32, (LENGTH, 1), 0)
    first, second = position == length, position == length + 1
    key_rows = keys[0]
    value_rows = values[0]
    key_rows = jnp.where(first, keys_new[0, 0:1], jnp.where(second, keys_new[0, 1:2], key_rows))
    value_rows = jnp.where(
        first, values_new[0, 0:1], jnp.where(second, values_new[0, 1:2], value_rows)
    )
    head_rows = STEPS * QH
    group = lax.broadcasted_iota(jnp.int32, (head_rows, KW), 0) % N // (N // KH)
    own = group == lax.broadcasted_iota(jnp.int32, (head_rows, KW), 1) // HD
    asked = queries[0]
    spread = jnp.where(own, jnp.concatenate([asked] * KH, axis=1), jnp.zeros((), BF16))
    scores = lax.dot_general(
        spread, key_rows, (((1,), (1,)), ((), ())), preferred_element_type=F32
    ) * (1.0 / math.sqrt(HD))
    step = lax.broadcasted_iota(jnp.int32, (head_rows, LENGTH), 0) // QH
    seen = lax.broadcasted_iota(jnp.int32, (head_rows, LENGTH), 1) <= length + step
    scores = jnp.where(seen, scores, -jnp.inf)
    weights = jnp.exp(scores - jnp.max(scores, axis=1, keepdims=True))
    totals = jnp.sum(weights, axis=1, keepdims=True)
    mixed = jnp.dot(weights.astype(BF16), value_rows, preferred_element_type=F32)
    mixed = jnp.where(own, mixed, 0.0)
    attended = mixed[:, :HD]
    for k in range(1, KH):
        attended = attended + mixed[:, k * HD : (k + 1) * HD]
    out[0] = (attended / totals).astype(BF16)


def shrink_out_kernel(attended, entry, maps, kept, out):
    part = attended[...].reshape(ALL_ROWS, QF)
    used = entry[...]
    dims = (((1,), (1,)), ((), ()))
    loaded = lax.dot_general(maps[...], part, dims, preferred_element_type=F32)
    first = lax.dot_general(kept[...], part, dims, preferred_element_type=F32)
    loads = STEPS * LOADS
    chosen = lax.broadcasted_iota(jnp.int32, (loads, ALL_ROWS), 0) + 1 == used
    rows = [
        jnp.sum(jnp.where(chosen, loaded[r * loads : (r + 1) * loads], 0.0), axis=0, keepdims=True)
        for r in range(RANK)
    ]
    out[...] = (jnp.concatenate(rows, axis=0) + jnp.where(used == 0, first, 0.0)).astype(BF16)


def base_out_kernel(attended, weight, out, total):
    total[...] = jnp.zeros_like(total)

    @pl.loop(0, N)
    def _(t):
        part = attended[:, t].reshape(ALL_ROWS, QF)
        total[...] += jnp.dot(part, weight[t], preferred_element_type=F32)

    out[...] = total[...]


def final_kernel(parts, entry, base, up, out):
    shrunk = jnp.sum(parts[...].astype(F32), axis=0).astype(BF16).astype(F32)
    wide = expand(shrunk, entry[...])
    total = base[...] + low_rank_scale * contract(wide, up[...])
    for t in range(N):
        for s in range(STEPS):
            low = t * MINE + s * LOCAL
            out[s, t * LOCAL : (t + 1) * LOCAL, :] = total[low : low + LOCAL]


def shard(
    hidden, w_query, w_key, w_value, w_out, key_cache, value_cache, lengths, row_slot, evict_slot,
    evict_adapter, owner, pool_a_in, pool_b_q, pool_b_k, pool_b_v, pool_a_o, pool_b_o,
    slot_a_in, slot_b_q, slot_b_k, slot_b_v, slot_a_o, slot_b_o,
):
    me = lax.axis_index("group")
    part = lax.axis_index("tp")

    with jax.named_scope("gather_in_maps"):
        whole_in = lax.all_gather(pool_a_in, "group").reshape(N * HELD, IN_RANK, IN_PART)

    with jax.named_scope("positions"):
        position = jnp.sum(
            jnp.where(evict_adapter[..., None] == jnp.arange(N * HELD), owner, 0), axis=-1
        )
        wanted = position.reshape(STEPS, N, LOADS).transpose(1, 0, 2).reshape(N, STEPS * LOADS)
        targets = lax.dynamic_slice_in_dim(evict_slot, me * LOADS, LOADS, 1)
        survivor = SLOTS * (SLOTS - 1) // 2 - jnp.sum(targets[0])
        placed = targets[:, :, None] == jnp.arange(SLOTS)
        order = 1 + jnp.arange(STEPS * LOADS).reshape(STEPS, LOADS, 1)
        slot_entry = jnp.sum(jnp.where(placed, order, 0), axis=1)
        second = jnp.where(slot_entry[1] > 0, slot_entry[1], slot_entry[0])
        slot_entry = jnp.stack([slot_entry[0], second])
        entry = jnp.sum(
            jnp.where(
                row_slot[:, :, None] == jnp.arange(SLOTS), slot_entry[:, None, :], 0
            ),
            axis=-1,
        )
        by_step = entry.reshape(1, ALL_ROWS)
        by_owner = entry.reshape(STEPS, N, LOCAL).transpose(1, 0, 2).reshape(1, ALL_ROWS)
        my_wanted = lax.dynamic_index_in_dim(wanted, me, 0, keepdims=False)
        index = jnp.concatenate([survivor[None], my_wanted]).astype(jnp.int32)

    with jax.named_scope("exchange_rest"):
        rest = jnp.concatenate([pool_b_q, pool_b_k, pool_b_v, pool_a_o, pool_b_o], axis=2)
        width = rest.shape[2]
        by_rank = lax.all_to_all(
            rest.transpose(1, 0, 2), "group", split_axis=0, concat_axis=0, tiled=True
        ).reshape(N * HELD, width)
        pick = (wanted.reshape(-1, 1) == jnp.arange(N * HELD)).astype(BF16)
        sent = jnp.dot(pick, by_rank, preferred_element_type=F32).astype(BF16)
        loaded = lax.all_to_all(
            sent.reshape(N, STEPS * LOADS, width), "group", split_axis=0, concat_axis=0, tiled=True
        ).reshape(RANK * STEPS * LOADS, width)
        kept = jnp.concatenate(
            [
                lax.dynamic_index_in_dim(piece, survivor, 0, keepdims=False)
                for piece in (slot_b_q, slot_b_k, slot_b_v, slot_a_o, slot_b_o)
            ],
            axis=1,
        )
        ends = (QF, QF + 2 * KF, 2 * QF + 2 * KF)
        up = jnp.concatenate([loaded, kept], axis=0)
        up_q, up_kv, up_o = up[:, : ends[0]], up[:, ends[0] : ends[1]], up[:, ends[2] :]
        out_maps, out_kept = loaded[:, ends[1] : ends[2]], kept[:, ends[1] : ends[2]]

    with jax.named_scope("columns_of_w_out"):
        columns = lax.all_to_all(
            w_out.reshape(QF, N, OUT_PART).transpose(1, 0, 2),
            "tp", split_axis=0, concat_axis=0, tiled=True,
        )

    with jax.named_scope("base_projections"):
        tokens = hidden.reshape(ALL_ROWS, -1)
        base_q = jnp.dot(tokens, w_query, preferred_element_type=F32)
        base_kv = jnp.concatenate(
            [
                jnp.dot(tokens, w_key, preferred_element_type=F32),
                jnp.dot(tokens, w_value, preferred_element_type=F32),
            ],
            axis=1,
        )
        tokens_part = lax.dynamic_slice_in_dim(tokens, part * IN_PART, IN_PART, 1)

    with jax.named_scope("shrink"):
        partial_in = pl.pallas_call(
            shrink_kernel,
            out_shape=jax.ShapeDtypeStruct((IN_RANK, ALL_ROWS), BF16),
            in_specs=[smem(), hbm(), hbm(), vmem(), vmem()],
            out_specs=vmem(),
            scratch_shapes=[
                pltpu.VMEM((ENTRIES * IN_RANK, IN_PART), BF16),
                pltpu.SemaphoreType.DMA((ENTRIES,)),
            ],
            compiler_params=params(),
            cost_estimate=cost(2 * ENTRIES * IN_RANK * IN_PART * ALL_ROWS, 2 << 20),
            name="shrink",
        )(index, whole_in, slot_a_in, tokens_part, by_step)
        copies = jnp.broadcast_to(partial_in, (N, IN_RANK, ALL_ROWS))
        partials = lax.all_to_all(copies, "tp", split_axis=0, concat_axis=0, tiled=True)

    with jax.named_scope("project"):
        projected = pl.pallas_call(
            project_kernel,
            out_shape=jax.ShapeDtypeStruct((N, MINE, QF + 2 * KF), F32),
            in_specs=[vmem()] * 6,
            out_specs=vmem(),
            compiler_params=params(),
            cost_estimate=cost(2 * 400 * 512 * ALL_ROWS, 1 << 20),
            name="project",
        )(partials, by_step, base_q, base_kv, up_q, up_kv)
        received = lax.all_to_all(
            projected.astype(BF16), "tp", split_axis=0, concat_axis=0, tiled=True
        )

    with jax.named_scope("attend"):
        received = received.reshape(N, STEPS, LOCAL, QF + 2 * KF)
        queries = received[..., :QF].reshape(N, STEPS, LOCAL, 2, HD)
        queries = queries.transpose(2, 1, 3, 0, 4).reshape(LOCAL, STEPS * QH, HD)
        fresh = received[..., QF:].reshape(N, STEPS, LOCAL, 2, KF)
        fresh = fresh.transpose(3, 2, 1, 0, 4).reshape(2, LOCAL, STEPS, KW)
        attended = pl.pallas_call(
            attend_kernel,
            out_shape=jax.ShapeDtypeStruct((LOCAL, STEPS * QH, HD), BF16),
            grid_spec=pltpu.PrefetchScalarGridSpec(
                num_scalar_prefetch=1,
                grid=(LOCAL,),
                in_specs=[
                    pl.BlockSpec((1, STEPS * QH, HD), lambda i, _: (i, 0, 0)),
                    pl.BlockSpec((1, STEPS, KW), lambda i, _: (i, 0, 0)),
                    pl.BlockSpec((1, STEPS, KW), lambda i, _: (i, 0, 0)),
                    pl.BlockSpec((1, LENGTH, KW), lambda i, _: (i, 0, 0)),
                    pl.BlockSpec((1, LENGTH, KW), lambda i, _: (i, 0, 0)),
                ],
                out_specs=pl.BlockSpec((1, STEPS * QH, HD), lambda i, _: (i, 0, 0)),
            ),
            compiler_params=params(),
            cost_estimate=cost(4 * LOCAL * 64 * KW * LENGTH, 8 << 20),
            name="attend",
        )(lengths, queries, fresh[0], fresh[1], key_cache, value_cache)
        attended = attended.reshape(LOCAL, STEPS, 2, N, HD).transpose(3, 1, 0, 2, 4)
        attended = attended.reshape(N, MINE, QF)
        gathered = lax.all_to_all(
            jnp.broadcast_to(attended, (N, N, MINE, QF)),
            "tp", split_axis=0, concat_axis=0, tiled=True,
        )

    with jax.named_scope("output"):
        own_heads = lax.dynamic_index_in_dim(gathered, part, 1, keepdims=False)
        partial_out = pl.pallas_call(
            shrink_out_kernel,
            out_shape=jax.ShapeDtypeStruct((RANK, ALL_ROWS), BF16),
            in_specs=[vmem()] * 4,
            out_specs=vmem(),
            compiler_params=params(),
            cost_estimate=cost(2 * 400 * QF * ALL_ROWS, 1 << 20),
            name="shrink_out",
        )(own_heads, by_owner, out_maps, out_kept)
        partials_out = lax.all_to_all(
            jnp.broadcast_to(partial_out, (N, RANK, ALL_ROWS)),
            "tp", split_axis=0, concat_axis=0, tiled=True,
        )
        base_out = pl.pallas_call(
            base_out_kernel,
            out_shape=jax.ShapeDtypeStruct((ALL_ROWS, OUT_PART), F32),
            in_specs=[vmem()] * 2,
            out_specs=vmem(),
            scratch_shapes=[pltpu.VMEM((ALL_ROWS, OUT_PART), F32)],
            compiler_params=params(),
            cost_estimate=cost(2 * ALL_ROWS * FEATURES * OUT_PART, 6 << 20),
            name="base_out",
        )(gathered, columns)
        return pl.pallas_call(
            final_kernel,
            out_shape=jax.ShapeDtypeStruct((STEPS, ROWS, OUT_PART), F32),
            in_specs=[vmem()] * 4,
            out_specs=vmem(),
            compiler_params=params(),
            cost_estimate=cost(2 * 400 * OUT_PART * ALL_ROWS, 1 << 20),
            name="final",
        )(partials_out, by_owner, base_out, up_o).astype(BF16)


def solution(mesh):
    pooled = P("group", None, "tp")
    cached = P(("group", "tp"), None, None)
    placed = (
        P(None, "group", None), P(None, "tp"), P(None, "tp"), P(None, "tp"), P("tp", None),
        cached, cached, P(("group", "tp")), P(None, "group"), P(), P(), P(),
    ) + (pooled,) * 12
    return jax.shard_map(
        shard, mesh=mesh, in_specs=placed, out_specs=P(None, "group", "tp"), check_vma=False
    )
```

time: 587 us -> 273 us (0.47); the launches traced: 576 us -> 270 us
  blocking collectives: 150 us -> 11.2 us
  starting transfers between devices: 107 us -> 36.1 us
  matrix products: 66.5 us -> 6.76 us
  local copies, waits for them, and re-layouts: 61.6 us -> 39 us
  other arithmetic: 24.4 us -> 3.98 us
  Pallas kernels: 0 us -> 17.1 us
  waiting for transfers between devices: 151 us -> 141 us
    psum x2 -> x0, blocking collectives: 150 us -> none  [the longest x1 76.2 us: shards(): shrunk = lax.psum(partial_in, 'tp').astype(jnp.bfloat16)]
    all_to_all x20 -> x6, starting transfers between devices: 107 us -> 36.1 us  [the longest x1 8.59 us: shard(): lax.all_to_all(rest.transpose(1, 0, 2), 'group', split_axis=0, concat_axi...]
    dot_general x56 -> x4, matrix products: 66.5 us -> 6.76 us  [the longest x1 3.68 us: shard(): jnp.dot(tokens, w_value, preferred_element_type=F32)]
    all_gather x0 -> x1, waiting for transfers between devices: none -> 41.8 us  [shard(): lax.all_gather(pool_a_in, 'group').reshape(N * HELD, IN_RANK, IN_PART)]
    all_to_all x20 -> x6, waiting for transfers between devices: 128 us -> 98.3 us  [the longest x1 57.3 us: shard(): lax.all_to_all(w_out.reshape(QF, N, OUT_PART).transpose(1, 0, 2), 'tp', s...]
    psum x1 -> x0, waiting for transfers between devices: 23.7 us -> none  [shards(): summed_out, shrunk_out = lax.psum((base_output, shrink_part), 'tp')]
    unnamed x195 -> x36, local copies, waits for them, and re-layouts: 42.2 us -> 19.7 us
    pallas_call x0 -> x6, Pallas kernels: none -> 17.1 us  [the longest x1 5.94 us: shard(): pl.pallas_call(base_out_kernel, out_shape=jax.ShapeDtypeStruct((ALL_ROWS,...]
  transfers between devices with their start and end apart: 21 -> 7, of which waited for: 19 -> 6; matrix products, arithmetic and copies ran while one was open for 20% -> 13% of each run, Pallas kernels for 0% -> 4%
where the time goes in v1:
time: 273 us; the launch traced here: 270 us
  waiting for transfers between devices  141 us (52%)
  local copies, waits for them, and re-layouts  39 us (14%)
  starting transfers between devices  36.1 us (13%)
  Pallas kernels  17.1 us (6%)
  between operations  15.1 us (6%)
  blocking collectives  11.2 us (4%)
  matrix products  6.76 us (2%)
  other arithmetic  3.98 us (1%)
    all_to_all x1, waiting for transfers between devices, shard(): lax.all_to_all(w_out.reshape(QF, N, OUT_PART).transpose(1, 0, 2), 'tp', s...  57.3 us
    all_gather x1, waiting for transfers between devices, shard(): lax.all_gather(pool_a_in, 'group').reshape(N * HELD, IN_RANK, IN_PART)  41.8 us
    unnamed x36, local copies, waits for them, and re-layouts  19.7 us
    all_to_all x1, waiting for transfers between devices, shard(): lax.all_to_all(jnp.broadcast_to(attended, (N, N, MINE, QF)), 'tp', split_...  15.8 us
    all_to_all x1, waiting for transfers between devices, shard(): lax.all_to_all(rest.transpose(1, 0, 2), 'group', split_axis=0, concat_axi...  14.8 us
    all_to_all x1, blocking collectives, shard(): lax.all_to_all(projected.astype(BF16), 'tp', split_axis=0, concat_axis=0,...  11.2 us
    all_to_all x1, waiting for transfers between devices, shard(): lax.all_to_all(copies, 'tp', split_axis=0, concat_axis=0, tiled=True)  9.52 us
    all_to_all x1, starting transfers between devices, shard(): lax.all_to_all(rest.transpose(1, 0, 2), 'group', split_axis=0, concat_axi...  8.59 us
  transfers between devices with their start and end apart: 7, of which 6 were waited for; matrix products, arithmetic and copies ran while one was open for 13% of the time, Pallas kernels for 4%

profile of v1, /device:TPU:32, one launch (start us, length us, event | category | flops | bytes accessed | tf_op | source)
XLA Modules:
  0.0 270.2 jit_solution(5193289599944919422)
XLA Ops:
  8.9 0.9 copy.65
  10.8 1.0 copy.69
  11.8 1.2 concatenate.17
  13.0 8.6 %all-to-all-start.1 = ((bf16[16,12,1088]{2,1,0:T(8,128)(2,1)}), bf16[16,12,1088]{2,1,0:T(8,128)(2,1)S(1)}, u32[]{:S(2)}, u32[]{:S(2)}) async-start(bf16[16,12,1088]{2,1,0:T(8,128)(2,1)} %bitcast.5), calls=%async_computation.1 | async-start | bytes 1179648 | tf_op jit(solution)/shard_map/exchange_rest/all_to_all | solution.py:217
  21.6 0.9 select_reduce_fusion
  26.6 14.8 %all-to-all-done.1 = bf16[16,12,1088]{2,1,0:T(8,128)(2,1)S(1)} async-done(((bf16[16,12,1088]{2,1,0:T(8,128)(2,1)}), bf16[16,12,1088]{2,1,0:T(8,128)(2,1)S(1)}, u32[]{:S(2)}, u32[]{:S(2)}) %all-to-all-start.1) | async-done | bytes 417824 | tf_op jit(solution)/shard_map/exchange_rest/all_to_all | solution.py:217
  42.2 2.0 copy.70
  44.2 8.1 %all-to-all-start.2 = ((bf16[16,24,1088]{2,1,0:T(8,128)(2,1)}), bf16[16,24,1088]{2,1,0:T(8,128)(2,1)S(1)}, u32[]{:S(2)}, u32[]{:S(2)}) async-start(bf16[16,24,1088]{2,1,0:T(8,128)(2,1)} %bitcast.6), calls=%async_computation.2 | async-start | bytes 1769472 | tf_op jit(solution)/shard_map/exchange_rest/all_to_all | solution.py:222
  52.6 1.1 constant_dynamic-slice_fusion.tokens
  53.7 3.7 %fusion.8 = f32[256,32]{1,0:T(8,128)S(1)} fusion(bf16[256,8192]{1,0:T(8,128)(2,1)} %bitcast.67, bf16[8192,32]{0,1:T(8,128)(2,1)S(1)} %copy-done), kind=kOutput, calls=%fused_computation.34 | convolution fusion | flops 134217728 | bytes 4751360 | tf_op jit(solution)/shard_map/base_projections/dot_general | solution.py:249
  57.4 1.2 fusion.7
  58.7 1.2 fusion.6.base_q
  60.0 41.8 %all-gather.3.cloned.1.call-done.pool = bf16[192,48,512]{2,1,0:T(8,128)(2,1)} async-done(((bf16[12,48,512]{2,1,0:T(8,128)(2,1)}), bf16[192,48,512]{2,1,0:T(8,128)(2,1)}) %all-gather.3.cloned.1.call-update) | async-done | bytes 9437200 | tf_op jit(solution)/shard_map/gather_in_maps/all_gather | solution.py:189
  101.7 3.7 %copy-done.1 = bf16[192,48,512]{2,1,0:T(8,128)(2,1)S(1)} copy-done((bf16[192,48,512]{2,1,0:T(8,128)(2,1)S(1)}, bf16[192,48,512]{2,1,0:T(8,128)(2,1)}, u32[]{:S(2)}) %copy-start.1) | copy-done | bytes 9437208
  105.4 4.0 %shrink.1 = bf16[48,256]{1,0:T(8,128)(2,1)S(1)} custom-call(s32[25]{0:T(128)S(1)} %pad_add_fusion.1.index, bf16[192,48,512]{2,1,0:T(8,128)(2,1)S(1)} %copy-done.1, bf16[13,48,512]{2,1,0:T(8,128)(2,1)S(1)} %copy-done.4, bf16[256,512]{1,0:T(8,128)(2,1)S(1)} %constant_dynamic-slice_fusion.tokens, s32[1,256]{1,0:T(1,128)S(1)} %bitcast.52), custom_call_target="tpu_custom_call" | custom-call | flops 314572800 | bytes 2097152 | tf_op jit(solution)/shard_map/shrink/shrink/pallas_call | solution.py:256
  110.3 7.0 %all-to-all-start = ((bf16[16,48,256]{2,1,0:T(8,128)(2,1)}), bf16[16,48,256]{2,1,0:T(8,128)(2,1)S(1)}, u32[]{:S(2)}, u32[]{:S(2)}) async-start(bf16[16,48,256]{2,1,0:T(8,128)(2,1)} %broadcast_in_dim.59), calls=%async_computation | async-start | bytes 786432 | tf_op jit(solution)/shard_map/shrink/all_to_all | solution.py:270
  118.3 9.5 %all-to-all-done.parts = bf16[16,48,256]{2,1,0:T(8,128)(2,1)S(1)} async-done(((bf16[16,48,256]{2,1,0:T(8,128)(2,1)}), bf16[16,48,256]{2,1,0:T(8,128)(2,1)S(1)}, u32[]{:S(2)}, u32[]{:S(2)}) %all-to-all-start) | async-done | bytes 393248 | tf_op jit(solution)/shard_map/shrink/all_to_all | solution.py:270
  128.3 11.2 %all_to_all.35 = bf16[16,16,320]{2,1,0:T(8,128)(2,1)S(1)} all-to-all(bf16[16,16,320]{2,1,0:T(8,128)(2,1)S(1)} %convert_element_type.11), channel_id=1, replica_groups=mesh['group'=16,'tp'=16] {'tp'}, dimensions={0} | all-to-all | bytes 327680 | tf_op jit(solution)/shard_map/project/all_to_all | solution.py:282
  140.3 2.2 copy-done.2
  142.5 2.2 copy-done.3
  144.7 5.2 %attend.1 = bf16[8,64,128]{2,1,0:T(8,128)(2,1)S(1)} custom-call(s32[8]{0:T(128)S(1)} %copy-done.7, bf16[8,64,128]{2,1,0:T(8,128)(2,1)S(1)} %bitcast.50, bf16[8,2,512]{2,1,0:T(2,128)(2,1)S(1)} %squeeze.42.keys_new, bf16[8,2,512]{2,1,0:T(2,128)(2,1)S(1)} %squeeze.43.values_new, bf16[8,512,512]{2,1,0:T(8,128)(2,1)S(1)} %copy-done.2, ...), custom_call_target="tpu_custom_call" | custom-call | flops 536870912 | bytes 8388608 | tf_op jit(solution)/shard_map/attend/attend/pallas_call | solution.py:292
  150.0 1.6 broadcast_in_dim.60
  151.6 3.7 %all-to-all-start.4 = ((bf16[16,16,16,256]{3,2,1,0:T(8,128)(2,1)}), bf16[16,16,16,256]{3,2,1,0:T(8,128)(2,1)S(1)}, u32[]{:S(2)}, u32[]{:S(2)}) async-start(bf16[16,16,16,256]{3,2,1,0:T(8,128)(2,1)} %broadcast_in_dim.60), calls=%async_computation.4 | async-start | bytes 4194304 | tf_op jit(solution)/shard_map/attend/all_to_all | solution.py:313
  155.3 6.4 %copy.76 = bf16[256,8192]{0,1:T(8,128)(2,1)} copy(bf16[256,8192]{1,0:T(8,128)(2,1)} %param.28) | data formatting | bytes 8388608 | tf_op args[4]
  161.7 6.5 %copy.77 = bf16[256,16,512]{2,0,1:T(8,128)(2,1)} copy(bf16[256,16,512]{0,2,1:T(8,128)(2,1)} %bitcast.55) | data formatting | bytes 8388608 | tf_op jit(solution)/shard_map/columns_of_w_out/reshape | solution.py:239
  168.2 15.8 %all-to-all-done.4.attended = bf16[16,16,16,256]{3,2,1,0:T(8,128)(2,1)S(1)} async-done(((bf16[16,16,16,256]{3,2,1,0:T(8,128)(2,1)}), bf16[16,16,16,256]{3,2,1,0:T(8,128)(2,1)S(1)}, u32[]{:S(2)}, u32[]{:S(2)}) %all-to-all-start.4) | async-done | bytes 2097184 | tf_op jit(solution)/shard_map/attend/all_to_all | solution.py:313
  184.0 4.5 %all-to-all-start.6 = ((bf16[16,256,512]{2,1,0:T(8,128)(2,1)}), bf16[16,256,512]{2,1,0:T(8,128)(2,1)}, u32[]{:S(2)}, u32[]{:S(2)}) async-start(bf16[16,256,512]{2,1,0:T(8,128)(2,1)} %bitcast.54), calls=%async_computation.6 | async-start | bytes 8388608 | tf_op jit(solution)/shard_map/columns_of_w_out/all_to_all | solution.py:238
  190.5 57.3 %all-to-all-done.6.weight = bf16[16,256,512]{2,1,0:T(8,128)(2,1)} async-done(((bf16[16,256,512]{2,1,0:T(8,128)(2,1)}), bf16[16,256,512]{2,1,0:T(8,128)(2,1)}, u32[]{:S(2)}, u32[]{:S(2)}) %all-to-all-start.6) | async-done | bytes 4194336 | tf_op jit(solution)/shard_map/columns_of_w_out/all_to_all | solution.py:238
  248.5 4.2 %all-to-all-start.5 = ((bf16[16,16,256]{2,1,0:T(8,128)(2,1)}), bf16[16,16,256]{2,1,0:T(8,128)(2,1)}, u32[]{:S(2)}, u32[]{:S(2)}) async-start(bf16[16,16,256]{2,1,0:T(8,128)(2,1)} %broadcast_in_dim.61), calls=%async_computation.5 | async-start | bytes 262144 | tf_op jit(solution)/shard_map/output/all_to_all | solution.py:329
  252.7 1.2 pad_maximum_fusion.up
  254.0 5.9 %base_out.1.base = f32[256,512]{1,0:T(8,128)S(1)} custom-call(bf16[16,16,16,256]{3,2,1,0:T(8,128)(2,1)S(1)} %all-to-all-done.4.attended, bf16[16,256,512]{2,1,0:T(8,128)(2,1)} %all-to-all-done.6.weight), custom_call_target="tpu_custom_call" | custom-call | flops 1073741824 | bytes 6291456 | tf_op jit(solution)/shard_map/output/base_out/pallas_call | solution.py:333
  261.4 1.2 final.1
  (79 shorter events, 14.9 us)
Async XLA Ops:
  6.5 47.2 %copy-start = (bf16[8192,32]{0,1:T(8,128)(2,1)S(1)}, bf16[8192,32]{0,1:T(8,128)(2,1)}, u32[]{:S(2)}) copy-start(bf16[8192,32]{0,1:T(8,128)(2,1)} %param.27) | copy-start | bytes 1572868
  6.5 16.3 %copy-start.12 = (s32[2,192]{1,0:T(2,128)S(1)}, s32[2,192]{1,0:T(2,128)}, u32[]{:S(2)}) copy-start(s32[2,192]{1,0:T(2,128)} %param.33) | copy-start | bytes 4612
  6.5 95.2 %all-gather.3.cloned.1.call-start = ((), (), s32[]{:S(2)}) async-start(), calls=%async_computation.7 | async-start | bytes 10027008 | tf_op jit(solution)/shard_map/gather_in_maps/all_gather | solution.py:189
  11.8 40.7 %copy-start.11 = (s32[2,128]{1,0:T(2,128)S(1)}, s32[2,128]{1,0:T(2,128)}, u32[]{:S(2)}) copy-start(s32[2,128]{1,0:T(2,128)} %param.32) | copy-start | bytes 3076
  13.0 28.4 %all-to-all-start.1 = ((bf16[16,12,1088]{2,1,0:T(8,128)(2,1)}), bf16[16,12,1088]{2,1,0:T(8,128)(2,1)S(1)}, u32[]{:S(2)}, u32[]{:S(2)}) async-start(bf16[16,12,1088]{2,1,0:T(8,128)(2,1)} %bitcast.5), calls=%async_computation.1 | async-start | bytes 1179648 | tf_op jit(solution)/shard_map/exchange_rest/all_to_all | solution.py:217
  42.2 15.2 %copy-start.14 = (bf16[8192,32]{0,1:T(8,128)(2,1)S(1)}, bf16[8192,32]{0,1:T(8,128)(2,1)}, u32[]{:S(2)}) copy-start(bf16[8192,32]{0,1:T(8,128)(2,1)} %param.26) | copy-start | bytes 1572868
  44.2 65.2 %all-to-all-start.2 = ((bf16[16,24,1088]{2,1,0:T(8,128)(2,1)}), bf16[16,24,1088]{2,1,0:T(8,128)(2,1)S(1)}, u32[]{:S(2)}, u32[]{:S(2)}) async-start(bf16[16,24,1088]{2,1,0:T(8,128)(2,1)} %bitcast.6), calls=%async_computation.2 | async-start | bytes 1769472 | tf_op jit(solution)/shard_map/exchange_rest/all_to_all | solution.py:222
  52.5 4.9 %copy-start.10 = (bf16[2,128,8192]{2,1,0:T(8,128)(2,1)S(1)}, bf16[2,128,8192]{2,1,0:T(8,128)(2,1)}, u32[]{:S(2)}) copy-start(bf16[2,128,8192]{2,1,0:T(8,128)(2,1)} %param.24) | copy-start | bytes 12582916
  53.7 5.0 %copy-start.13 = (bf16[8192,256]{1,0:T(8,128)(2,1)S(1)}, bf16[8192,256]{1,0:T(8,128)(2,1)}, u32[]{:S(2)}) copy-start(bf16[8192,256]{1,0:T(8,128)(2,1)} %param.25) | copy-start | bytes 12582916
  58.7 43.1 %copy-start.4 = (bf16[13,48,512]{2,1,0:T(8,128)(2,1)S(1)}, bf16[13,48,512]{2,1,0:T(8,128)(2,1)}, u32[]{:S(2)}) copy-start(bf16[13,48,512]{2,1,0:T(8,128)(2,1)} %slot.1) | copy-start | bytes 1916932
  101.7 3.7 %copy-start.1 = (bf16[192,48,512]{2,1,0:T(8,128)(2,1)S(1)}, bf16[192,48,512]{2,1,0:T(8,128)(2,1)}, u32[]{:S(2)}) copy-start(bf16[192,48,512]{2,1,0:T(8,128)(2,1)} %all-gather.3.cloned.1.call-done.pool) | copy-start | bytes 28311556
  109.4 30.9 %copy-start.7 = (s32[8]{0:T(128)S(1)}, s32[8]{0:T(128)}, u32[]{:S(2)}) copy-start(s32[8]{0:T(128)} %lengths.1) | copy-start | bytes 100
  109.5 80.6 %copy-start.8 = (bf16[16,24,1088]{2,1,0:T(8,128)(2,1)}, bf16[16,24,1088]{2,1,0:T(8,128)(2,1)S(1)}, u32[]{:S(2)}) copy-start(bf16[16,24,1088]{2,1,0:T(8,128)(2,1)S(1)} %all-to-all-done.2) | copy-start | bytes 2506756
  110.3 17.5 %all-to-all-start = ((bf16[16,48,256]{2,1,0:T(8,128)(2,1)}), bf16[16,48,256]{2,1,0:T(8,128)(2,1)S(1)}, u32[]{:S(2)}, u32[]{:S(2)}) async-start(bf16[16,48,256]{2,1,0:T(8,128)(2,1)} %broadcast_in_dim.59), calls=%async_computation | async-start | bytes 786432 | tf_op jit(solution)/shard_map/shrink/all_to_all | solution.py:270
  118.2 31.7 %copy-start.9 = (bf16[16,1088]{1,0:T(8,128)(2,1)}, bf16[16,1088]{1,0:T(8,128)(2,1)S(1)}, u32[]{:S(2)}) copy-start(bf16[16,1088]{1,0:T(8,128)(2,1)S(1)} %concatenate.18) | copy-start | bytes 104452
  140.3 2.2 copy-start.2
  142.5 2.2 copy-start.3
  151.6 32.4 %all-to-all-start.4 = ((bf16[16,16,16,256]{3,2,1,0:T(8,128)(2,1)}), bf16[16,16,16,256]{3,2,1,0:T(8,128)(2,1)S(1)}, u32[]{:S(2)}, u32[]{:S(2)}) async-start(bf16[16,16,16,256]{3,2,1,0:T(8,128)(2,1)} %broadcast_in_dim.60), calls=%async_computation.4 | async-start | bytes 4194304 | tf_op jit(solution)/shard_map/attend/all_to_all | solution.py:313
  184.0 63.9 %all-to-all-start.6 = ((bf16[16,256,512]{2,1,0:T(8,128)(2,1)}), bf16[16,256,512]{2,1,0:T(8,128)(2,1)}, u32[]{:S(2)}, u32[]{:S(2)}) async-start(bf16[16,256,512]{2,1,0:T(8,128)(2,1)} %bitcast.54), calls=%async_computation.6 | async-start | bytes 8388608 | tf_op jit(solution)/shard_map/columns_of_w_out/all_to_all | solution.py:238
  190.1 62.7 %copy-start.5 = (s32[1,256]{1,0:T(1,128)}, s32[1,256]{1,0:T(1,128)S(1)}, u32[]{:S(2)}) copy-start(s32[1,256]{1,0:T(1,128)S(1)} %reshape.99.entry) | copy-start | bytes 3076
  248.5 12.2 %all-to-all-start.5 = ((bf16[16,16,256]{2,1,0:T(8,128)(2,1)}), bf16[16,16,256]{2,1,0:T(8,128)(2,1)}, u32[]{:S(2)}, u32[]{:S(2)}) async-start(bf16[16,16,256]{2,1,0:T(8,128)(2,1)} %broadcast_in_dim.61), calls=%async_computation.5 | async-start | bytes 262144 | tf_op jit(solution)/shard_map/output/all_to_all | solution.py:329
  260.7 0.7 copy-start.6
Sparse Core Ops, SparseCore 0:
  9.2 92.5 all-gather.2

commit v2 on v1

--- a/solution.py
+++ b/solution.py
@@ -47,8 +47,8 @@
     return pl.BlockSpec(memory_space=pltpu.SMEM)
 
 
-def params():
-    return pltpu.CompilerParams(vmem_limit_bytes=40 * 1024 * 1024)
+def params(mib=40):
+    return pltpu.CompilerParams(vmem_limit_bytes=mib * 1024 * 1024)
 
 
 def cost(flops, nbytes):
@@ -141,36 +141,60 @@
     out[0] = (attended / totals).astype(BF16)
 
 
-def shrink_out_kernel(attended, entry, maps, kept, out):
-    part = attended[...].reshape(ALL_ROWS, QF)
-    used = entry[...]
-    dims = (((1,), (1,)), ((), ()))
-    loaded = lax.dot_general(maps[...], part, dims, preferred_element_type=F32)
-    first = lax.dot_general(kept[...], part, dims, preferred_element_type=F32)
+def shrink_out_kernel(attended, entry, maps, out):
+    total = jnp.zeros((MINE, ENTRIES * RANK), F32)
+    for t in range(N):
+        total = total + lax.dot_general(
+            attended[t], maps[t], (((1,), (1,)), ((), ())), preferred_element_type=F32
+        )
+    column = lax.broadcasted_iota(jnp.int32, total.shape, 1)
+    placed = jnp.where(order_of(column) == entry[...], total, 0.0).astype(BF16)
+    shape = (ENTRIES * RANK, QF)
+    fold = rank_of(lax.broadcasted_iota(jnp.int32, shape, 0)) == lax.broadcasted_iota(
+        jnp.int32, shape, 1
+    )
+    shrunk = jnp.dot(placed, fold.astype(BF16), preferred_element_type=F32)
+    out[...] = shrunk.astype(BF16)
+
+
+def order_of(column):
     loads = STEPS * LOADS
-    chosen = lax.broadcasted_iota(jnp.int32, (loads, ALL_ROWS), 0) + 1 == used
-    rows = [
-        jnp.sum(jnp.where(chosen, loaded[r * loads : (r + 1) * loads], 0.0), axis=0, keepdims=True)
-        for r in range(RANK)
-    ]
-    out[...] = (jnp.concatenate(rows, axis=0) + jnp.where(used == 0, first, 0.0)).astype(BF16)
-
-
-def base_out_kernel(attended, weight, out, total):
-    total[...] = jnp.zeros_like(total)
-
-    @pl.loop(0, N)
-    def _(t):
-        part = attended[:, t].reshape(ALL_ROWS, QF)
-        total[...] += jnp.dot(part, weight[t], preferred_element_type=F32)
-
-    out[...] = total[...]
-
-
-def final_kernel(parts, entry, base, up, out):
-    shrunk = jnp.sum(parts[...].astype(F32), axis=0).astype(BF16).astype(F32)
-    wide = expand(shrunk, entry[...])
-    total = base[...] + low_rank_scale * contract(wide, up[...])
+    return jnp.where(column < RANK * loads, column % loads + 1, 0)
+
+
+def rank_of(column):
+    loads = STEPS * LOADS
+    return jnp.where(column < RANK * loads, column // loads, column - RANK * loads)
+
+
+def output_kernel(index, side, attended, entry, mine, others, pool, slot, out, up, arrived):
+    copies = []
+    for i in range(ENTRIES):
+        origin = slot.at[index[0]] if i == 0 else pool.at[index[i]]
+        copy = pltpu.make_async_copy(origin, up.at[pl.ds(i * RANK, RANK)], arrived.at[i])
+        copy.start()
+        copies.append(copy)
+    total = jnp.zeros((ALL_ROWS, OUT_PART), F32)
+    for t in range(N):
+        low = attended[:, t, :, : QF // 2].reshape(ALL_ROWS, QF // 2)
+        high = attended[:, t, :, QF // 2 :].reshape(ALL_ROWS, QF // 2)
+        near = jnp.where(side[0] == 0, low, high)
+        far = jnp.where(side[0] == 0, high, low)
+        left = jnp.concatenate([near, far], axis=1)
+        right = jnp.concatenate([mine[t], others[t]], axis=0)
+        total = total + jnp.dot(left, right, preferred_element_type=F32)
+    shrunk = attended[:, N].reshape(ALL_ROWS, QF)
+    shape = (QF, ENTRIES * RANK)
+    repeat = lax.broadcasted_iota(jnp.int32, shape, 1) % RANK == lax.broadcasted_iota(
+        jnp.int32, shape, 0
+    )
+    wide = jnp.dot(shrunk, repeat.astype(BF16), preferred_element_type=F32)
+    column = lax.broadcasted_iota(jnp.int32, wide.shape, 1)
+    wide = jnp.where(column // RANK == entry[...], wide, 0.0).astype(BF16)
+    for copy in copies:
+        copy.wait()
+    total = total + low_rank_scale * jnp.dot(wide, up[...], preferred_element_type=F32)
+    total = total.astype(BF16).astype(F32)
     for t in range(N):
         for s in range(STEPS):
             low = t * MINE + s * LOCAL
@@ -207,12 +231,14 @@
             axis=-1,
         )
         by_step = entry.reshape(1, ALL_ROWS)
-        by_owner = entry.reshape(STEPS, N, LOCAL).transpose(1, 0, 2).reshape(1, ALL_ROWS)
+        by_owner = entry.reshape(STEPS, N, LOCAL).transpose(1, 0, 2)
+        of_mine = lax.dynamic_index_in_dim(by_owner, part, 0, keepdims=False).reshape(MINE, 1)
+        by_owner = by_owner.reshape(ALL_ROWS, 1)
         my_wanted = lax.dynamic_index_in_dim(wanted, me, 0, keepdims=False)
         index = jnp.concatenate([survivor[None], my_wanted]).astype(jnp.int32)
 
     with jax.named_scope("exchange_rest"):
-        rest = jnp.concatenate([pool_b_q, pool_b_k, pool_b_v, pool_a_o, pool_b_o], axis=2)
+        rest = jnp.concatenate([pool_b_q, pool_b_k, pool_b_v, pool_a_o], axis=2)
         width = rest.shape[2]
         by_rank = lax.all_to_all(
             rest.transpose(1, 0, 2), "group", split_axis=0, concat_axis=0, tiled=True
@@ -225,20 +251,20 @@
         kept = jnp.concatenate(
             [
                 lax.dynamic_index_in_dim(piece, survivor, 0, keepdims=False)
-                for piece in (slot_b_q, slot_b_k, slot_b_v, slot_a_o, slot_b_o)
+                for piece in (slot_b_q, slot_b_k, slot_b_v, slot_a_o)
             ],
             axis=1,
         )
-        ends = (QF, QF + 2 * KF, 2 * QF + 2 * KF)
         up = jnp.concatenate([loaded, kept], axis=0)
-        up_q, up_kv, up_o = up[:, : ends[0]], up[:, ends[0] : ends[1]], up[:, ends[2] :]
-        out_maps, out_kept = loaded[:, ends[1] : ends[2]], kept[:, ends[1] : ends[2]]
+        up_q, up_kv, out_maps = up[:, :QF], up[:, QF : QF + 2 * KF], up[:, QF + 2 * KF :]
+        whole_out_maps = lax.all_gather(out_maps, "tp")
 
     with jax.named_scope("columns_of_w_out"):
-        columns = lax.all_to_all(
-            w_out.reshape(QF, N, OUT_PART).transpose(1, 0, 2),
-            "tp", split_axis=0, concat_axis=0, tiled=True,
-        )
+        side = me % 2
+        half = lax.dynamic_slice_in_dim(w_out, side * (QF // 2), QF // 2, 0)
+        half = jnp.stack([half[:, t * OUT_PART : (t + 1) * OUT_PART] for t in range(N)])
+        mine = lax.all_to_all(half, "tp", split_axis=0, concat_axis=0, tiled=True)
+        others = lax.ppermute(mine, "group", [(i, i ^ 1) for i in range(N)])
 
     with jax.named_scope("base_projections"):
         tokens = hidden.reshape(ALL_ROWS, -1)
@@ -262,10 +288,13 @@
                 pltpu.VMEM((ENTRIES * IN_RANK, IN_PART), BF16),
                 pltpu.SemaphoreType.DMA((ENTRIES,)),
             ],
-            compiler_params=params(),
+            compiler_params=params(56),
             cost_estimate=cost(2 * ENTRIES * IN_RANK * IN_PART * ALL_ROWS, 2 << 20),
             name="shrink",
         )(index, whole_in, slot_a_in, tokens_part, by_step)
+        partial_in, mine = lax.optimization_barrier((partial_in, mine))
+        partial_in, pool_b_o = lax.optimization_barrier((partial_in, pool_b_o))
+        whole_b_o = lax.all_gather(pool_b_o, "group").reshape(N * HELD, RANK, OUT_PART)
         copies = jnp.broadcast_to(partial_in, (N, IN_RANK, ALL_ROWS))
         partials = lax.all_to_all(copies, "tp", split_axis=0, concat_axis=0, tiled=True)
 
@@ -304,51 +333,43 @@
                 ],
                 out_specs=pl.BlockSpec((1, STEPS * QH, HD), lambda i, _: (i, 0, 0)),
             ),
-            compiler_params=params(),
+            compiler_params=params(56),
             cost_estimate=cost(4 * LOCAL * 64 * KW * LENGTH, 8 << 20),
             name="attend",
         )(lengths, queries, fresh[0], fresh[1], key_cache, value_cache)
         attended = attended.reshape(LOCAL, STEPS, 2, N, HD).transpose(3, 1, 0, 2, 4)
         attended = attended.reshape(N, MINE, QF)
-        gathered = lax.all_to_all(
-            jnp.broadcast_to(attended, (N, N, MINE, QF)),
-            "tp", split_axis=0, concat_axis=0, tiled=True,
-        )
-
-    with jax.named_scope("output"):
-        own_heads = lax.dynamic_index_in_dim(gathered, part, 1, keepdims=False)
-        partial_out = pl.pallas_call(
+        shrunk_out = pl.pallas_call(
             shrink_out_kernel,
-            out_shape=jax.ShapeDtypeStruct((RANK, ALL_ROWS), BF16),
-            in_specs=[vmem()] * 4,
+            out_shape=jax.ShapeDtypeStruct((MINE, QF), BF16),
+            in_specs=[vmem()] * 3,
             out_specs=vmem(),
             compiler_params=params(),
-            cost_estimate=cost(2 * 400 * QF * ALL_ROWS, 1 << 20),
+            cost_estimate=cost(2 * 400 * FEATURES * MINE, 4 << 20),
             name="shrink_out",
-        )(own_heads, by_owner, out_maps, out_kept)
-        partials_out = lax.all_to_all(
-            jnp.broadcast_to(partial_out, (N, RANK, ALL_ROWS)),
+        )(attended, of_mine, whole_out_maps)
+        payload = jnp.concatenate([attended, shrunk_out[None]], axis=0)
+        gathered = lax.all_to_all(
+            jnp.broadcast_to(payload, (N, N + 1, MINE, QF)),
             "tp", split_axis=0, concat_axis=0, tiled=True,
         )
-        base_out = pl.pallas_call(
-            base_out_kernel,
-            out_shape=jax.ShapeDtypeStruct((ALL_ROWS, OUT_PART), F32),
-            in_specs=[vmem()] * 2,
+
+    with jax.named_scope("output"):
+        return pl.pallas_call(
+            output_kernel,
+            out_shape=jax.ShapeDtypeStruct((STEPS, ROWS, OUT_PART), F32),
+            in_specs=[smem(), smem(), vmem(), vmem(), vmem(), vmem(), hbm(), hbm()],
             out_specs=vmem(),
-            scratch_shapes=[pltpu.VMEM((ALL_ROWS, OUT_PART), F32)],
+            scratch_shapes=[
+                pltpu.VMEM((ENTRIES * RANK, OUT_PART), BF16),
+                pltpu.SemaphoreType.DMA((ENTRIES,)),
+            ],
             compiler_params=params(),
-            cost_estimate=cost(2 * ALL_ROWS * FEATURES * OUT_PART, 6 << 20),
-            name="base_out",
-        )(gathered, columns)
-        return pl.pallas_call(
-            final_kernel,
-            out_shape=jax.ShapeDtypeStruct((STEPS, ROWS, OUT_PART), F32),
-            in_specs=[vmem()] * 4,
-            out_specs=vmem(),
-            compiler_params=params(),
-            cost_estimate=cost(2 * 400 * OUT_PART * ALL_ROWS, 1 << 20),
-            name="final",
-        )(partials_out, by_owner, base_out, up_o).astype(BF16)
+            cost_estimate=cost(2 * ALL_ROWS * (FEATURES + 400) * OUT_PART, 7 << 20),
+            name="output",
+        )(
+            index, side[None], gathered, by_owner, mine, others, whole_b_o, slot_b_o
+        ).astype(BF16)
 
 
 def solution(mesh):

time: 273 us -> 238 us (0.87)
  waiting for transfers between devices: 141 us -> 105 us
  blocking collectives: 11.2 us -> 0 us
  local copies, waits for them, and re-layouts: 39 us -> 43.6 us
  matrix products: 6.76 us -> 11 us
  Pallas kernels: 17.1 us -> 19.9 us
    all_gather x1, waiting for transfers between devices: 41.8 us -> 0.01 us  [shard(): lax.all_gather(pool_a_in, 'group').reshape(N * HELD, IN_RANK, IN_PART)]
    all_to_all x1, waiting for transfers between devices: 0.01 us -> 13.4 us  [shard(): lax.all_to_all(sent.reshape(N, STEPS * LOADS, width), 'group', split_axis...]
    unnamed x36 -> x45, local copies, waits for them, and re-layouts: 19.7 us -> 31.1 us
    all_to_all x1 -> x0, blocking collectives: 11.2 us -> none  [shard(): lax.all_to_all(projected.astype(BF16), 'tp', split_axis=0, concat_axis=0,...]
    reshape x3 -> x4, local copies, waits for them, and re-layouts: 7.35 us -> 1.26 us  [the longest x1 0.99 us: shard(): attended = attended.reshape(LOCAL, STEPS, 2, N, HD).transpose(3, 1, 0, 2, 4)]
    all_to_all x3, waiting for transfers between devices: 74 us -> 68.1 us  [the longest x1 30.5 us: shard(): mine = lax.all_to_all(half, 'tp', split_axis=0, concat_axis=0, tiled=True)]
    pallas_call x1, Pallas kernels: 5.21 us -> 9.39 us  [shard(): pl.pallas_call(attend_kernel, out_shape=jax.ShapeDtypeStruct((LOCAL, STEP...]
    all_to_all x1, starting transfers between devices: 7.04 us -> 3.55 us  [shard(): lax.all_to_all(copies, 'tp', split_axis=0, concat_axis=0, tiled=True)]
  transfers between devices with their start and end apart: 7 -> 10, of which waited for: 6 -> 6; matrix products, arithmetic and copies ran while one was open for 13% -> 24% of each run, Pallas kernels for 4% -> 6%
where the time goes in v2:
time: 238 us; the launch traced here: 234 us
  waiting for transfers between devices  105 us (44%)
  local copies, waits for them, and re-layouts  43.6 us (18%)
  starting transfers between devices  33.9 us (14%)
  Pallas kernels  19.9 us (8%)
  between operations  14.8 us (6%)
  matrix products  11 us (5%)
  other arithmetic  5.74 us (2%)
    unnamed x45, local copies, waits for them, and re-layouts  31.1 us
    all_to_all x1, waiting for transfers between devices, shard(): mine = lax.all_to_all(half, 'tp', split_axis=0, concat_axis=0, tiled=True)  30.5 us
    all_to_all x1, waiting for transfers between devices, shard(): lax.all_to_all(jnp.broadcast_to(payload, (N, N + 1, MINE, QF)), 'tp', spl...  29.6 us
    all_to_all x1, waiting for transfers between devices, shard(): lax.all_to_all(sent.reshape(N, STEPS * LOADS, width), 'group', split_axis...  13.4 us
    all_to_all x1, waiting for transfers between devices, shard(): lax.all_to_all(copies, 'tp', split_axis=0, concat_axis=0, tiled=True)  11.5 us
    all_to_all x1, waiting for transfers between devices, shard(): lax.all_to_all(rest.transpose(1, 0, 2), 'group', split_axis=0, concat_axi...  11.3 us
    pallas_call x1, Pallas kernels, shard(): pl.pallas_call(attend_kernel, out_shape=jax.ShapeDtypeStruct((LOCAL, STEP...  9.39 us
    all_to_all x1, starting transfers between devices, shard(): lax.all_to_all(rest.transpose(1, 0, 2), 'group', split_axis=0, concat_axi...  8.72 us
  transfers between devices with their start and end apart: 10, of which 6 were waited for; matrix products, arithmetic and copies ran while one was open for 24% of the time, Pallas kernels for 6%

profile of v2, /device:TPU:32, one launch (start us, length us, event | category | flops | bytes accessed | tf_op | source)
XLA Modules:
  0.0 234.1 jit_solution(9762865373999078302)
XLA Ops:
  11.7 8.7 %all-to-all-start.2 = ((bf16[16,12,576]{2,1,0:T(8,128)(2,1)}), bf16[16,12,576]{2,1,0:T(8,128)(2,1)S(1)}, u32[]{:S(2)}, u32[]{:S(2)}) async-start(bf16[16,12,576]{2,1,0:T(8,128)(2,1)} %maximum_bitcast_fusion), calls=%async_computation.2 | async-start | bytes 655360 | tf_op jit(solution)/shard_map/exchange_rest/all_to_all | solution.py:243
  20.9 11.3 %all-to-all-done.2 = bf16[16,12,576]{2,1,0:T(8,128)(2,1)S(1)} async-done(((bf16[16,12,576]{2,1,0:T(8,128)(2,1)}), bf16[16,12,576]{2,1,0:T(8,128)(2,1)S(1)}, u32[]{:S(2)}, u32[]{:S(2)}) %all-to-all-start.2) | async-done | bytes 221216 | tf_op jit(solution)/shard_map/exchange_rest/all_to_all | solution.py:243
  33.8 7.0 %all-to-all-start.3 = ((bf16[16,24,576]{2,1,0:T(8,128)(2,1)}), bf16[16,24,576]{2,1,0:T(8,128)(2,1)S(1)}, u32[]{:S(2)}, u32[]{:S(2)}) async-start(bf16[16,24,576]{2,1,0:T(8,128)(2,1)} %bitcast.23), calls=%async_computation.3 | async-start | bytes 983040 | tf_op jit(solution)/shard_map/exchange_rest/all_to_all | solution.py:248
  44.3 13.4 %all-to-all-done.3 = bf16[16,24,576]{2,1,0:T(8,128)(2,1)S(1)} async-done(((bf16[16,24,576]{2,1,0:T(8,128)(2,1)}), bf16[16,24,576]{2,1,0:T(8,128)(2,1)S(1)}, u32[]{:S(2)}, u32[]{:S(2)}) %all-to-all-start.3) | async-done | bytes 442400 | tf_op jit(solution)/shard_map/exchange_rest/all_to_all | solution.py:248
  60.0 1.6 fusion.15
  61.6 1.6 fusion.14
  63.2 1.6 fusion.13
  64.8 1.6 fusion.12
  67.9 1.6 fusion.10
  72.7 1.6 fusion.7
  74.3 1.6 fusion.6
  75.8 1.6 fusion.5
  77.4 1.6 fusion.4
  79.0 1.6 fusion.3
  80.6 1.6 fusion.2
  83.8 7.2 %all-to-all-start = ((bf16[16,128,512]{2,1,0:T(8,128)(2,1)}), bf16[16,128,512]{2,1,0:T(8,128)(2,1)}, u32[]{:S(2)}, u32[]{:S(2)}) async-start(bf16[16,128,512]{2,1,0:T(8,128)(2,1)} %fusion.1), calls=%async_computation | async-start | bytes 4194304 | tf_op jit(solution)/shard_map/columns_of_w_out/all_to_all | solution.py:266
  92.8 1.7 constant_dynamic-slice_fusion.1.tokens
  94.4 4.2 %shrink.1 = bf16[48,256]{1,0:T(8,128)(2,1)} custom-call(s32[25]{0:T(128)} %pad_add_fusion.1.index, bf16[192,48,512]{2,1,0:T(8,128)(2,1)} %all-gather.7.cloned.1.call-done.pool, bf16[13,48,512]{2,1,0:T(8,128)(2,1)} %slot.2, bf16[256,512]{1,0:T(8,128)(2,1)} %constant_dynamic-slice_fusion.1.tokens, s32[1,256]{1,0:T(1,128)} %bitcast.116), custom_call_target="tpu_custom_call" | custom-call | flops 314572800 | bytes 2097152 | tf_op jit(solution)/shard_map/shrink/shrink/pallas_call | solution.py:282
  98.7 30.5 %all-to-all-done.mine = bf16[16,128,512]{2,1,0:T(8,128)(2,1)} async-done(((bf16[16,128,512]{2,1,0:T(8,128)(2,1)}), bf16[16,128,512]{2,1,0:T(8,128)(2,1)}, u32[]{:S(2)}, u32[]{:S(2)}) %all-to-all-start) | async-done | bytes 2097184 | tf_op jit(solution)/shard_map/columns_of_w_out/all_to_all | solution.py:266
  129.2 3.6 %fusion.25 = f32[256,32]{1,0:T(8,128)S(1)} fusion(bf16[256,8192]{1,0:T(8,128)(2,1)} %bitcast.129, bf16[8192,32]{0,1:T(8,128)(2,1)S(1)} %copy-done), kind=kOutput, calls=%fused_computation.68 | convolution fusion | flops 134217728 | bytes 4751360 | tf_op jit(solution)/shard_map/base_projections/dot_general | solution.py:275
  132.8 3.6 %fusion.23.base_q = f32[256,256]{1,0:T(8,128)S(1)} fusion(bf16[256,8192]{1,0:T(8,128)(2,1)S(1)} %bitcast.131, bf16[8192,256]{1,0:T(8,128)(2,1)} %param.25), kind=kOutput, calls=%fused_computation.66 | convolution fusion | flops 1073741824 | bytes 8650752 | tf_op jit(solution)/shard_map/base_projections/dot_general | solution.py:271
  137.1 3.6 %all-to-all-start.1 = ((bf16[16,48,256]{2,1,0:T(8,128)(2,1)}), bf16[16,48,256]{2,1,0:T(8,128)(2,1)S(1)}, u32[]{:S(2)}, u32[]{:S(2)}) async-start(bf16[16,48,256]{2,1,0:T(8,128)(2,1)} %broadcast_in_dim.63), calls=%async_computation.1 | async-start | bytes 786432 | tf_op jit(solution)/shard_map/shrink/all_to_all | solution.py:299
  140.7 3.5 %fusion.24 = f32[256,32]{1,0:T(8,128)S(1)} fusion(bf16[256,8192]{1,0:T(8,128)(2,1)} %bitcast.130, bf16[8192,32]{0,1:T(8,128)(2,1)S(1)} %copy-done.12), kind=kOutput, calls=%fused_computation.67 | convolution fusion | flops 134217728 | bytes 4751360 | tf_op jit(solution)/shard_map/base_projections/dot_general | solution.py:274
  144.5 11.5 %all-to-all-done.1.parts = bf16[16,48,256]{2,1,0:T(8,128)(2,1)S(1)} async-done(((bf16[16,48,256]{2,1,0:T(8,128)(2,1)}), bf16[16,48,256]{2,1,0:T(8,128)(2,1)S(1)}, u32[]{:S(2)}, u32[]{:S(2)}) %all-to-all-start.1) | async-done | bytes 393248 | tf_op jit(solution)/shard_map/shrink/all_to_all | solution.py:299
  157.1 3.5 %all-to-all-start.4 = ((bf16[16,16,320]{2,1,0:T(8,128)(2,1)}), bf16[16,16,320]{2,1,0:T(8,128)(2,1)S(1)}, u32[]{:S(2)}, u32[]{:S(2)}) async-start(bf16[16,16,320]{2,1,0:T(8,128)(2,1)} %convert_element_type.11), calls=%async_computation.4 | async-start | bytes 393216 | tf_op jit(solution)/shard_map/project/all_to_all | solution.py:311
  160.9 8.1 %all-to-all-done.4 = bf16[16,16,320]{2,1,0:T(8,128)(2,1)S(1)} async-done(((bf16[16,16,320]{2,1,0:T(8,128)(2,1)}), bf16[16,16,320]{2,1,0:T(8,128)(2,1)S(1)}, u32[]{:S(2)}, u32[]{:S(2)}) %all-to-all-start.4) | async-done | bytes 163872 | tf_op jit(solution)/shard_map/project/all_to_all | solution.py:311
  171.5 9.4 %attend.1 = bf16[8,64,128]{2,1,0:T(8,128)(2,1)} custom-call(s32[8]{0:T(128)} %lengths.1, bf16[8,64,128]{2,1,0:T(8,128)(2,1)} %bitcast.124, bf16[8,2,512]{2,1,0:T(2,128)(2,1)} %squeeze.35.keys_new, bf16[8,2,512]{2,1,0:T(2,128)(2,1)} %squeeze.36.values_new, bf16[8,512,512]{2,1,0:T(8,128)(2,1)} %keys.1, bf16[8,512,512]{2,1,0:T(8,128)(2,1)} %values.1), custom_call_target="tpu_custom_call" | custom-call | flops 536870912 | bytes 8388608 | tf_op jit(solution)/shard_map/attend/attend/pallas_call | solution.py:321
  181.9 2.0 copy-done.1
  186.6 3.9 %all-to-all-start.5 = ((bf16[16,17,16,256]{3,2,1,0:T(8,128)(2,1)}), bf16[16,17,16,256]{3,2,1,0:T(8,128)(2,1)S(1)}, u32[]{:S(2)}, u32[]{:S(2)}) async-start(bf16[16,17,16,256]{3,2,1,0:T(8,128)(2,1)} %broadcast_in_dim.65), calls=%async_computation.5 | async-start | bytes 4456448 | tf_op jit(solution)/shard_map/attend/all_to_all | solution.py:352
  190.6 29.6 %all-to-all-done.5.attended = bf16[16,17,16,256]{3,2,1,0:T(8,128)(2,1)S(1)} async-done(((bf16[16,17,16,256]{3,2,1,0:T(8,128)(2,1)}), bf16[16,17,16,256]{3,2,1,0:T(8,128)(2,1)S(1)}, u32[]{:S(2)}, u32[]{:S(2)}) %all-to-all-start.5) | async-done | bytes 2228256 | tf_op jit(solution)/shard_map/attend/all_to_all | solution.py:352
  220.2 1.9 copy-done.2
  222.1 4.8 %output.1 = f32[2,128,512]{2,1,0:T(8,128)S(1)} custom-call(s32[25]{0:T(128)S(1)} %copy-done.5, s32[1]{0:T(128)} %bitcast.3.side, bf16[16,17,16,256]{3,2,1,0:T(8,128)(2,1)S(1)} %all-to-all-done.5.attended, s32[256,1]{1,0:T(8,128)S(1)} %reshape.114.entry, bf16[16,128,512]{2,1,0:T(8,128)(2,1)} %all-to-all-done.mine, ...), custom_call_target="tpu_custom_call" | custom-call | flops 1178599424 | bytes 7340032 | tf_op jit(solution)/shard_map/output/output/pallas_call | solution.py:358
  (93 shorter events, 29.3 us)
Async XLA Ops:
  6.5 122.6 %copy-start = (bf16[8192,32]{0,1:T(8,128)(2,1)S(1)}, bf16[8192,32]{0,1:T(8,128)(2,1)}, u32[]{:S(2)}) copy-start(bf16[8192,32]{0,1:T(8,128)(2,1)} %param.27) | copy-start | bytes 1572868
  6.5 13.8 %copy-start.9 = (s32[192]{0:T(256)S(1)}, s32[192]{0:T(256)}, u32[]{:S(2)}) copy-start(s32[192]{0:T(256)} %param.35) | copy-start | bytes 2308
  6.5 13.9 %copy-start.8 = (s32[2,192]{1,0:T(2,128)S(1)}, s32[2,192]{1,0:T(2,128)}, u32[]{:S(2)}) copy-start(s32[2,192]{1,0:T(2,128)} %param.34) | copy-start | bytes 4612
  6.5 87.9 %all-gather.7.cloned.1.call-start = ((), (), s32[]{:S(2)}) async-start(), calls=%async_computation.6 | async-start | bytes 10027008 | tf_op jit(solution)/shard_map/gather_in_maps/all_gather | solution.py:213
  11.7 29.1 %copy-start.11 = (s32[2,192]{1,0:T(2,128)S(1)}, s32[2,192]{1,0:T(2,128)}, u32[]{:S(2)}) copy-start(s32[2,192]{1,0:T(2,128)} %param.33) | copy-start | bytes 4612
  11.7 20.6 %all-to-all-start.2 = ((bf16[16,12,576]{2,1,0:T(8,128)(2,1)}), bf16[16,12,576]{2,1,0:T(8,128)(2,1)S(1)}, u32[]{:S(2)}, u32[]{:S(2)}) async-start(bf16[16,12,576]{2,1,0:T(8,128)(2,1)} %maximum_bitcast_fusion), calls=%async_computation.2 | async-start | bytes 655360 | tf_op jit(solution)/shard_map/exchange_rest/all_to_all | solution.py:243
  33.8 23.8 %all-to-all-start.3 = ((bf16[16,24,576]{2,1,0:T(8,128)(2,1)}), bf16[16,24,576]{2,1,0:T(8,128)(2,1)S(1)}, u32[]{:S(2)}, u32[]{:S(2)}) async-start(bf16[16,24,576]{2,1,0:T(8,128)(2,1)} %bitcast.23), calls=%async_computation.3 | async-start | bytes 983040 | tf_op jit(solution)/shard_map/exchange_rest/all_to_all | solution.py:248
  40.7 141.2 %all-gather.9.cloned.1.call-start = ((), (), s32[]{:S(2)}) async-start(), calls=%async_computation.7 | async-start | bytes 3481600 | tf_op jit(solution)/shard_map/exchange_rest/all_gather | solution.py:260
  83.8 8.3 %copy-start.10 = (s32[2,128]{1,0:T(2,128)S(1)}, s32[2,128]{1,0:T(2,128)}, u32[]{:S(2)}) copy-start(s32[2,128]{1,0:T(2,128)} %param.32) | copy-start | bytes 3076
  83.8 45.4 %all-to-all-start = ((bf16[16,128,512]{2,1,0:T(8,128)(2,1)}), bf16[16,128,512]{2,1,0:T(8,128)(2,1)}, u32[]{:S(2)}, u32[]{:S(2)}) async-start(bf16[16,128,512]{2,1,0:T(8,128)(2,1)} %fusion.1), calls=%async_computation | async-start | bytes 4194304 | tf_op jit(solution)/shard_map/columns_of_w_out/all_to_all | solution.py:266
  91.0 129.2 %all-gather.11.cloned.1.call-start = ((), (), s32[]{:S(2)}) async-start(), calls=%async_computation.8 | async-start | bytes 3342336 | tf_op jit(solution)/shard_map/shrink/all_gather | solution.py:297
  129.2 3.6 %copy-start.7 = (bf16[2,128,8192]{2,1,0:T(8,128)(2,1)S(1)}, bf16[2,128,8192]{2,1,0:T(8,128)(2,1)}, u32[]{:S(2)}) copy-start(bf16[2,128,8192]{2,1,0:T(8,128)(2,1)} %param.24) | copy-start | bytes 12582916
  132.8 3.6 %copy-start.6 = (bf16[48,256]{1,0:T(8,128)(2,1)S(1)}, bf16[48,256]{1,0:T(8,128)(2,1)}, u32[]{:S(2)}) copy-start(bf16[48,256]{1,0:T(8,128)(2,1)} %shrink.1) | copy-start | bytes 73732
  132.8 7.9 %copy-start.12 = (bf16[8192,32]{0,1:T(8,128)(2,1)S(1)}, bf16[8192,32]{0,1:T(8,128)(2,1)}, u32[]{:S(2)}) copy-start(bf16[8192,32]{0,1:T(8,128)(2,1)} %param.26) | copy-start | bytes 1572868
  137.1 18.8 %all-to-all-start.1 = ((bf16[16,48,256]{2,1,0:T(8,128)(2,1)}), bf16[16,48,256]{2,1,0:T(8,128)(2,1)S(1)}, u32[]{:S(2)}, u32[]{:S(2)}) async-start(bf16[16,48,256]{2,1,0:T(8,128)(2,1)} %broadcast_in_dim.63), calls=%async_computation.1 | async-start | bytes 786432 | tf_op jit(solution)/shard_map/shrink/all_to_all | solution.py:299
  144.2 11.8 %copy-start.4 = (s32[2,128]{1,0:T(2,128)S(1)}, s32[2,128]{1,0:T(2,128)}, u32[]{:S(2)}) copy-start(s32[2,128]{1,0:T(2,128)} %fusion.17) | copy-start | bytes 3076
  157.1 11.8 %all-to-all-start.4 = ((bf16[16,16,320]{2,1,0:T(8,128)(2,1)}), bf16[16,16,320]{2,1,0:T(8,128)(2,1)S(1)}, u32[]{:S(2)}, u32[]{:S(2)}) async-start(bf16[16,16,320]{2,1,0:T(8,128)(2,1)} %convert_element_type.11), calls=%async_computation.4 | async-start | bytes 393216 | tf_op jit(solution)/shard_map/project/all_to_all | solution.py:311
  160.8 29.8 %collective-permute-start = (bf16[16,128,512]{2,1,0:T(8,128)(2,1)}, bf16[16,128,512]{2,1,0:T(8,128)(2,1)}, u32[]{:S(2)}, u32[]{:S(2)}) collective-permute-start(bf16[16,128,512]{2,1,0:T(8,128)(2,1)} %all-to-all-done.mine), channel_id=1, source_target_pairs={{0,16},{16,0},{32,48},{48,32},{64,80},{80,64},{96,112},{112,96},{1... | collective-permute-start | bytes 6291464 | tf_op jit(solution)/shard_map/columns_of_w_out/ppermute | solution.py:267
  181.9 2.0 copy-start.1
  186.6 33.6 %copy-start.3 = (bf16[13,16,512]{2,1,0:T(8,128)(2,1)S(1)}, bf16[13,16,512]{2,1,0:T(8,128)(2,1)}, u32[]{:S(2)}) copy-start(bf16[13,16,512]{2,1,0:T(8,128)(2,1)} %slot.3) | copy-start | bytes 638980
  186.6 33.6 %copy-start.5 = (s32[25]{0:T(128)S(1)}, s32[25]{0:T(128)}, u32[]{:S(2)}) copy-start(s32[25]{0:T(128)} %pad_add_fusion.1.index) | copy-start | bytes 304
  186.6 33.6 %all-to-all-start.5 = ((bf16[16,17,16,256]{3,2,1,0:T(8,128)(2,1)}), bf16[16,17,16,256]{3,2,1,0:T(8,128)(2,1)S(1)}, u32[]{:S(2)}, u32[]{:S(2)}) async-start(bf16[16,17,16,256]{3,2,1,0:T(8,128)(2,1)} %broadcast_in_dim.65), calls=%async_computation.5 | async-start | bytes 4456448 | tf_op jit(solution)/shard_map/attend/all_to_all | solution.py:352
  220.2 1.9 copy-start.2
Sparse Core Ops, SparseCore 0:
  9.2 77.2 all-gather.6
  88.9 69.7 all-gather.8
  160.6 39.6 all-gather.10

commit v3 on v2

v3 whole, which is shorter than its diff:
```python
import math

import jax
import jax.numpy as jnp
from jax import lax
from jax.experimental import pallas as pl
from jax.experimental.pallas import tpu as pltpu
from jax.sharding import PartitionSpec as P

QH = 32
KH = 4
HD = 128
STEPS = 2
ROWS = 128
RANK = 16
LOADS = 12
SLOTS = 13
HELD = 12
N = 16
ALL_ROWS = STEPS * ROWS
LOCAL = ROWS // N
MINE = STEPS * LOCAL
ENTRIES = 1 + STEPS * LOADS
IN_RANK = 3 * RANK
PER_DOT = 5
QF = 256
KF = 32
IN_PART = 512
OUT_PART = 512
FEATURES = QH * HD
LENGTH = 512
KW = KH * HD
BF16 = jnp.bfloat16
F32 = jnp.float32
low_rank_scale = 0.5


def vmem():
    return pl.BlockSpec(memory_space=pltpu.VMEM)


def hbm():
    return pl.BlockSpec(memory_space=pl.ANY)


def smem():
    return pl.BlockSpec(memory_space=pltpu.SMEM)


def params(mib=40):
    return pltpu.CompilerParams(vmem_limit_bytes=mib * 1024 * 1024)


def cost(flops, nbytes):
    return pl.CostEstimate(flops=flops, bytes_accessed=nbytes, transcendentals=0)


def iota(shape, axis):
    return lax.broadcasted_iota(jnp.int32, shape, axis)


def shrink_kernel(index, pool, slot, tokens, entry, out, maps, arrived):
    copies = []
    for i in range(ENTRIES):
        origin = slot.at[index[0]] if i == 0 else pool.at[index[i]]
        copy = pltpu.make_async_copy(origin, maps.at[pl.ds(i * IN_RANK, IN_RANK)], arrived.at[i])
        copy.start()
        copies.append(copy)
    used = entry[...]
    total = jnp.zeros((IN_RANK, ALL_ROWS), F32)
    for first in range(0, ENTRIES, PER_DOT):
        for i in range(first, first + PER_DOT):
            copies[i].wait()
        block = maps[pl.ds(first * IN_RANK, PER_DOT * IN_RANK), :]
        product = lax.dot_general(
            block, tokens[...], (((1,), (1,)), ((), ())), preferred_element_type=F32
        )
        for k in range(PER_DOT):
            piece = product[k * IN_RANK : (k + 1) * IN_RANK]
            total = total + jnp.where(used == first + k, piece, 0.0)
    out[...] = total.astype(BF16)


def expand(shrunk, entry):
    loads = STEPS * LOADS
    load = iota((loads, ALL_ROWS), 0) + 1
    chosen = load == entry
    blocks = [jnp.where(chosen, shrunk[r : r + 1, :], 0.0) for r in range(RANK)]
    kept = jnp.where(entry == 0, shrunk, 0.0)
    return jnp.concatenate(blocks + [kept], axis=0).astype(BF16)


def contract(left, right):
    return lax.dot_general(left, right, (((0,), (0,)), ((), ())), preferred_element_type=F32)


def project_kernel(parts, entry, base_q, base_kv, up_q, up_kv, out):
    shrunk = jnp.sum(parts[...].astype(F32), axis=0).astype(BF16).astype(F32)
    used = entry[...]
    wide_q = expand(shrunk[:RANK], used)
    wide_k = expand(shrunk[RANK : 2 * RANK], used)
    wide_v = expand(shrunk[2 * RANK :], used)
    query = base_q[...] + low_rank_scale * contract(wide_q, up_q[...])
    delta_k = contract(wide_k, up_kv[...])
    delta_v = contract(wide_v, up_kv[...])
    column = iota(delta_k.shape, 1)
    delta = jnp.where(column < KF, delta_k, delta_v)
    fresh = base_kv[...] + low_rank_scale * delta
    for t in range(N):
        lows = [s * ROWS + t * LOCAL for s in range(STEPS)]
        out[t, :, :QF] = jnp.concatenate([query[n : n + LOCAL] for n in lows], 0).astype(BF16)
        out[t, :, QF:] = jnp.concatenate([fresh[n : n + LOCAL] for n in lows], 0).astype(BF16)


def split_kernel(side, weight, out, arrived):
    rows = pl.ds(pl.multiple_of(side[0] * (QF // 2), QF // 2), QF // 2)
    copies = [
        pltpu.make_async_copy(
            weight.at[rows, pl.ds(t * OUT_PART, OUT_PART)], out.at[t], arrived.at[t]
        )
        for t in range(N)
    ]
    for copy in copies:
        copy.start()
    for copy in copies:
        copy.wait()


def transposing():
    shape = (N * MINE, N * MINE)
    row, column = iota(shape, 0), iota(shape, 1)
    return ((row // N == column % N) & (row % N == column // N)).astype(BF16)


def attend_kernel(
    lengths, received, entry, keys, values, maps, out, key_rows, value_rows, map_rows, by_row,
    key_sem, value_sem, map_sem,
):
    loads = []
    for i in range(LOCAL):
        pair = (
            pltpu.make_async_copy(keys.at[i], key_rows.at[i], key_sem.at[i]),
            pltpu.make_async_copy(values.at[i], value_rows.at[i], value_sem.at[i]),
        )
        for copy in pair:
            copy.start()
        loads.append(pair)
    maps_load = pltpu.make_async_copy(maps, map_rows, map_sem)
    maps_load.start()

    swap = transposing()
    mine = jnp.dot(swap, received[...].reshape(N * MINE, -1), preferred_element_type=F32)
    mine = mine.astype(BF16)
    shape = (2 * KF, KW)
    feature, column = iota(shape, 0), iota(shape, 1) % KF
    block = iota((N * MINE, KW), 1) // KF == iota((N * MINE, KW), 0) % N
    fold = (iota((MINE, N * MINE), 1) // N == iota((MINE, N * MINE), 0)).astype(BF16)

    def fresh(first):
        repeat = (feature - first == column).astype(BF16)
        wide = jnp.dot(mine[:, QF:], repeat, preferred_element_type=F32)
        wide = jnp.where(block, wide, 0.0).astype(BF16)
        return jnp.dot(fold, wide, preferred_element_type=F32).astype(BF16)

    keys_new, values_new = fresh(0), fresh(KF)

    head_rows = STEPS * QH
    own = iota((head_rows, KW), 0) % N // (N // KH) == iota((head_rows, KW), 1) // HD
    place = iota((head_rows, LENGTH), 1)
    shape = (head_rows, MINE)
    new_step, new_row = iota(shape, 1) // LOCAL, iota(shape, 1) % LOCAL
    in_time = new_step <= iota(shape, 0) // QH
    scale = 1.0 / math.sqrt(HD)
    dims = (((1,), (1,)), ((), ()))
    for i in range(LOCAL):
        asked = []
        for s in range(STEPS):
            low = (s * LOCAL + i) * N
            asked += [mine[low : low + N, :HD], mine[low : low + N, HD:QF]]
        asked = jnp.concatenate(asked, axis=0)
        spread = jnp.where(own, jnp.concatenate([asked] * KH, axis=1), jnp.zeros((), BF16))
        new = lax.dot_general(spread, keys_new, dims, preferred_element_type=F32) * scale
        new = jnp.where(in_time & (new_row == i), new, -jnp.inf)
        loads[i][0].wait()
        old = lax.dot_general(spread, key_rows[i], dims, preferred_element_type=F32) * scale
        old = jnp.where(place < lengths[i], old, -jnp.inf)
        highest = jnp.maximum(
            jnp.max(old, axis=1, keepdims=True), jnp.max(new, axis=1, keepdims=True)
        )
        old, new = jnp.exp(old - highest), jnp.exp(new - highest)
        totals = jnp.sum(old, axis=1, keepdims=True) + jnp.sum(new, axis=1, keepdims=True)
        loads[i][1].wait()
        mixed = jnp.dot(old.astype(BF16), value_rows[i], preferred_element_type=F32)
        mixed = mixed + jnp.dot(new.astype(BF16), values_new, preferred_element_type=F32)
        mixed = jnp.where(own, mixed, 0.0)
        attended = mixed[:, :HD]
        for k in range(1, KH):
            attended = attended + mixed[:, k * HD : (k + 1) * HD]
        attended = (attended / totals).astype(BF16)
        for s in range(STEPS):
            low = (s * LOCAL + i) * N
            for half in range(2):
                piece = attended[(2 * s + half) * N : (2 * s + half + 1) * N]
                by_row[low : low + N, half * HD : (half + 1) * HD] = piece

    attended = jnp.dot(swap, by_row[...], preferred_element_type=F32).astype(BF16)
    maps_load.wait()
    total = jnp.zeros((MINE, ENTRIES * RANK), F32)
    for t in range(N):
        total = total + lax.dot_general(
            attended[t * MINE : (t + 1) * MINE], map_rows[t], dims, preferred_element_type=F32
        )
    column = iota(total.shape, 1)
    placed = jnp.where(order_of(column) == entry[...], total, 0.0).astype(BF16)
    shape = (ENTRIES * RANK, QF)
    gather = (rank_of(iota(shape, 0)) == iota(shape, 1)).astype(BF16)
    shrunk = jnp.dot(placed, gather, preferred_element_type=F32).astype(BF16)
    for n in range(N):
        for t in range(N):
            out[n, t] = attended[t * MINE : (t + 1) * MINE]
        out[n, N] = shrunk


def order_of(column):
    loads = STEPS * LOADS
    return jnp.where(column < RANK * loads, column % loads + 1, 0)


def rank_of(column):
    loads = STEPS * LOADS
    return jnp.where(column < RANK * loads, column // loads, column - RANK * loads)


def output_kernel(index, side, attended, entry, mine, others, pool, slot, out, up, arrived):
    copies = []
    for i in range(ENTRIES):
        origin = slot.at[index[0]] if i == 0 else pool.at[index[i]]
        copy = pltpu.make_async_copy(origin, up.at[pl.ds(i * RANK, RANK)], arrived.at[i])
        copy.start()
        copies.append(copy)
    total = jnp.zeros((ALL_ROWS, OUT_PART), F32)
    for t in range(N):
        low = attended[:, t, :, : QF // 2].reshape(ALL_ROWS, QF // 2)
        high = attended[:, t, :, QF // 2 :].reshape(ALL_ROWS, QF // 2)
        near = jnp.where(side[0] == 0, low, high)
        far = jnp.where(side[0] == 0, high, low)
        left = jnp.concatenate([near, far], axis=1)
        right = jnp.concatenate([mine[t], others[t]], axis=0)
        total = total + jnp.dot(left, right, preferred_element_type=F32)
    shrunk = attended[:, N].reshape(ALL_ROWS, QF)
    shape = (QF, ENTRIES * RANK)
    repeat = iota(shape, 1) % RANK == lax.broadcasted_iota(
        jnp.int32, shape, 0
    )
    wide = jnp.dot(shrunk, repeat.astype(BF16), preferred_element_type=F32)
    column = iota(wide.shape, 1)
    wide = jnp.where(column // RANK == entry[...], wide, 0.0).astype(BF16)
    for copy in copies:
        copy.wait()
    total = total + low_rank_scale * jnp.dot(wide, up[...], preferred_element_type=F32)
    for s in range(STEPS):
        lows = [t * MINE + s * LOCAL for t in range(N)]
        out[s] = jnp.concatenate([total[n : n + LOCAL] for n in lows], axis=0).astype(BF16)


def shard(
    hidden, w_query, w_key, w_value, w_out, key_cache, value_cache, lengths, row_slot, evict_slot,
    evict_adapter, owner, pool_a_in, pool_b_q, pool_b_k, pool_b_v, pool_a_o, pool_b_o,
    slot_a_in, slot_b_q, slot_b_k, slot_b_v, slot_a_o, slot_b_o,
):
    me = lax.axis_index("group")
    part = lax.axis_index("tp")

    with jax.named_scope("gather_in_maps"):
        whole_in = lax.all_gather(pool_a_in, "group").reshape(N * HELD, IN_RANK, IN_PART)

    with jax.named_scope("positions"):
        position = jnp.sum(
            jnp.where(evict_adapter[..., None] == jnp.arange(N * HELD), owner, 0), axis=-1
        )
        wanted = position.reshape(STEPS, N, LOADS).transpose(1, 0, 2).reshape(N, STEPS * LOADS)
        targets = lax.dynamic_slice_in_dim(evict_slot, me * LOADS, LOADS, 1)
        survivor = SLOTS * (SLOTS - 1) // 2 - jnp.sum(targets[0])
        placed = targets[:, :, None] == jnp.arange(SLOTS)
        order = 1 + jnp.arange(STEPS * LOADS).reshape(STEPS, LOADS, 1)
        slot_entry = jnp.sum(jnp.where(placed, order, 0), axis=1)
        second = jnp.where(slot_entry[1] > 0, slot_entry[1], slot_entry[0])
        slot_entry = jnp.stack([slot_entry[0], second])
        entry = jnp.sum(
            jnp.where(
                row_slot[:, :, None] == jnp.arange(SLOTS), slot_entry[:, None, :], 0
            ),
            axis=-1,
        )
        by_step = entry.reshape(1, ALL_ROWS)
        by_owner = entry.reshape(STEPS, N, LOCAL).transpose(1, 0, 2)
        of_mine = lax.dynamic_index_in_dim(by_owner, part, 0, keepdims=False).reshape(MINE, 1)
        by_owner = by_owner.reshape(ALL_ROWS, 1)
        my_wanted = lax.dynamic_index_in_dim(wanted, me, 0, keepdims=False)
        index = jnp.concatenate([survivor[None], my_wanted]).astype(jnp.int32)

    with jax.named_scope("columns_of_w_out"):
        side = (me % 2)[None]
        half = pl.pallas_call(
            split_kernel,
            out_shape=jax.ShapeDtypeStruct((N, QF // 2, OUT_PART), BF16),
            in_specs=[smem(), hbm()],
            out_specs=vmem(),
            scratch_shapes=[pltpu.SemaphoreType.DMA((N,))],
            compiler_params=params(56),
            cost_estimate=cost(0, 4 << 20),
            name="split",
        )(side, w_out)
        mine = lax.all_to_all(half, "tp", split_axis=0, concat_axis=0, tiled=True)
        others = lax.ppermute(mine, "group", [(i, i ^ 1) for i in range(N)])

    with jax.named_scope("base_projections"):
        tokens = hidden.reshape(ALL_ROWS, -1)
        base_q = jnp.dot(tokens, w_query, preferred_element_type=F32)
        base_kv = jnp.concatenate(
            [
                jnp.dot(tokens, w_key, preferred_element_type=F32),
                jnp.dot(tokens, w_value, preferred_element_type=F32),
            ],
            axis=1,
        )
        tokens_part = lax.dynamic_slice_in_dim(tokens, part * IN_PART, IN_PART, 1)

    with jax.named_scope("exchange_rest"):
        rest = jnp.concatenate([pool_b_q, pool_b_k, pool_b_v, pool_a_o], axis=2)
        width = rest.shape[2]
        rest, mine, base_q, base_kv, tokens_part = lax.optimization_barrier(
            (rest, mine, base_q, base_kv, tokens_part)
        )
        by_rank = lax.all_to_all(
            rest.transpose(1, 0, 2), "group", split_axis=0, concat_axis=0, tiled=True
        ).reshape(N * HELD, width)
        pick = (wanted.reshape(-1, 1) == jnp.arange(N * HELD)).astype(BF16)
        sent = jnp.dot(pick, by_rank, preferred_element_type=F32).astype(BF16)
        loaded = lax.all_to_all(
            sent.reshape(N, STEPS * LOADS, width), "group", split_axis=0, concat_axis=0, tiled=True
        ).reshape(RANK * STEPS * LOADS, width)
        kept = jnp.concatenate(
            [
                lax.dynamic_index_in_dim(piece, survivor, 0, keepdims=False)
                for piece in (slot_b_q, slot_b_k, slot_b_v, slot_a_o)
            ],
            axis=1,
        )
        up = jnp.concatenate([loaded, kept], axis=0)
        up_q, up_kv, out_maps = up[:, :QF], up[:, QF : QF + 2 * KF], up[:, QF + 2 * KF :]
        whole_out_maps = lax.all_gather(out_maps, "tp")

    with jax.named_scope("shrink"):
        partial_in = pl.pallas_call(
            shrink_kernel,
            out_shape=jax.ShapeDtypeStruct((IN_RANK, ALL_ROWS), BF16),
            in_specs=[smem(), hbm(), hbm(), vmem(), vmem()],
            out_specs=vmem(),
            scratch_shapes=[
                pltpu.VMEM((ENTRIES * IN_RANK, IN_PART), BF16),
                pltpu.SemaphoreType.DMA((ENTRIES,)),
            ],
            compiler_params=params(56),
            cost_estimate=cost(2 * ENTRIES * IN_RANK * IN_PART * ALL_ROWS, 2 << 20),
            name="shrink",
        )(index, whole_in, slot_a_in, tokens_part, by_step)
        partial_in, pool_b_o = lax.optimization_barrier((partial_in, pool_b_o))
        whole_b_o = lax.all_gather(pool_b_o, "group").reshape(N * HELD, RANK, OUT_PART)
        copies = jnp.broadcast_to(partial_in, (N, IN_RANK, ALL_ROWS))
        partials = lax.all_to_all(copies, "tp", split_axis=0, concat_axis=0, tiled=True)

    with jax.named_scope("project"):
        projected = pl.pallas_call(
            project_kernel,
            out_shape=jax.ShapeDtypeStruct((N, MINE, QF + 2 * KF), BF16),
            in_specs=[vmem()] * 6,
            out_specs=vmem(),
            compiler_params=params(),
            cost_estimate=cost(2 * 400 * 512 * ALL_ROWS, 1 << 20),
            name="project",
        )(partials, by_step, base_q, base_kv, up_q, up_kv)
        received = lax.all_to_all(projected, "tp", split_axis=0, concat_axis=0, tiled=True)

    with jax.named_scope("attend"):
        payload = pl.pallas_call(
            attend_kernel,
            out_shape=jax.ShapeDtypeStruct((N, N + 1, MINE, QF), BF16),
            in_specs=[smem(), vmem(), vmem(), hbm(), hbm(), hbm()],
            out_specs=vmem(),
            scratch_shapes=[
                pltpu.VMEM((LOCAL, LENGTH, KW), BF16),
                pltpu.VMEM((LOCAL, LENGTH, KW), BF16),
                pltpu.VMEM((N, ENTRIES * RANK, QF), BF16),
                pltpu.VMEM((N * MINE, QF), BF16),
                pltpu.SemaphoreType.DMA((LOCAL,)),
                pltpu.SemaphoreType.DMA((LOCAL,)),
                pltpu.SemaphoreType.DMA,
            ],
            compiler_params=params(56),
            cost_estimate=cost(4 * LOCAL * 64 * KW * LENGTH, 12 << 20),
            name="attend",
        )(lengths, received, of_mine, key_cache, value_cache, whole_out_maps)
        gathered = lax.all_to_all(payload, "tp", split_axis=0, concat_axis=0, tiled=True)

    with jax.named_scope("output"):
        return pl.pallas_call(
            output_kernel,
            out_shape=jax.ShapeDtypeStruct((STEPS, ROWS, OUT_PART), BF16),
            in_specs=[smem(), smem(), vmem(), vmem(), vmem(), vmem(), hbm(), hbm()],
            out_specs=vmem(),
            scratch_shapes=[
                pltpu.VMEM((ENTRIES * RANK, OUT_PART), BF16),
                pltpu.SemaphoreType.DMA((ENTRIES,)),
            ],
            compiler_params=params(56),
            cost_estimate=cost(2 * ALL_ROWS * (FEATURES + 400) * OUT_PART, 7 << 20),
            name="output",
        )(index, side, gathered, by_owner, mine, others, whole_b_o, slot_b_o)


def solution(mesh):
    pooled = P("group", None, "tp")
    cached = P(("group", "tp"), None, None)
    placed = (
        P(None, "group", None), P(None, "tp"), P(None, "tp"), P(None, "tp"), P("tp", None),
        cached, cached, P(("group", "tp")), P(None, "group"), P(), P(), P(),
    ) + (pooled,) * 12
    return jax.shard_map(
        shard, mesh=mesh, in_specs=placed, out_specs=P(None, "group", "tp"), check_vma=False
    )
```

time: 238 us -> 213 us (0.89)
  local copies, waits for them, and re-layouts: 43.6 us -> 12.2 us
  Pallas kernels: 19.9 us -> 26.2 us
  waiting for transfers between devices: 105 us -> 110 us
    unnamed x45 -> x34, local copies, waits for them, and re-layouts: 31.1 us -> 2.76 us
    all_gather x1, waiting for transfers between devices: 0.02 us -> 21.8 us  [shard(): whole_out_maps = lax.all_gather(out_maps, 'tp')]
    all_to_all x1, waiting for transfers between devices: 30.5 us -> 22.4 us  [shard(): mine = lax.all_to_all(half, 'tp', split_axis=0, concat_axis=0, tiled=True)]
    all_to_all x2, waiting for transfers between devices: 37.7 us -> 31.8 us  [the longest x1 31.8 us: shard(): lax.all_to_all(payload, 'tp', split_axis=0, concat_axis=0, tiled=True)]
    pallas_call x2, Pallas kernels: 10.5 us -> 15.3 us  [the longest x1 12.2 us: shard(): pl.pallas_call(attend_kernel, out_shape=jax.ShapeDtypeStruct((N, N + 1, M...]
    all_to_all x1, waiting for transfers between devices: 13.4 us -> 9.84 us  [shard(): lax.all_to_all(sent.reshape(N, STEPS * LOADS, width), 'group', split_axis...]
  transfers between devices with their start and end apart: 10 -> 10, of which waited for: 6 -> 6; matrix products, arithmetic and copies ran while one was open for 24% -> 11% of each run, Pallas kernels for 6% -> 10%
where the time goes in v3:
time: 213 us; the launch traced here: 211 us
  waiting for transfers between devices  110 us (52%)
  starting transfers between devices  34.4 us (16%)
  Pallas kernels  26.2 us (12%)
  between operations  14.7 us (7%)
  local copies, waits for them, and re-layouts  12.2 us (6%)
  matrix products  8.63 us (4%)
  other arithmetic  4.92 us (2%)
    all_to_all x1, waiting for transfers between devices, shard(): lax.all_to_all(payload, 'tp', split_axis=0, concat_axis=0, tiled=True)  31.8 us
    all_to_all x1, waiting for transfers between devices, shard(): mine = lax.all_to_all(half, 'tp', split_axis=0, concat_axis=0, tiled=True)  22.4 us
    all_gather x1, waiting for transfers between devices, shard(): whole_out_maps = lax.all_gather(out_maps, 'tp')  21.8 us
    pallas_call x1, Pallas kernels, shard(): pl.pallas_call(attend_kernel, out_shape=jax.ShapeDtypeStruct((N, N + 1, M...  12.2 us
    all_to_all x1, waiting for transfers between devices, shard(): lax.all_to_all(rest.transpose(1, 0, 2), 'group', split_axis=0, concat_axi...  12 us
    all_to_all x1, waiting for transfers between devices, shard(): lax.all_to_all(copies, 'tp', split_axis=0, concat_axis=0, tiled=True)  11.4 us
    all_to_all x1, waiting for transfers between devices, shard(): lax.all_to_all(sent.reshape(N, STEPS * LOADS, width), 'group', split_axis...  9.84 us
    all_to_all x1, starting transfers between devices, shard(): lax.all_to_all(rest.transpose(1, 0, 2), 'group', split_axis=0, concat_axi...  8.59 us
  transfers between devices with their start and end apart: 10, of which 6 were waited for; matrix products, arithmetic and copies ran while one was open for 11% of the time, Pallas kernels for 10%

profile of v3, /device:TPU:32, one launch (start us, length us, event | category | flops | bytes accessed | tf_op | source)
XLA Modules:
  0.0 211.1 jit_solution(14891819315645828339)
XLA Ops:
  7.3 3.1 %split.1 = bf16[16,128,512]{2,1,0:T(8,128)(2,1)} custom-call(s32[1]{0:T(128)} %bitcast.3.side, bf16[256,8192]{1,0:T(8,128)(2,1)} %weight.1), custom_call_target="tpu_custom_call" | custom-call | bytes 4194304 | tf_op jit(solution)/shard_map/columns_of_w_out/split/pallas_call | solution.py:304
  10.4 7.0 %all-to-all-start = ((bf16[16,128,512]{2,1,0:T(8,128)(2,1)}), bf16[16,128,512]{2,1,0:T(8,128)(2,1)S(1)}, u32[]{:S(2)}, u32[]{:S(2)}) async-start(bf16[16,128,512]{2,1,0:T(8,128)(2,1)} %split.1), calls=%async_computation | async-start | bytes 4194304 | tf_op jit(solution)/shard_map/columns_of_w_out/all_to_all | solution.py:314
  17.7 3.6 %fusion.7 = f32[256,32]{1,0:T(8,128)S(1)} fusion(bf16[256,8192]{1,0:T(8,128)(2,1)} %bitcast.36, bf16[8192,32]{0,1:T(8,128)(2,1)S(1)} %copy-done), kind=kOutput, calls=%fused_computation.31 | convolution fusion | flops 134217728 | bytes 4751360 | tf_op jit(solution)/shard_map/base_projections/dot_general | solution.py:322
  21.3 2.4 %fusion.8 = f32[256,32]{1,0:T(8,128)S(1)} fusion(bf16[256,8192]{1,0:T(8,128)(2,1)S(1)} %bitcast.37, bf16[8192,32]{0,1:T(8,128)(2,1)} %param.27), kind=kOutput, calls=%fused_computation.32 | convolution fusion | flops 134217728 | bytes 4751360 | tf_op jit(solution)/shard_map/base_projections/dot_general | solution.py:323
  23.8 0.7 constant_dynamic-slice_fusion.1.tokens
  24.6 0.9 pad_maximum_fusion
  25.5 1.2 fusion.6.base_q
  26.7 22.4 %all-to-all-done.mine = bf16[16,128,512]{2,1,0:T(8,128)(2,1)S(1)} async-done(((bf16[16,128,512]{2,1,0:T(8,128)(2,1)}), bf16[16,128,512]{2,1,0:T(8,128)(2,1)S(1)}, u32[]{:S(2)}, u32[]{:S(2)}) %all-to-all-start) | async-done | bytes 2097184 | tf_op jit(solution)/shard_map/columns_of_w_out/all_to_all | solution.py:314
  49.2 8.6 %all-to-all-start.2 = ((bf16[16,12,576]{2,1,0:T(8,128)(2,1)}), bf16[16,12,576]{2,1,0:T(8,128)(2,1)S(1)}, u32[]{:S(2)}, u32[]{:S(2)}) async-start(bf16[16,12,576]{2,1,0:T(8,128)(2,1)} %bitcast.6), calls=%async_computation.2 | async-start | bytes 655360 | tf_op jit(solution)/shard_map/exchange_rest/all_to_all | solution.py:335
  58.2 12.0 %all-to-all-done.2 = bf16[16,12,576]{2,1,0:T(8,128)(2,1)S(1)} async-done(((bf16[16,12,576]{2,1,0:T(8,128)(2,1)}), bf16[16,12,576]{2,1,0:T(8,128)(2,1)S(1)}, u32[]{:S(2)}, u32[]{:S(2)}) %all-to-all-start.2) | async-done | bytes 221216 | tf_op jit(solution)/shard_map/exchange_rest/all_to_all | solution.py:335
  70.3 0.8 reshape.72
  71.1 1.4 convolution_convert_fusion
  72.5 1.0 copy.60
  73.5 7.2 %all-to-all-start.3 = ((bf16[16,24,576]{2,1,0:T(8,128)(2,1)}), bf16[16,24,576]{2,1,0:T(8,128)(2,1)S(1)}, u32[]{:S(2)}, u32[]{:S(2)}) async-start(bf16[16,24,576]{2,1,0:T(8,128)(2,1)} %bitcast.33), calls=%async_computation.3 | async-start | bytes 983040 | tf_op jit(solution)/shard_map/exchange_rest/all_to_all | solution.py:340
  84.0 0.7 dynamic-slice_bitcast_fusion
  84.7 9.8 %all-to-all-done.3 = bf16[16,24,576]{2,1,0:T(8,128)(2,1)S(1)} async-done(((bf16[16,24,576]{2,1,0:T(8,128)(2,1)}), bf16[16,24,576]{2,1,0:T(8,128)(2,1)S(1)}, u32[]{:S(2)}, u32[]{:S(2)}) %all-to-all-start.3) | async-done | bytes 442400 | tf_op jit(solution)/shard_map/exchange_rest/all_to_all | solution.py:340
  94.5 0.8 pad_maximum_fusion.1
  95.4 0.7 copy.57
  98.4 1.3 fusion.1
  99.7 4.2 %shrink.1 = bf16[48,256]{1,0:T(8,128)(2,1)} custom-call(s32[25]{0:T(128)} %pad_add_fusion.1.index, bf16[192,48,512]{2,1,0:T(8,128)(2,1)} %all-gather.7.cloned.1.call-done.pool, bf16[13,48,512]{2,1,0:T(8,128)(2,1)} %slot.2, bf16[256,512]{1,0:T(8,128)(2,1)} %constant_dynamic-slice_fusion.1.tokens, s32[1,256]{1,0:T(1,128)} %bitcast.27), custom_call_target="tpu_custom_call" | custom-call | flops 314572800 | bytes 2097152 | tf_op jit(solution)/shard_map/shrink/shrink/pallas_call | solution.py:355
  103.9 1.5 broadcast_in_dim.57
  105.4 3.6 %all-to-all-start.1 = ((bf16[16,48,256]{2,1,0:T(8,128)(2,1)}), bf16[16,48,256]{2,1,0:T(8,128)(2,1)S(1)}, u32[]{:S(2)}, u32[]{:S(2)}) async-start(bf16[16,48,256]{2,1,0:T(8,128)(2,1)} %broadcast_in_dim.57), calls=%async_computation.1 | async-start | bytes 786432 | tf_op jit(solution)/shard_map/shrink/all_to_all | solution.py:371
  109.2 11.4 %all-to-all-done.1.parts = bf16[16,48,256]{2,1,0:T(8,128)(2,1)S(1)} async-done(((bf16[16,48,256]{2,1,0:T(8,128)(2,1)}), bf16[16,48,256]{2,1,0:T(8,128)(2,1)S(1)}, u32[]{:S(2)}, u32[]{:S(2)}) %all-to-all-start.1) | async-done | bytes 393248 | tf_op jit(solution)/shard_map/shrink/all_to_all | solution.py:371
  120.6 1.1 project.1
  121.7 3.5 %all-to-all-start.4 = ((bf16[16,16,320]{2,1,0:T(8,128)(2,1)}), bf16[16,16,320]{2,1,0:T(8,128)(2,1)S(1)}, u32[]{:S(2)}, u32[]{:S(2)}) async-start(bf16[16,16,320]{2,1,0:T(8,128)(2,1)} %project.1), calls=%async_computation.4 | async-start | bytes 393216 | tf_op jit(solution)/shard_map/project/all_to_all | solution.py:383
  126.0 21.8 %all-gather.9.cloned.1.call-done = bf16[6400,256]{1,0:T(8,128)(2,1)} async-done(((bf16[400,256]{1,0:T(8,128)(2,1)}), bf16[6400,256]{1,0:T(8,128)(2,1)}) %all-gather.9.cloned.1.call-update) | async-done | bytes 3276816 | tf_op jit(solution)/shard_map/exchange_rest/all_gather | solution.py:352
  148.5 12.2 %attend.1 = bf16[16,17,16,256]{3,2,1,0:T(8,128)(2,1)} custom-call(s32[8]{0:T(128)} %lengths.1, bf16[16,16,320]{2,1,0:T(8,128)(2,1)} %copy-done.4, s32[16,1]{1,0:T(8,128)} %reshape.84.entry, bf16[8,512,512]{2,1,0:T(8,128)(2,1)} %keys.1, bf16[8,512,512]{2,1,0:T(8,128)(2,1)} %values.1, bf16[16,400,256]{2,1,0:T(8,128)(2,1)} %bitcast.32), custom_call_target="tpu_custom_call" | custom-call | flops 536870912 | bytes 12582912 | tf_op jit(solution)/shard_map/attend/attend/pallas_call | solution.py:386
  160.7 4.4 %all-to-all-start.5 = ((bf16[16,17,16,256]{3,2,1,0:T(8,128)(2,1)}), bf16[16,17,16,256]{3,2,1,0:T(8,128)(2,1)S(1)}, u32[]{:S(2)}, u32[]{:S(2)}) async-start(bf16[16,17,16,256]{3,2,1,0:T(8,128)(2,1)} %attend.1), calls=%async_computation.5 | async-start | bytes 4456448 | tf_op jit(solution)/shard_map/attend/all_to_all | solution.py:404
  165.1 0.8 reshape.85.entry
  165.8 31.8 %all-to-all-done.5.attended = bf16[16,17,16,256]{3,2,1,0:T(8,128)(2,1)S(1)} async-done(((bf16[16,17,16,256]{3,2,1,0:T(8,128)(2,1)}), bf16[16,17,16,256]{3,2,1,0:T(8,128)(2,1)S(1)}, u32[]{:S(2)}, u32[]{:S(2)}) %all-to-all-start.5) | async-done | bytes 2228256 | tf_op jit(solution)/shard_map/attend/all_to_all | solution.py:404
  197.6 1.4 copy-done.2
  199.0 5.6 %output.1 = bf16[2,128,512]{2,1,0:T(8,128)(2,1)} custom-call(s32[25]{0:T(128)} %pad_add_fusion.1.index, s32[1]{0:T(128)} %bitcast.3.side, bf16[16,17,16,256]{3,2,1,0:T(8,128)(2,1)} %copy-done.2, s32[256,1]{1,0:T(8,128)} %reshape.85.entry, bf16[16,128,512]{2,1,0:T(8,128)(2,1)} %copy-done.3, bf16[16,128,512]{2,1,0:T(8,128)(2,1)} %collective-permute-done.others, ...), custom_call_target="tpu_custom_call" | custom-call | flops 1178599424 | bytes 7340032 | tf_op jit(solution)/shard_map/output/output/pallas_call | solution.py:407
  (67 shorter events, 7.4 us)
Async XLA Ops:
  6.5 11.2 %copy-start = (bf16[8192,32]{0,1:T(8,128)(2,1)S(1)}, bf16[8192,32]{0,1:T(8,128)(2,1)}, u32[]{:S(2)}) copy-start(bf16[8192,32]{0,1:T(8,128)(2,1)} %param.26) | copy-start | bytes 1572868
  6.5 93.1 %all-gather.7.cloned.1.call-start = ((), (), s32[]{:S(2)}) async-start(), calls=%async_computation.6 | async-start | bytes 10027008 | tf_op jit(solution)/shard_map/gather_in_maps/all_gather | solution.py:275
  7.3 10.2 %copy-start.5 = (bf16[12,16,256]{2,1,0:T(8,128)(2,1)S(1)}, bf16[12,16,256]{2,1,0:T(8,128)(2,1)}, u32[]{:S(2)}) copy-start(bf16[12,16,256]{2,1,0:T(8,128)(2,1)} %param.37) | copy-start | bytes 294916
  7.3 10.3 %copy-start.6 = (bf16[12,16,256]{2,1,0:T(8,128)(2,1)S(1)}, bf16[12,16,256]{2,1,0:T(8,128)(2,1)}, u32[]{:S(2)}) copy-start(bf16[12,16,256]{2,1,0:T(8,128)(2,1)} %param.40) | copy-start | bytes 294916
  7.3 10.3 %copy-start.7 = (bf16[12,16,32]{2,1,0:T(8,128)(2,1)S(1)}, bf16[12,16,32]{2,1,0:T(8,128)(2,1)}, u32[]{:S(2)}) copy-start(bf16[12,16,32]{2,1,0:T(8,128)(2,1)} %param.38) | copy-start | bytes 36868
  7.3 10.3 %copy-start.8 = (bf16[12,16,32]{2,1,0:T(8,128)(2,1)S(1)}, bf16[12,16,32]{2,1,0:T(8,128)(2,1)}, u32[]{:S(2)}) copy-start(bf16[12,16,32]{2,1,0:T(8,128)(2,1)} %param.39) | copy-start | bytes 36868
  10.4 38.7 %all-to-all-start = ((bf16[16,128,512]{2,1,0:T(8,128)(2,1)}), bf16[16,128,512]{2,1,0:T(8,128)(2,1)S(1)}, u32[]{:S(2)}, u32[]{:S(2)}) async-start(bf16[16,128,512]{2,1,0:T(8,128)(2,1)} %split.1), calls=%async_computation | async-start | bytes 4194304 | tf_op jit(solution)/shard_map/columns_of_w_out/all_to_all | solution.py:314
  17.7 3.6 %copy-start.9 = (bf16[2,128,8192]{2,1,0:T(8,128)(2,1)S(1)}, bf16[2,128,8192]{2,1,0:T(8,128)(2,1)}, u32[]{:S(2)}) copy-start(bf16[2,128,8192]{2,1,0:T(8,128)(2,1)} %param.24) | copy-start | bytes 12582916
  21.3 4.2 %copy-start.14 = (bf16[8192,256]{1,0:T(8,128)(2,1)S(1)}, bf16[8192,256]{1,0:T(8,128)(2,1)}, u32[]{:S(2)}) copy-start(bf16[8192,256]{1,0:T(8,128)(2,1)} %param.25) | copy-start | bytes 12582916
  25.5 32.3 %copy-start.11 = (s32[2,192]{1,0:T(2,128)S(1)}, s32[2,192]{1,0:T(2,128)}, u32[]{:S(2)}) copy-start(s32[2,192]{1,0:T(2,128)} %param.34) | copy-start | bytes 4612
  25.5 32.3 %copy-start.12 = (s32[192]{0:T(256)S(1)}, s32[192]{0:T(256)}, u32[]{:S(2)}) copy-start(s32[192]{0:T(256)} %param.35) | copy-start | bytes 2308
  25.5 55.3 %copy-start.13 = (s32[2,192]{1,0:T(2,128)S(1)}, s32[2,192]{1,0:T(2,128)}, u32[]{:S(2)}) copy-start(s32[2,192]{1,0:T(2,128)} %param.33) | copy-start | bytes 4612
  49.2 50.5 %copy-start.3 = (bf16[16,128,512]{2,1,0:T(8,128)(2,1)}, bf16[16,128,512]{2,1,0:T(8,128)(2,1)S(1)}, u32[]{:S(2)}) copy-start(bf16[16,128,512]{2,1,0:T(8,128)(2,1)S(1)} %all-to-all-done.mine) | copy-start | bytes 6291460
  49.2 21.1 %all-to-all-start.2 = ((bf16[16,12,576]{2,1,0:T(8,128)(2,1)}), bf16[16,12,576]{2,1,0:T(8,128)(2,1)S(1)}, u32[]{:S(2)}, u32[]{:S(2)}) async-start(bf16[16,12,576]{2,1,0:T(8,128)(2,1)} %bitcast.6), calls=%async_computation.2 | async-start | bytes 655360 | tf_op jit(solution)/shard_map/exchange_rest/all_to_all | solution.py:335
  73.5 21.0 %all-to-all-start.3 = ((bf16[16,24,576]{2,1,0:T(8,128)(2,1)}), bf16[16,24,576]{2,1,0:T(8,128)(2,1)S(1)}, u32[]{:S(2)}, u32[]{:S(2)}) async-start(bf16[16,24,576]{2,1,0:T(8,128)(2,1)} %bitcast.33), calls=%async_computation.3 | async-start | bytes 983040 | tf_op jit(solution)/shard_map/exchange_rest/all_to_all | solution.py:340
  80.7 67.1 %all-gather.9.cloned.1.call-start = ((), (), s32[]{:S(2)}) async-start(), calls=%async_computation.7 | async-start | bytes 3481600 | tf_op jit(solution)/shard_map/exchange_rest/all_gather | solution.py:352
  80.8 0.5 copy-start.10
  95.4 102.2 %all-gather.11.cloned.1.call-start = ((), (), s32[]{:S(2)}) async-start(), calls=%async_computation.8 | async-start | bytes 3342336 | tf_op jit(solution)/shard_map/shrink/all_gather | solution.py:369
  99.7 20.9 %copy-start.1 = (s32[2,128]{1,0:T(2,128)S(1)}, s32[2,128]{1,0:T(2,128)}, u32[]{:S(2)}) copy-start(s32[2,128]{1,0:T(2,128)} %fusion.1) | copy-start | bytes 3076
  105.4 15.1 %all-to-all-start.1 = ((bf16[16,48,256]{2,1,0:T(8,128)(2,1)}), bf16[16,48,256]{2,1,0:T(8,128)(2,1)S(1)}, u32[]{:S(2)}, u32[]{:S(2)}) async-start(bf16[16,48,256]{2,1,0:T(8,128)(2,1)} %broadcast_in_dim.57), calls=%async_computation.1 | async-start | bytes 786432 | tf_op jit(solution)/shard_map/shrink/all_to_all | solution.py:371
  121.7 26.1 %all-to-all-start.4 = ((bf16[16,16,320]{2,1,0:T(8,128)(2,1)}), bf16[16,16,320]{2,1,0:T(8,128)(2,1)S(1)}, u32[]{:S(2)}, u32[]{:S(2)}) async-start(bf16[16,16,320]{2,1,0:T(8,128)(2,1)} %project.1), calls=%async_computation.4 | async-start | bytes 393216 | tf_op jit(solution)/shard_map/project/all_to_all | solution.py:383
  126.0 39.8 %collective-permute-start = (bf16[16,128,512]{2,1,0:T(8,128)(2,1)}, bf16[16,128,512]{2,1,0:T(8,128)(2,1)}, u32[]{:S(2)}, u32[]{:S(2)}) collective-permute-start(bf16[16,128,512]{2,1,0:T(8,128)(2,1)} %copy-done.3), channel_id=1, source_target_pairs={{0,16},{16,0},{32,48},{48,32},{64,80},{80,64},{96,112},{112,96},{1... | collective-permute-start | bytes 6291464 | tf_op jit(solution)/shard_map/columns_of_w_out/ppermute | solution.py:315
  147.8 0.7 copy-start.4
  160.7 36.9 %all-to-all-start.5 = ((bf16[16,17,16,256]{3,2,1,0:T(8,128)(2,1)}), bf16[16,17,16,256]{3,2,1,0:T(8,128)(2,1)S(1)}, u32[]{:S(2)}, u32[]{:S(2)}) async-start(bf16[16,17,16,256]{3,2,1,0:T(8,128)(2,1)} %attend.1), calls=%async_computation.5 | async-start | bytes 4456448 | tf_op jit(solution)/shard_map/attend/all_to_all | solution.py:404
  197.6 1.4 copy-start.2
Sparse Core Ops, SparseCore 0:
  9.2 68.6 all-gather.6
  95.5 52.2 all-gather.8
  149.6 39.5 all-gather.10

commit v4 on v3

v4 whole, which is shorter than its diff:
```python
import math

import jax
import jax.numpy as jnp
from jax import lax
from jax.experimental import pallas as pl
from jax.experimental.pallas import tpu as pltpu
from jax.sharding import PartitionSpec as P

QH = 32
KH = 4
HD = 128
STEPS = 2
ROWS = 128
RANK = 16
LOADS = 12
SLOTS = 13
HELD = 12
N = 16
SIDE = 4
RING = 8
PAIR = 2
ALL_ROWS = STEPS * ROWS
LOCAL = ROWS // N
MINE = STEPS * LOCAL
ENTRIES = 1 + STEPS * LOADS
IN_RANK = 3 * RANK
PER_DOT = 5
QF = 256
KF = 32
IN_PART = 512
OUT_PART = 512
FEATURES = QH * HD
WIDE = RING * QF
QKV = QF + 2 * KF
TP = ("hi", "lo", "x")
AROUND = ("hi", "x")
LENGTH = 512
KW = KH * HD
BF16 = jnp.bfloat16
F32 = jnp.float32
low_rank_scale = 0.5


def vmem():
    return pl.BlockSpec(memory_space=pltpu.VMEM)


def hbm():
    return pl.BlockSpec(memory_space=pl.ANY)


def smem():
    return pl.BlockSpec(memory_space=pltpu.SMEM)


def params(mib=40):
    return pltpu.CompilerParams(vmem_limit_bytes=mib * 1024 * 1024)


def cost(flops, nbytes):
    return pl.CostEstimate(flops=flops, bytes_accessed=nbytes, transcendentals=0)


def iota(shape, axis):
    return lax.broadcasted_iota(jnp.int32, shape, axis)


def shrink_kernel(index, pool, slot, tokens, entry, out, maps, arrived):
    copies = []
    for i in range(ENTRIES):
        origin = slot.at[index[0]] if i == 0 else pool.at[index[i]]
        copy = pltpu.make_async_copy(origin, maps.at[pl.ds(i * IN_RANK, IN_RANK)], arrived.at[i])
        copy.start()
        copies.append(copy)
    used = entry[...]
    total = jnp.zeros((IN_RANK, ALL_ROWS), F32)
    for first in range(0, ENTRIES, PER_DOT):
        for i in range(first, first + PER_DOT):
            copies[i].wait()
        block = maps[pl.ds(first * IN_RANK, PER_DOT * IN_RANK), :]
        product = lax.dot_general(
            block, tokens[...], (((1,), (1,)), ((), ())), preferred_element_type=F32
        )
        for k in range(PER_DOT):
            piece = product[k * IN_RANK : (k + 1) * IN_RANK]
            total = total + jnp.where(used == first + k, piece, 0.0)
    total = total.astype(BF16)
    for n in range(N):
        out[n] = total


def expand(shrunk, entry):
    blocks = [jnp.where(entry == i, shrunk, 0.0) for i in range(ENTRIES)]
    return jnp.concatenate(blocks, axis=0).astype(BF16)


def expand_by_rank(shrunk, entry):
    loads = STEPS * LOADS
    chosen = iota((loads, ALL_ROWS), 0) + 1 == entry
    blocks = [jnp.where(chosen, shrunk[r : r + 1, :], 0.0) for r in range(RANK)]
    kept = jnp.where(entry == 0, shrunk, 0.0)
    return jnp.concatenate(blocks + [kept], axis=0).astype(BF16)


def contract(left, right):
    return lax.dot_general(left, right, (((0,), (0,)), ((), ())), preferred_element_type=F32)


def project_kernel(parts, entry, base_q, base_kv, up, out):
    shrunk = jnp.sum(parts[...].astype(F32), axis=0).astype(BF16).astype(F32)
    used = entry[...]
    up_q, up_kv = up[:, :QF], up[:, QF:]
    wide_q = expand_by_rank(shrunk[:RANK], used)
    wide_k = expand_by_rank(shrunk[RANK : 2 * RANK], used)
    wide_v = expand_by_rank(shrunk[2 * RANK :], used)
    query = base_q[...] + low_rank_scale * contract(wide_q, up_q)
    delta_k = contract(wide_k, up_kv)
    delta_v = contract(wide_v, up_kv)
    column = iota(delta_k.shape, 1)
    delta = jnp.where(column < KF, delta_k, delta_v)
    fresh = base_kv[...] + low_rank_scale * delta
    for t in range(N):
        lows = [s * ROWS + t * LOCAL for s in range(STEPS)]
        out[t, :, :QF] = jnp.concatenate([query[n : n + LOCAL] for n in lows], 0).astype(BF16)
        out[t, :, QF:] = jnp.concatenate([fresh[n : n + LOCAL] for n in lows], 0).astype(BF16)


def split_kernel(place, weight, *rest):
    outs, arrived = rest[:RING], rest[RING]
    copies = []
    for k in range(RING):
        other = lax.rem(place[0] + k, RING)
        for n in range(PAIR):
            block = (other // SIDE * PAIR + n) * SIDE + lax.rem(other, SIDE)
            column = pl.multiple_of(block * OUT_PART, OUT_PART)
            source = weight.at[:, pl.ds(column, OUT_PART)]
            copies.append(pltpu.make_async_copy(source, outs[k].at[n], arrived.at[k, n]))
    for copy in copies:
        copy.start()
    for copy in copies:
        copy.wait()


def transposing():
    shape = (N * MINE, N * MINE)
    row, column = iota(shape, 0), iota(shape, 1)
    return ((row // N == column % N) & (row % N == column // N)).astype(BF16)


def attend_kernel(
    lengths, received, keys, values, out, key_rows, value_rows, by_row, ready, key_sem, value_sem,
    sent,
):
    loads = []
    for i in range(LOCAL):
        pair = (
            pltpu.make_async_copy(keys.at[i], key_rows.at[i], key_sem.at[i]),
            pltpu.make_async_copy(values.at[i], value_rows.at[i], value_sem.at[i]),
        )
        for copy in pair:
            copy.start()
        loads.append(pair)
    swap = transposing()
    mine = jnp.dot(swap, received[...].reshape(N * MINE, -1), preferred_element_type=F32)
    mine = mine.astype(BF16)
    shape = (2 * KF, KW)
    feature, column = iota(shape, 0), iota(shape, 1) % KF
    block = iota((N * MINE, KW), 1) // KF == iota((N * MINE, KW), 0) % N
    fold = (iota((MINE, N * MINE), 1) // N == iota((MINE, N * MINE), 0)).astype(BF16)

    def fresh(first):
        repeat = (feature - first == column).astype(BF16)
        wide = jnp.dot(mine[:, QF:], repeat, preferred_element_type=F32)
        wide = jnp.where(block, wide, 0.0).astype(BF16)
        return jnp.dot(fold, wide, preferred_element_type=F32).astype(BF16)

    keys_new, values_new = fresh(0), fresh(KF)

    head_rows = STEPS * QH
    own = iota((head_rows, KW), 0) % N // (N // KH) == iota((head_rows, KW), 1) // HD
    place = iota((head_rows, LENGTH), 1)
    shape = (head_rows, MINE)
    new_step, new_row = iota(shape, 1) // LOCAL, iota(shape, 1) % LOCAL
    in_time = new_step <= iota(shape, 0) // QH
    scale = 1.0 / math.sqrt(HD)
    dims = (((1,), (1,)), ((), ()))
    for i in range(LOCAL):
        asked = []
        for s in range(STEPS):
            low = (s * LOCAL + i) * N
            asked += [mine[low : low + N, :HD], mine[low : low + N, HD:QF]]
        asked = jnp.concatenate(asked, axis=0)
        spread = jnp.where(own, jnp.concatenate([asked] * KH, axis=1), jnp.zeros((), BF16))
        new = lax.dot_general(spread, keys_new, dims, preferred_element_type=F32) * scale
        new = jnp.where(in_time & (new_row == i), new, -jnp.inf)
        loads[i][0].wait()
        old = lax.dot_general(spread, key_rows[i], dims, preferred_element_type=F32) * scale
        old = jnp.where(place < lengths[i], old, -jnp.inf)
        highest = jnp.maximum(
            jnp.max(old, axis=1, keepdims=True), jnp.max(new, axis=1, keepdims=True)
        )
        old, new = jnp.exp(old - highest), jnp.exp(new - highest)
        totals = jnp.sum(old, axis=1, keepdims=True) + jnp.sum(new, axis=1, keepdims=True)
        loads[i][1].wait()
        mixed = jnp.dot(old.astype(BF16), value_rows[i], preferred_element_type=F32)
        mixed = mixed + jnp.dot(new.astype(BF16), values_new, preferred_element_type=F32)
        mixed = jnp.where(own, mixed, 0.0)
        attended = mixed[:, :HD]
        for k in range(1, KH):
            attended = attended + mixed[:, k * HD : (k + 1) * HD]
        attended = (attended / totals).astype(BF16)
        for s in range(STEPS):
            low = (s * LOCAL + i) * N
            for half in range(2):
                piece = attended[(2 * s + half) * N : (2 * s + half + 1) * N]
                by_row[low : low + N, half * HD : (half + 1) * HD] = piece

    attended = jnp.dot(swap, by_row[...], preferred_element_type=F32).astype(BF16)
    for t in range(N):
        high, low, x = t // (PAIR * SIDE), t // SIDE % PAIR, t % SIDE
        ready[low, high * SIDE + x] = attended[t * MINE : (t + 1) * MINE]
    copies = [
        pltpu.make_async_copy(ready.at[n // SIDE % PAIR], out.at[n], sent.at[n]) for n in range(N)
    ]
    for copy in copies:
        copy.start()
    for copy in copies:
        copy.wait()


def pick_kernel(index, slot_in, slot_up, pool, maps, up, map_sem, up_sem):
    copies = []
    for i in range(ENTRIES):
        if i == 0:
            first, second = slot_in.at[index[0]], slot_up.at[index[0]]
        else:
            first = pool.at[index[i], :, pl.ds(0, QF)]
            second = pool.at[index[i], :, pl.ds(QF, OUT_PART)]
        rows = pl.ds(i * RANK, RANK)
        copies.append(pltpu.make_async_copy(first, maps.at[rows], map_sem.at[i]))
        copies.append(pltpu.make_async_copy(second, up.at[rows], up_sem.at[i]))
    for copy in copies:
        copy.start()
    for copy in copies:
        copy.wait()


def shrink_out_kernel(place, attended, entry, maps, out):
    heads = attended[:, pl.ds(place[0], 1)].reshape(ALL_ROWS, QF)
    product = lax.dot_general(
        maps[...], heads, (((1,), (1,)), ((), ())), preferred_element_type=F32
    )
    used = entry[...]
    shrunk = jnp.zeros((RANK, ALL_ROWS), F32)
    for i in range(ENTRIES):
        shrunk = shrunk + jnp.where(used == i, product[i * RANK : (i + 1) * RANK], 0.0)
    shrunk = shrunk.astype(BF16)
    for n in range(N):
        out[n] = shrunk


def base_out_kernel(place, member, attended, *rest):
    sources = rest[:RING]
    out, columns, column_sem = rest[RING:]
    copies = []
    for k in range(RING):
        copy = pltpu.make_async_copy(
            sources[k].at[member[0]], columns.at[pl.ds(k * QF, QF)], column_sem.at[k]
        )
        copy.start()
        copies.append(copy)
    heads = []
    for k in range(RING):
        block = lax.rem(place[0] + RING - k, RING)
        heads.append(attended[:, pl.ds(block, 1)].reshape(ALL_ROWS, QF))
    total = jnp.zeros((ALL_ROWS, OUT_PART), F32)
    for k in range(0, RING, PAIR):
        for copy in copies[k : k + PAIR]:
            copy.wait()
        part = jnp.concatenate(heads[k : k + PAIR], axis=1)
        rows = columns[k * QF : (k + PAIR) * QF]
        total = total + jnp.dot(part, rows, preferred_element_type=F32)
    out[...] = total.astype(out.dtype)


def final_kernel(parts, entry, kept, arrived, up, out):
    shrunk = jnp.sum(parts[...].astype(F32), axis=0).astype(BF16).astype(F32)
    wide = expand(shrunk, entry[...])
    total = kept[...] + arrived[...].astype(F32)
    total = total + low_rank_scale * contract(wide, up[...])
    for s in range(STEPS):
        lows = [t * MINE + s * LOCAL for t in range(N)]
        out[s] = jnp.concatenate([total[n : n + LOCAL] for n in lows], axis=0).astype(BF16)


def shard(
    hidden, w_query, w_key, w_value, w_out, key_cache, value_cache, lengths, row_slot, evict_slot,
    evict_adapter, owner, pool_a_in, pool_b_q, pool_b_k, pool_b_v, pool_a_o, pool_b_o,
    slot_a_in, slot_b_q, slot_b_k, slot_b_v, slot_a_o, slot_b_o,
):
    me = lax.axis_index("group")
    part = lax.axis_index(TP)
    place = lax.axis_index(AROUND)[None]
    member = lax.axis_index("lo")[None]

    with jax.named_scope("gather_in_maps"):
        whole_in = lax.all_gather(pool_a_in, "group").reshape(N * HELD, IN_RANK, IN_PART)

    with jax.named_scope("positions"):
        position = jnp.sum(
            jnp.where(evict_adapter[..., None] == jnp.arange(N * HELD), owner, 0), axis=-1
        )
        position = position.reshape(STEPS, N, LOADS)
        wanted = position.transpose(1, 0, 2).reshape(N, STEPS * LOADS)
        targets = lax.dynamic_slice_in_dim(evict_slot, me * LOADS, LOADS, 1)
        survivor = SLOTS * (SLOTS - 1) // 2 - jnp.sum(targets[0])
        placed = targets[:, :, None] == jnp.arange(SLOTS)
        order = 1 + jnp.arange(STEPS * LOADS).reshape(STEPS, LOADS, 1)
        slot_entry = jnp.sum(jnp.where(placed, order, 0), axis=1)
        second = jnp.where(slot_entry[1] > 0, slot_entry[1], slot_entry[0])
        slot_entry = jnp.stack([slot_entry[0], second])
        entry = jnp.sum(
            jnp.where(
                row_slot[:, :, None] == jnp.arange(SLOTS), slot_entry[:, None, :], 0
            ),
            axis=-1,
        )
        by_step = entry.reshape(1, ALL_ROWS)
        by_owner = entry.reshape(STEPS, N, LOCAL).transpose(1, 0, 2)
        by_owner = by_owner.reshape(1, ALL_ROWS)
        my_wanted = lax.dynamic_index_in_dim(position, me, 1, keepdims=False)
        my_wanted = my_wanted.reshape(STEPS * LOADS)
        index = jnp.concatenate([survivor[None], my_wanted]).astype(jnp.int32)

    turns = [[(i, (i + k) % RING) for i in range(RING)] for k in range(1, RING)]
    with jax.named_scope("columns_of_w_out"):
        block = jax.ShapeDtypeStruct((PAIR, QF, OUT_PART), BF16)
        columns = pl.pallas_call(
            split_kernel,
            out_shape=[block] * RING,
            in_specs=[smem(), hbm()],
            out_specs=[vmem()] * RING,
            scratch_shapes=[pltpu.SemaphoreType.DMA((RING, PAIR))],
            compiler_params=params(56),
            cost_estimate=cost(0, 8 << 20),
            name="split",
        )(place, w_out)

    with jax.named_scope("base_projections"):
        tokens = hidden.reshape(ALL_ROWS, -1)
        base_q = jnp.dot(tokens, w_query, preferred_element_type=F32)
        base_kv = jnp.concatenate(
            [
                jnp.dot(tokens, w_key, preferred_element_type=F32),
                jnp.dot(tokens, w_value, preferred_element_type=F32),
            ],
            axis=1,
        )
        tokens_part = lax.dynamic_slice_in_dim(tokens, part * IN_PART, IN_PART, 1)

    with jax.named_scope("exchange_up_maps"):
        rest = jnp.concatenate([pool_b_q, pool_b_k, pool_b_v], axis=2)
        rest, *columns = lax.optimization_barrier((rest, *columns))
        by_rank = lax.all_to_all(
            rest.transpose(1, 0, 2), "group", split_axis=0, concat_axis=0, tiled=True
        ).reshape(N * HELD, QKV)
        pick = (wanted.reshape(-1, 1) == jnp.arange(N * HELD)).astype(BF16)
        sent = jnp.dot(pick, by_rank, preferred_element_type=F32).astype(BF16)
        loaded = lax.all_to_all(
            sent.reshape(N, STEPS * LOADS, QKV), "group", split_axis=0, concat_axis=0, tiled=True
        ).reshape(RANK * STEPS * LOADS, QKV)
        columns = columns[:1] + [
            lax.ppermute(c, AROUND, turn) for c, turn in zip(columns[1:], turns)
        ]
        survived = lambda piece: lax.dynamic_index_in_dim(piece, survivor, 0, keepdims=False)
        kept = jnp.concatenate([survived(p) for p in (slot_b_q, slot_b_k, slot_b_v)], axis=1)
        up = jnp.concatenate([loaded, kept], axis=0)

    with jax.named_scope("gather_out_maps"):
        out_pool = jnp.concatenate([pool_a_o, pool_b_o], axis=2)
        out_pool, index, up, base_q, base_kv, tokens_part, *columns = lax.optimization_barrier(
            (out_pool, index, up, base_q, base_kv, tokens_part, *columns)
        )
        out_pool = lax.all_gather(out_pool, "group").reshape(N * HELD, RANK, QF + OUT_PART)

    with jax.named_scope("shrink"):
        partial_in = pl.pallas_call(
            shrink_kernel,
            out_shape=jax.ShapeDtypeStruct((N, IN_RANK, ALL_ROWS), BF16),
            in_specs=[smem(), hbm(), hbm(), vmem(), vmem()],
            out_specs=vmem(),
            scratch_shapes=[
                pltpu.VMEM((ENTRIES * IN_RANK, IN_PART), BF16),
                pltpu.SemaphoreType.DMA((ENTRIES,)),
            ],
            compiler_params=params(56),
            cost_estimate=cost(2 * ENTRIES * IN_RANK * IN_PART * ALL_ROWS, 2 << 20),
            name="shrink",
        )(index, whole_in, slot_a_in, tokens_part, by_step)
        partials = lax.all_to_all(partial_in, TP, split_axis=0, concat_axis=0, tiled=True)

    with jax.named_scope("project"):
        projected = pl.pallas_call(
            project_kernel,
            out_shape=jax.ShapeDtypeStruct((N, MINE, QF + 2 * KF), BF16),
            in_specs=[vmem()] * 5,
            out_specs=vmem(),
            compiler_params=params(16),
            cost_estimate=cost(2 * 400 * 512 * ALL_ROWS, 1 << 20),
            name="project",
        )(partials, by_step, base_q, base_kv, up)

    with jax.named_scope("attend"):
        received = lax.all_to_all(projected, TP, split_axis=0, concat_axis=0, tiled=True)
        payload = pl.pallas_call(
            attend_kernel,
            out_shape=jax.ShapeDtypeStruct((N, RING, MINE, QF), BF16),
            in_specs=[smem(), vmem(), hbm(), hbm()],
            out_specs=hbm(),
            scratch_shapes=[
                pltpu.VMEM((LOCAL, LENGTH, KW), BF16),
                pltpu.VMEM((LOCAL, LENGTH, KW), BF16),
                pltpu.VMEM((N * MINE, QF), BF16),
                pltpu.VMEM((PAIR, RING, MINE, QF), BF16),
                pltpu.SemaphoreType.DMA((LOCAL,)),
                pltpu.SemaphoreType.DMA((LOCAL,)),
                pltpu.SemaphoreType.DMA((N,)),
            ],
            compiler_params=params(56),
            cost_estimate=cost(4 * LOCAL * 64 * KW * LENGTH, 12 << 20),
            name="attend",
        )(lengths, received, key_cache, value_cache)
        gathered = lax.all_to_all(payload, TP, split_axis=0, concat_axis=0, tiled=True)

        payload, picks = lax.optimization_barrier((payload, index))
        maps, up_o = pl.pallas_call(
            pick_kernel,
            out_shape=[
                jax.ShapeDtypeStruct((ENTRIES * RANK, QF), BF16),
                jax.ShapeDtypeStruct((ENTRIES * RANK, OUT_PART), BF16),
            ],
            in_specs=[smem()] + [hbm()] * 3,
            out_specs=[vmem()] * 2,
            scratch_shapes=[pltpu.SemaphoreType.DMA((ENTRIES,))] * 2,
            compiler_params=params(56),
            cost_estimate=cost(0, 3 << 20),
            name="pick",
        )(picks, slot_a_o, slot_b_o, out_pool)

    with jax.named_scope("output"):
        partial_out = pl.pallas_call(
            shrink_out_kernel,
            out_shape=jax.ShapeDtypeStruct((N, RANK, ALL_ROWS), BF16),
            in_specs=[smem()] + [vmem()] * 3,
            out_specs=vmem(),
            compiler_params=params(16),
            cost_estimate=cost(2 * 400 * QF * ALL_ROWS, 1 << 20),
            name="shrink_out",
        )(place, gathered, by_owner, maps)
        partial_out, member = lax.optimization_barrier((partial_out, member))
        partials_out = lax.all_to_all(partial_out, TP, split_axis=0, concat_axis=0, tiled=True)

        def base_out(whose, dtype):
            return pl.pallas_call(
                base_out_kernel,
                out_shape=jax.ShapeDtypeStruct((ALL_ROWS, OUT_PART), dtype),
                in_specs=[smem()] * 2 + [vmem()] + [hbm()] * RING,
                out_specs=vmem(),
                scratch_shapes=[
                    pltpu.VMEM((RING * QF, OUT_PART), BF16),
                    pltpu.SemaphoreType.DMA((RING,)),
                ],
                compiler_params=params(56),
                cost_estimate=cost(2 * ALL_ROWS * WIDE * OUT_PART, 3 << 20),
                name="base_out",
            )(place, whose, gathered, *columns)

        passed = lax.ppermute(base_out(1 - member, BF16), "lo", [(0, 1), (1, 0)])
        kept_out = base_out(member, F32)
        return pl.pallas_call(
            final_kernel,
            out_shape=jax.ShapeDtypeStruct((STEPS, ROWS, OUT_PART), BF16),
            in_specs=[vmem()] * 5,
            out_specs=vmem(),
            compiler_params=params(16),
            cost_estimate=cost(2 * 400 * OUT_PART * ALL_ROWS, 1 << 20),
            name="final",
        )(partials_out, by_owner, kept_out, passed, up_o)


def solution(mesh):
    grid = jax.sharding.Mesh(mesh.devices.reshape(N, SIDE // PAIR, PAIR, SIDE), ("group",) + TP)
    pooled = P("group", None, TP)
    cached = P(("group",) + TP, None, None)
    placed = (
        P(None, "group", None), P(None, TP), P(None, TP), P(None, TP), P(TP, None),
        cached, cached, P(("group",) + TP), P(None, "group"), P(), P(), P(),
    ) + (pooled,) * 12
    return jax.shard_map(
        shard, mesh=grid, in_specs=placed, out_specs=P(None, "group", TP), check_vma=False
    )
```

time: 213 us -> 177 us (0.83)
  waiting for transfers between devices: 110 us -> 40.1 us
  blocking collectives: 0 us -> 26.9 us
  Pallas kernels: 26.2 us -> 31.9 us
  starting transfers between devices: 34.4 us -> 38.8 us
  local copies, waits for them, and re-layouts: 12.2 us -> 8.83 us
    all_to_all x5 -> x3, waiting for transfers between devices: 75.4 us -> 16.5 us  [the longest x1 11 us: shard(): lax.all_to_all(payload, TP, split_axis=0, concat_axis=0, tiled=True)]
    all_to_all x0 -> x2, blocking collectives: none -> 26.9 us  [the longest x1 15.3 us: shard(): lax.all_to_all(partial_in, TP, split_axis=0, concat_axis=0, tiled=True)]
    ppermute x1 -> x8, waiting for transfers between devices: 0.01 us -> 22.9 us  [the longest x7 22.9 us: shard(): lax.ppermute(c, AROUND, turn)]
    all_gather x2 -> x1, waiting for transfers between devices: 21.8 us -> 0.02 us  [shard(): lax.all_gather(out_pool, 'group').reshape(N * HELD, RANK, QF + OUT_PART)]
    ppermute x1 -> x8, starting transfers between devices: 0.01 us -> 15.2 us  [the longest x7 15.1 us: shard(): lax.ppermute(c, AROUND, turn)]
    all_to_all x1, waiting for transfers between devices: 12 us -> 0.01 us  [shard(): lax.all_to_all(rest.transpose(1, 0, 2), 'group', split_axis=0, concat_axi...]
    all_to_all x5 -> x3, starting transfers between devices: 25.7 us -> 15 us  [the longest x1 7.25 us: shard(): lax.all_to_all(sent.reshape(N, STEPS * LOADS, QKV), 'group', split_axis=0...]
    pallas_call x4 -> x8, Pallas kernels: 25.1 us -> 31.5 us  [the longest x1 9.52 us: shard(): pl.pallas_call(attend_kernel, out_shape=jax.ShapeDtypeStruct((N, RING, MI...]
  transfers between devices with their start and end apart: 10 -> 14, of which waited for: 6 -> 7; matrix products, arithmetic and copies ran while one was open for 11% -> 12% of each run, Pallas kernels for 10% -> 15%
where the time goes in v4:
time: 177 us; the launch traced here: 176 us
  waiting for transfers between devices  40.1 us (23%)
  starting transfers between devices  38.8 us (22%)
  Pallas kernels  31.9 us (18%)
  blocking collectives  26.9 us (15%)
  between operations  15 us (8%)
  matrix products  10.3 us (6%)
  local copies, waits for them, and re-layouts  8.83 us (5%)
  other arithmetic  3.96 us (2%)
    ppermute x7, waiting for transfers between devices, shard(): lax.ppermute(c, AROUND, turn)  22.9 us
    all_to_all x1, blocking collectives, shard(): lax.all_to_all(partial_in, TP, split_axis=0, concat_axis=0, tiled=True)  15.3 us
    ppermute x7, starting transfers between devices, shard(): lax.ppermute(c, AROUND, turn)  15.1 us
    all_to_all x1, blocking collectives, shard(): lax.all_to_all(projected, TP, split_axis=0, concat_axis=0, tiled=True)  11.6 us
    all_to_all x1, waiting for transfers between devices, shard(): lax.all_to_all(payload, TP, split_axis=0, concat_axis=0, tiled=True)  11 us
    pallas_call x1, Pallas kernels, shard(): pl.pallas_call(attend_kernel, out_shape=jax.ShapeDtypeStruct((N, RING, MI...  9.52 us
    all_to_all x1, starting transfers between devices, shard(): lax.all_to_all(rest.transpose(1, 0, 2), 'group', split_axis=0, concat_axi...  8.59 us
    pallas_call x2, Pallas kernels, base_out(): pl.pallas_call(base_out_kernel, out_shape=jax.ShapeDtypeStruct((ALL_ROWS,...  8.13 us
  transfers between devices with their start and end apart: 14, of which 7 were waited for; matrix products, arithmetic and copies ran while one was open for 12% of the time, Pallas kernels for 15%

profile of v4, /device:TPU:32, one launch (start us, length us, event | category | flops | bytes accessed | tf_op | source)
XLA Modules:
  0.0 175.9 jit_solution(831759138241692792)
XLA Ops:
  7.3 0.9 copy.43
  9.9 4.4 %split.1 = (bf16[2,256,512]{2,1,0:T(8,128)(2,1)}, bf16[2,256,512]{2,1,0:T(8,128)(2,1)}, bf16[2,256,512]{2,1,0:T(8,128)(2,1)}, bf16[2,256,512]{2,1,0:T(8,128)(2,1...) custom-call(s32[1]{0:T(128)} %bitcast.place, ...), custom_call_target="tpu_custom_call" | custom-call | bytes 8388608 | tf_op jit(solution)/shard_map/columns_of_w_out/split/pallas_call | solution.py:339
  15.1 8.6 %all-to-all-start = ((bf16[16,12,320]{2,1,0:T(8,128)(2,1)}), bf16[16,12,320]{2,1,0:T(8,128)(2,1)S(1)}, u32[]{:S(2)}, u32[]{:S(2)}) async-start(bf16[16,12,320]{2,1,0:T(8,128)(2,1)} %bitcast.3), calls=%async_computation | async-start | bytes 393216 | tf_op jit(solution)/shard_map/exchange_up_maps/all_to_all | solution.py:365
  23.7 1.5 collective-permute-start
  25.2 2.7 %collective-permute-start.1 = (bf16[2,256,512]{2,1,0:T(8,128)(2,1)}, bf16[2,256,512]{2,1,0:T(8,128)(2,1)S(1)}, u32[]{:S(2)}, u32[]{:S(2)}) collective-permute-start(bf16[2,256,512]{2,1,0:T(8,128)(2,1)} %get-tuple-element.52), channel_id=1, source_target_pairs={{0,2},{1,3},{2,8},{3,9},{8,10},{9,11},{10,0},{11,1},{4,6},{5,7},{6... | collective-permute-start | bytes 1572872 | tf_op jit(solution)/shard_map/exchange_up_maps/ppermute | solution.py:374
  27.9 4.1 %collective-permute-start.2 = (bf16[2,256,512]{2,1,0:T(8,128)(2,1)}, bf16[2,256,512]{2,1,0:T(8,128)(2,1)S(1)}, u32[]{:S(2)}, u32[]{:S(2)}) collective-permute-start(bf16[2,256,512]{2,1,0:T(8,128)(2,1)} %get-tuple-element.53), channel_id=1, source_target_pairs={{0,3},{1,8},{2,9},{3,10},{8,11},{9,0},{10,1},{11,2},{4,7},{5,12},{... | collective-permute-start | bytes 1572872 | tf_op jit(solution)/shard_map/exchange_up_maps/ppermute | solution.py:374
  32.3 3.2 %collective-permute-start.4 = (bf16[2,256,512]{2,1,0:T(8,128)(2,1)}, bf16[2,256,512]{2,1,0:T(8,128)(2,1)}, u32[]{:S(2)}, u32[]{:S(2)}) collective-permute-start(bf16[2,256,512]{2,1,0:T(8,128)(2,1)} %get-tuple-element.55), channel_id=1, source_target_pairs={{0,9},{1,10},{2,11},{3,0},{8,1},{9,2},{10,3},{11,8},{4,13},{5,14},... | collective-permute-start | bytes 1572872 | tf_op jit(solution)/shard_map/exchange_up_maps/ppermute | solution.py:374
  39.0 3.7 %fusion.6 = f32[256,32]{1,0:T(8,128)S(1)} fusion(bf16[256,8192]{1,0:T(8,128)(2,1)} %bitcast.28, bf16[8192,32]{0,1:T(8,128)(2,1)S(1)} %copy-done), kind=kOutput, calls=%fused_computation.27 | convolution fusion | flops 134217728 | bytes 4751360 | tf_op jit(solution)/shard_map/base_projections/dot_general | solution.py:355
  42.8 1.3 fusion.7
  48.3 7.2 %all-to-all-start.1 = ((bf16[16,24,320]{2,1,0:T(8,128)(2,1)}), bf16[16,24,320]{2,1,0:T(8,128)(2,1)S(1)}, u32[]{:S(2)}, u32[]{:S(2)}) async-start(bf16[16,24,320]{2,1,0:T(8,128)(2,1)} %bitcast.4), calls=%async_computation.1 | async-start | bytes 589824 | tf_op jit(solution)/shard_map/exchange_up_maps/all_to_all | solution.py:370
  55.6 3.2 %collective-permute-start.5 = (bf16[2,256,512]{2,1,0:T(8,128)(2,1)}, bf16[2,256,512]{2,1,0:T(8,128)(2,1)}, u32[]{:S(2)}, u32[]{:S(2)}) collective-permute-start(bf16[2,256,512]{2,1,0:T(8,128)(2,1)} %get-tuple-element.56), channel_id=1, source_target_pairs={{0,10},{1,11},{2,0},{3,1},{8,2},{9,3},{10,8},{11,9},{4,14},{5,15},... | collective-permute-start | bytes 1572872 | tf_op jit(solution)/shard_map/exchange_up_maps/ppermute | solution.py:374
  58.8 2.0 %collective-permute-done.1.rest_2_ = bf16[2,256,512]{2,1,0:T(8,128)(2,1)S(1)} collective-permute-done((bf16[2,256,512]{2,1,0:T(8,128)(2,1)}, bf16[2,256,512]{2,1,0:T(8,128)(2,1)S(1)}, u32[]{:S(2)}, u32[]{:S(2)}) %collective-permute-start.1) | collective-permute-done | bytes 524320 | tf_op jit(solution)/shard_map/exchange_up_maps/ppermute | solution.py:374
  60.8 5.0 %fusion.5.base_q = f32[256,256]{1,0:T(8,128)S(1)} fusion(bf16[256,8192]{1,0:T(8,128)(2,1)} %bitcast.29, bf16[8192,256]{1,0:T(8,128)(2,1)} %param.25), kind=kOutput, calls=%fused_computation.26 | convolution fusion | flops 1073741824 | bytes 8650752 | tf_op jit(solution)/shard_map/base_projections/dot_general | solution.py:352
  65.8 1.6 all-to-all-done.1
  67.5 7.8 %collective-permute-done.3.rest_4_ = bf16[2,256,512]{2,1,0:T(8,128)(2,1)} collective-permute-done((bf16[2,256,512]{2,1,0:T(8,128)(2,1)}, bf16[2,256,512]{2,1,0:T(8,128)(2,1)}, u32[]{:S(2)}, u32[]{:S(2)}) %collective-permute-start.3) | collective-permute-done | bytes 524320 | tf_op jit(solution)/shard_map/exchange_up_maps/ppermute | solution.py:374
  75.3 5.4 %collective-permute-done.4.rest_5_ = bf16[2,256,512]{2,1,0:T(8,128)(2,1)} collective-permute-done((bf16[2,256,512]{2,1,0:T(8,128)(2,1)}, bf16[2,256,512]{2,1,0:T(8,128)(2,1)}, u32[]{:S(2)}, u32[]{:S(2)}) %collective-permute-start.4) | collective-permute-done | bytes 524320 | tf_op jit(solution)/shard_map/exchange_up_maps/ppermute | solution.py:374
  80.7 7.7 %collective-permute-done.6.rest_7_ = bf16[2,256,512]{2,1,0:T(8,128)(2,1)} collective-permute-done((bf16[2,256,512]{2,1,0:T(8,128)(2,1)}, bf16[2,256,512]{2,1,0:T(8,128)(2,1)}, u32[]{:S(2)}, u32[]{:S(2)}) %collective-permute-start.6) | collective-permute-done | bytes 524320 | tf_op jit(solution)/shard_map/exchange_up_maps/ppermute | solution.py:374
  89.4 4.4 %shrink.1 = bf16[16,48,256]{2,1,0:T(8,128)(2,1)} custom-call(s32[25]{0:T(128)} %pad_add_fusion.1.index, bf16[192,48,512]{2,1,0:T(8,128)(2,1)} %all-gather.5.cloned.1.call-done.pool, bf16[13,48,512]{2,1,0:T(8,128)(2,1)} %slot.1, bf16[256,512]{1,0:T(8,128)(2,1)} %constant_dynamic-slice_fusion.tokens, s32[1,256]{1,0:T(1,128)} %bitcast.23), custom_call_target="tpu_custom_call" | custom-call | flops 314572800 | bytes 2097152 | tf_op jit(solution)/shard_map/shrink/shrink/pallas_call | solution.py:388
  93.9 15.3 %all_to_all.30.parts = bf16[16,48,256]{2,1,0:T(8,128)(2,1)S(1)} all-to-all(bf16[16,48,256]{2,1,0:T(8,128)(2,1)} %shrink.1), channel_id=1, replica_groups=mesh['group'=16,'hi'=2,'lo'=2,'x'=4] {'hi','lo','x'}, dimensions={0} | all-to-all | bytes 786432 | tf_op jit(solution)/shard_map/shrink/all_to_all | solution.py:401
  109.6 11.6 %all_to_all.31.received = bf16[16,16,320]{2,1,0:T(8,128)(2,1)} all-to-all(bf16[16,16,320]{2,1,0:T(8,128)(2,1)S(1)} %project.1), channel_id=1, replica_groups=mesh['group'=16,'hi'=2,'lo'=2,'x'=4] {'hi','lo','x'}, dimensions={0} | all-to-all | bytes 327680 | tf_op jit(solution)/shard_map/attend/all_to_all | solution.py:415
  121.2 9.5 %attend.1 = bf16[16,8,16,256]{3,2,1,0:T(8,128)(2,1)} custom-call(s32[8]{0:T(128)} %lengths.1, bf16[16,16,320]{2,1,0:T(8,128)(2,1)} %all_to_all.31.received, bf16[8,512,512]{2,1,0:T(8,128)(2,1)} %keys.1, bf16[8,512,512]{2,1,0:T(8,128)(2,1)} %values.1), custom_call_target="tpu_custom_call" | custom-call | flops 536870912 | bytes 12582912 | tf_op jit(solution)/shard_map/attend/attend/pallas_call | solution.py:416
  130.8 3.7 %all-to-all-start.4 = ((bf16[16,8,16,256]{3,2,1,0:T(8,128)(2,1)}), bf16[16,8,16,256]{3,2,1,0:T(8,128)(2,1)S(1)}, u32[]{:S(2)}, u32[]{:S(2)}) async-start(bf16[16,8,16,256]{3,2,1,0:T(8,128)(2,1)} %attend.1), calls=%async_computation.4 | async-start | bytes 2097152 | tf_op jit(solution)/shard_map/attend/all_to_all | solution.py:434
  134.7 3.0 %pick.1 = (bf16[400,256]{1,0:T(8,128)(2,1)}, bf16[400,512]{1,0:T(8,128)(2,1)}) custom-call(s32[25]{0:T(128)} %pad_add_fusion.1.index, bf16[13,16,256]{2,1,0:T(8,128)(2,1)} %slot_in.1, bf16[13,16,512]{2,1,0:T(8,128)(2,1)} %slot_up.1, bf16[192,16,768]{2,1,0:T(8,128)(2,1)} %all-gather.7.cloned.1.call-done.pool), custom_call_target="tpu_custom_call" | custom-call | bytes 3145728 | tf_op jit(solution)/shard_map/attend/pick/pallas_call | solution.py:437
  137.7 11.0 %all-to-all-done.4.attended = bf16[16,8,16,256]{3,2,1,0:T(8,128)(2,1)S(1)} async-done(((bf16[16,8,16,256]{3,2,1,0:T(8,128)(2,1)}), bf16[16,8,16,256]{3,2,1,0:T(8,128)(2,1)S(1)}, u32[]{:S(2)}, u32[]{:S(2)}) %all-to-all-start.4) | async-done | bytes 1048608 | tf_op jit(solution)/shard_map/attend/all_to_all | solution.py:434
  148.7 1.1 copy-done.4
  149.8 0.9 shrink_out.1
  150.7 4.0 %base_out.3 = bf16[256,512]{1,0:T(8,128)(2,1)} custom-call(s32[1]{0:T(128)} %bitcast.place, s32[1]{0:T(128)S(6)} %sub.7.member, bf16[16,8,16,256]{3,2,1,0:T(8,128)(2,1)} %copy-done.1, bf16[2,256,512]{2,1,0:T(8,128)(2,1)} %get-tuple-element.68.rest_0_, bf16[2,256,512]{2,1,0:T(8,128)(2,1)} %copy-done.6, bf16[2,256,512]{2,1,0:T(8,128)(2,1)} %copy-done.7, ...), custom_call_target="tpu_custom_call" | custom-call | flops 536870912 | bytes 3145728 | tf_op jit(solution)/shard_map/output/base_out/pallas_call | solution.py:465
  154.9 4.1 %all-to-all-start.5 = ((bf16[16,16,256]{2,1,0:T(8,128)(2,1)}), bf16[16,16,256]{2,1,0:T(8,128)(2,1)S(1)}, u32[]{:S(2)}, u32[]{:S(2)}) async-start(bf16[16,16,256]{2,1,0:T(8,128)(2,1)} %shrink_out.1), calls=%async_computation.5 | async-start | bytes 262144 | tf_op jit(solution)/shard_map/output/all_to_all | solution.py:462
  159.0 4.1 %base_out.2.kept = f32[256,512]{1,0:T(8,128)} custom-call(s32[1]{0:T(128)} %bitcast.place, s32[1]{0:T(128)} %bitcast.12.member, bf16[16,8,16,256]{3,2,1,0:T(8,128)(2,1)} %copy-done.1, bf16[2,256,512]{2,1,0:T(8,128)(2,1)} %get-tuple-element.68.rest_0_, bf16[2,256,512]{2,1,0:T(8,128)(2,1)} %copy-done.6, bf16[2,256,512]{2,1,0:T(8,128)(2,1)} %copy-done.7, ...), custom_call_target="tpu_custom_call" | custom-call | flops 536870912 | bytes 3145728 | tf_op jit(solution)/shard_map/output/base_out/pallas_call | solution.py:465
  163.1 3.9 %all-to-all-done.5.parts = bf16[16,16,256]{2,1,0:T(8,128)(2,1)S(1)} async-done(((bf16[16,16,256]{2,1,0:T(8,128)(2,1)}), bf16[16,16,256]{2,1,0:T(8,128)(2,1)S(1)}, u32[]{:S(2)}, u32[]{:S(2)}) %all-to-all-start.5) | async-done | bytes 131104 | tf_op jit(solution)/shard_map/output/all_to_all | solution.py:462
  167.0 1.0 copy-done.2
  168.0 1.0 final.1
  (78 shorter events, 11.7 us)
Async XLA Ops:
  6.5 32.5 %copy-start = (bf16[8192,32]{0,1:T(8,128)(2,1)S(1)}, bf16[8192,32]{0,1:T(8,128)(2,1)}, u32[]{:S(2)}) copy-start(bf16[8192,32]{0,1:T(8,128)(2,1)} %param.26) | copy-start | bytes 1572868
  6.5 29.0 %copy-start.12 = (s32[2,192]{1,0:T(2,128)S(1)}, s32[2,192]{1,0:T(2,128)}, u32[]{:S(2)}) copy-start(s32[2,192]{1,0:T(2,128)} %param.34) | copy-start | bytes 4612
  6.5 29.0 %copy-start.13 = (s32[192]{0:T(256)S(1)}, s32[192]{0:T(256)}, u32[]{:S(2)}) copy-start(s32[192]{0:T(256)} %param.35) | copy-start | bytes 2308
  6.5 29.5 %copy-start.15 = (s32[2,192]{1,0:T(2,128)S(1)}, s32[2,192]{1,0:T(2,128)}, u32[]{:S(2)}) copy-start(s32[2,192]{1,0:T(2,128)} %param.33) | copy-start | bytes 4612
  6.5 82.9 %all-gather.5.cloned.1.call-start = ((), (), s32[]{:S(2)}) async-start(), calls=%async_computation.6 | async-start | bytes 10027008 | tf_op jit(solution)/shard_map/gather_in_maps/all_gather | solution.py:308
  9.9 32.9 %copy-start.16 = (bf16[8192,32]{0,1:T(8,128)(2,1)S(1)}, bf16[8192,32]{0,1:T(8,128)(2,1)}, u32[]{:S(2)}) copy-start(bf16[8192,32]{0,1:T(8,128)(2,1)} %param.27) | copy-start | bytes 1572868
  15.1 31.8 %all-to-all-start = ((bf16[16,12,320]{2,1,0:T(8,128)(2,1)}), bf16[16,12,320]{2,1,0:T(8,128)(2,1)S(1)}, u32[]{:S(2)}, u32[]{:S(2)}) async-start(bf16[16,12,320]{2,1,0:T(8,128)(2,1)} %bitcast.3), calls=%async_computation | async-start | bytes 393216 | tf_op jit(solution)/shard_map/exchange_up_maps/all_to_all | solution.py:365
  23.7 31.9 %collective-permute-start = (bf16[2,256,512]{2,1,0:T(8,128)(2,1)}, bf16[2,256,512]{2,1,0:T(8,128)(2,1)S(1)}, u32[]{:S(2)}, u32[]{:S(2)}) collective-permute-start(bf16[2,256,512]{2,1,0:T(8,128)(2,1)} %get-tuple-element.51), channel_id=1, source_target_pairs={{0,1},{1,2},{2,3},{3,8},{8,9},{9,10},{10,11},{11,0},{4,5},{5,6},{6... | collective-permute-start | bytes 1572872 | tf_op jit(solution)/shard_map/exchange_up_maps/ppermute | solution.py:374
  25.2 35.6 %collective-permute-start.1 = (bf16[2,256,512]{2,1,0:T(8,128)(2,1)}, bf16[2,256,512]{2,1,0:T(8,128)(2,1)S(1)}, u32[]{:S(2)}, u32[]{:S(2)}) collective-permute-start(bf16[2,256,512]{2,1,0:T(8,128)(2,1)} %get-tuple-element.52), channel_id=1, source_target_pairs={{0,2},{1,3},{2,8},{3,9},{8,10},{9,11},{10,0},{11,1},{4,6},{5,7},{6... | collective-permute-start | bytes 1572872 | tf_op jit(solution)/shard_map/exchange_up_maps/ppermute | solution.py:374
  27.9 39.6 %collective-permute-start.2 = (bf16[2,256,512]{2,1,0:T(8,128)(2,1)}, bf16[2,256,512]{2,1,0:T(8,128)(2,1)S(1)}, u32[]{:S(2)}, u32[]{:S(2)}) collective-permute-start(bf16[2,256,512]{2,1,0:T(8,128)(2,1)} %get-tuple-element.53), channel_id=1, source_target_pairs={{0,3},{1,8},{2,9},{3,10},{8,11},{9,0},{10,1},{11,2},{4,7},{5,12},{... | collective-permute-start | bytes 1572872 | tf_op jit(solution)/shard_map/exchange_up_maps/ppermute | solution.py:374
  32.0 43.4 %collective-permute-start.3 = (bf16[2,256,512]{2,1,0:T(8,128)(2,1)}, bf16[2,256,512]{2,1,0:T(8,128)(2,1)}, u32[]{:S(2)}, u32[]{:S(2)}) collective-permute-start(bf16[2,256,512]{2,1,0:T(8,128)(2,1)} %get-tuple-element.54), channel_id=1, source_target_pairs={{0,8},{1,9},{2,10},{3,11},{8,0},{9,1},{10,2},{11,3},{4,12},{5,13},... | collective-permute-start | bytes 1572872 | tf_op jit(solution)/shard_map/exchange_up_maps/ppermute | solution.py:374
  32.3 48.4 %collective-permute-start.4 = (bf16[2,256,512]{2,1,0:T(8,128)(2,1)}, bf16[2,256,512]{2,1,0:T(8,128)(2,1)}, u32[]{:S(2)}, u32[]{:S(2)}) collective-permute-start(bf16[2,256,512]{2,1,0:T(8,128)(2,1)} %get-tuple-element.55), channel_id=1, source_target_pairs={{0,9},{1,10},{2,11},{3,0},{8,1},{9,2},{10,3},{11,8},{4,13},{5,14},... | collective-permute-start | bytes 1572872 | tf_op jit(solution)/shard_map/exchange_up_maps/ppermute | solution.py:374
  38.1 4.6 %copy-start.11 = (bf16[2,128,8192]{2,1,0:T(8,128)(2,1)S(1)}, bf16[2,128,8192]{2,1,0:T(8,128)(2,1)}, u32[]{:S(2)}) copy-start(bf16[2,128,8192]{2,1,0:T(8,128)(2,1)} %param.24) | copy-start | bytes 12582916
  42.8 3.4 %copy-start.9 = (bf16[12,16,512]{2,1,0:T(8,128)(2,1)S(1)}, bf16[12,16,512]{2,1,0:T(8,128)(2,1)}, u32[]{:S(2)}) copy-start(bf16[12,16,512]{2,1,0:T(8,128)(2,1)} %param.41) | copy-start | bytes 589828
  42.8 3.4 %copy-start.10 = (bf16[12,16,256]{2,1,0:T(8,128)(2,1)S(1)}, bf16[12,16,256]{2,1,0:T(8,128)(2,1)}, u32[]{:S(2)}) copy-start(bf16[12,16,256]{2,1,0:T(8,128)(2,1)} %param.40) | copy-start | bytes 294916
  48.3 19.1 %all-to-all-start.1 = ((bf16[16,24,320]{2,1,0:T(8,128)(2,1)}), bf16[16,24,320]{2,1,0:T(8,128)(2,1)S(1)}, u32[]{:S(2)}, u32[]{:S(2)}) async-start(bf16[16,24,320]{2,1,0:T(8,128)(2,1)} %bitcast.4), calls=%async_computation.1 | async-start | bytes 589824 | tf_op jit(solution)/shard_map/exchange_up_maps/all_to_all | solution.py:370
  55.5 33.2 %copy-start.14 = (s32[2,128]{1,0:T(2,128)S(1)}, s32[2,128]{1,0:T(2,128)}, u32[]{:S(2)}) copy-start(s32[2,128]{1,0:T(2,128)} %param.32) | copy-start | bytes 3076
  55.5 79.1 %all-gather.7.cloned.1.call-start = ((), (), s32[]{:S(2)}) async-start(), calls=%async_computation.7 | async-start | bytes 5013504 | tf_op jit(solution)/shard_map/gather_out_maps/all_gather | solution.py:385
  55.6 10.2 %copy-start.6 = (bf16[2,256,512]{2,1,0:T(8,128)(2,1)}, bf16[2,256,512]{2,1,0:T(8,128)(2,1)S(1)}, u32[]{:S(2)}) copy-start(bf16[2,256,512]{2,1,0:T(8,128)(2,1)S(1)} %collective-permute-done.rest_1_) | copy-start | bytes 1572868
  55.6 25.1 %collective-permute-start.5 = (bf16[2,256,512]{2,1,0:T(8,128)(2,1)}, bf16[2,256,512]{2,1,0:T(8,128)(2,1)}, u32[]{:S(2)}, u32[]{:S(2)}) collective-permute-start(bf16[2,256,512]{2,1,0:T(8,128)(2,1)} %get-tuple-element.56), channel_id=1, source_target_pairs={{0,10},{1,11},{2,0},{3,1},{8,2},{9,3},{10,8},{11,9},{4,14},{5,15},... | collective-permute-start | bytes 1572872 | tf_op jit(solution)/shard_map/exchange_up_maps/ppermute | solution.py:374
  60.8 5.0 %copy-start.7 = (bf16[2,256,512]{2,1,0:T(8,128)(2,1)}, bf16[2,256,512]{2,1,0:T(8,128)(2,1)S(1)}, u32[]{:S(2)}) copy-start(bf16[2,256,512]{2,1,0:T(8,128)(2,1)S(1)} %collective-permute-done.1.rest_2_) | copy-start | bytes 1572868
  60.8 27.6 %collective-permute-start.6 = (bf16[2,256,512]{2,1,0:T(8,128)(2,1)}, bf16[2,256,512]{2,1,0:T(8,128)(2,1)}, u32[]{:S(2)}, u32[]{:S(2)}) collective-permute-start(bf16[2,256,512]{2,1,0:T(8,128)(2,1)} %get-tuple-element.57), channel_id=1, source_target_pairs={{0,11},{1,0},{2,1},{3,2},{8,3},{9,8},{10,9},{11,10},{4,15},{5,4},{... | collective-permute-start | bytes 1572872 | tf_op jit(solution)/shard_map/exchange_up_maps/ppermute | solution.py:374
  67.5 26.4 %copy-start.8 = (bf16[2,256,512]{2,1,0:T(8,128)(2,1)}, bf16[2,256,512]{2,1,0:T(8,128)(2,1)S(1)}, u32[]{:S(2)}) copy-start(bf16[2,256,512]{2,1,0:T(8,128)(2,1)S(1)} %collective-permute-done.2.rest_3_) | copy-start | bytes 1572868
  89.4 19.7 %copy-start.5 = (s32[2,128]{1,0:T(2,128)S(1)}, s32[2,128]{1,0:T(2,128)}, u32[]{:S(2)}) copy-start(s32[2,128]{1,0:T(2,128)} %fusion.1) | copy-start | bytes 3076
  130.8 17.9 %all-to-all-start.4 = ((bf16[16,8,16,256]{3,2,1,0:T(8,128)(2,1)}), bf16[16,8,16,256]{3,2,1,0:T(8,128)(2,1)S(1)}, u32[]{:S(2)}, u32[]{:S(2)}) async-start(bf16[16,8,16,256]{3,2,1,0:T(8,128)(2,1)} %attend.1), calls=%async_computation.4 | async-start | bytes 2097152 | tf_op jit(solution)/shard_map/attend/all_to_all | solution.py:434
  148.7 2.1 %copy-start.1 = (bf16[16,8,16,256]{3,2,1,0:T(8,128)(2,1)}, bf16[16,8,16,256]{3,2,1,0:T(8,128)(2,1)S(1)}, u32[]{:S(2)}) copy-start(bf16[16,8,16,256]{3,2,1,0:T(8,128)(2,1)S(1)} %all-to-all-done.4.attended) | copy-start | bytes 3145732
  148.7 1.1 copy-start.4
  154.8 12.2 %copy-start.3 = (bf16[400,512]{1,0:T(8,128)(2,1)S(1)}, bf16[400,512]{1,0:T(8,128)(2,1)}, u32[]{:S(2)}) copy-start(bf16[400,512]{1,0:T(8,128)(2,1)} %get-tuple-element.76.up) | copy-start | bytes 1228804
  154.8 12.2 %collective-permute-start.7 = (bf16[256,512]{1,0:T(8,128)(2,1)}, bf16[256,512]{1,0:T(8,128)(2,1)S(1)}, u32[]{:S(2)}, u32[]{:S(2)}) collective-permute-start(bf16[256,512]{1,0:T(8,128)(2,1)} %base_out.3), channel_id=1, source_target_pairs={{0,4},{4,0},{1,5},{5,1},{2,6},{6,2},{3,7},{7,3},{8,12},{12,8},{9,1... | collective-permute-start | bytes 786440 | tf_op jit(solution)/shard_map/output/ppermute | solution.py:479
  154.9 12.1 %all-to-all-start.5 = ((bf16[16,16,256]{2,1,0:T(8,128)(2,1)}), bf16[16,16,256]{2,1,0:T(8,128)(2,1)S(1)}, u32[]{:S(2)}, u32[]{:S(2)}) async-start(bf16[16,16,256]{2,1,0:T(8,128)(2,1)} %shrink_out.1), calls=%async_computation.5 | async-start | bytes 262144 | tf_op jit(solution)/shard_map/output/all_to_all | solution.py:462
  167.0 1.0 copy-start.2
Sparse Core Ops, SparseCore 0:
  9.2 72.1 all-gather.4
  88.5 42.2 all-gather.6

commit v5 on v4

--- a/solution.py
+++ b/solution.py
@@ -19,11 +19,16 @@
 N = 16
 SIDE = 4
 RING = 8
+GROUPED = 2
 PAIR = 2
 ALL_ROWS = STEPS * ROWS
 LOCAL = ROWS // N
 MINE = STEPS * LOCAL
 ENTRIES = 1 + STEPS * LOADS
+SHARED = 8
+Q_AT = HELD * 48
+KV_AT = Q_AT + HELD // 2 * RANK
+PACKED = KV_AT + 2 * RANK
 IN_RANK = 3 * RANK
 PER_DOT = 5
 QF = 256
@@ -66,10 +71,45 @@
     return lax.broadcasted_iota(jnp.int32, shape, axis)
 
 
+def pack_kernel(maps_in, maps_q, maps_k, maps_v, out, all_q, all_k, all_v, in_sem, sem):
+    copies = [
+        pltpu.make_async_copy(maps_q, all_q, sem.at[0]),
+        pltpu.make_async_copy(maps_k, all_k, sem.at[1]),
+        pltpu.make_async_copy(maps_v, all_v, sem.at[2]),
+    ]
+    for k in range(HELD):
+        rows = pl.ds(k * IN_RANK, IN_RANK)
+        copies.append(pltpu.make_async_copy(maps_in.at[k], out.at[rows], in_sem.at[k]))
+    for copy in copies:
+        copy.start()
+    for copy in copies[:3]:
+        copy.wait()
+    for k in range(HELD):
+        low, block = Q_AT + k // 2 * RANK, k % 2 * QF
+        out[low : low + RANK, block : block + QF] = all_q[k]
+    empty = jnp.zeros((RANK, 2 * KF), BF16)
+    for first in range(0, 2 * SHARED, SHARED):
+        pieces = []
+        for k in range(first, first + SHARED):
+            pieces += [all_k[k], all_v[k]] if k < HELD else [empty]
+        low = KV_AT + first // SHARED * RANK
+        out[low : low + RANK] = jnp.concatenate(pieces, axis=1)
+    for copy in copies[3:]:
+        copy.wait()
+
+
+def aligned(value, unit):
+    return pl.multiple_of(value * unit, unit)
+
+
 def shrink_kernel(index, pool, slot, tokens, entry, out, maps, arrived):
     copies = []
     for i in range(ENTRIES):
-        origin = slot.at[index[0]] if i == 0 else pool.at[index[i]]
+        if i == 0:
+            origin = slot.at[index[0]]
+        else:
+            rows = pl.ds(aligned(lax.rem(index[i], HELD), IN_RANK), IN_RANK)
+            origin = pool.at[index[i] // HELD, rows]
         copy = pltpu.make_async_copy(origin, maps.at[pl.ds(i * IN_RANK, IN_RANK)], arrived.at[i])
         copy.start()
         copies.append(copy)
@@ -95,47 +135,64 @@
     return jnp.concatenate(blocks, axis=0).astype(BF16)
 
 
-def expand_by_rank(shrunk, entry):
-    loads = STEPS * LOADS
-    chosen = iota((loads, ALL_ROWS), 0) + 1 == entry
-    blocks = [jnp.where(chosen, shrunk[r : r + 1, :], 0.0) for r in range(RANK)]
-    kept = jnp.where(entry == 0, shrunk, 0.0)
-    return jnp.concatenate(blocks + [kept], axis=0).astype(BF16)
-
-
 def contract(left, right):
     return lax.dot_general(left, right, (((0,), (0,)), ((), ())), preferred_element_type=F32)
 
 
-def project_kernel(parts, entry, base_q, base_kv, up, out):
+def pick_up_kernel(index, pool, slot_q, slot_k, slot_v, up_q, up_kv, q_sem, kv_sem):
+    copies = []
+    for i in range(ENTRIES):
+        rows = pl.ds(i * RANK, RANK)
+        if i == 0:
+            copies.append(pltpu.make_async_copy(slot_q.at[index[0]], up_q.at[rows], q_sem.at[0]))
+            continue
+        source, k = index[i] // HELD, lax.rem(index[i], HELD)
+        of_q = pl.ds(Q_AT + aligned(k // 2, RANK), RANK)
+        block = pl.ds(aligned(lax.rem(k, 2), QF), QF)
+        of_kv = pl.ds(KV_AT + aligned(k // SHARED, RANK), RANK)
+        copies.append(
+            pltpu.make_async_copy(pool.at[source, of_q, block], up_q.at[rows], q_sem.at[i])
+        )
+        copies.append(pltpu.make_async_copy(pool.at[source, of_kv], up_kv.at[rows], kv_sem.at[i]))
+    for copy in copies:
+        copy.start()
+    empty = jnp.zeros((RANK, IN_PART - 2 * KF), BF16)
+    up_kv[:RANK] = jnp.concatenate([slot_k[index[0]], slot_v[index[0]], empty], axis=1)
+    for copy in copies:
+        copy.wait()
+
+
+def project_kernel(parts, entry, block, base_q, base_kv, up_q, up_kv, out):
     shrunk = jnp.sum(parts[...].astype(F32), axis=0).astype(BF16).astype(F32)
     used = entry[...]
-    up_q, up_kv = up[:, :QF], up[:, QF:]
-    wide_q = expand_by_rank(shrunk[:RANK], used)
-    wide_k = expand_by_rank(shrunk[RANK : 2 * RANK], used)
-    wide_v = expand_by_rank(shrunk[2 * RANK :], used)
-    query = base_q[...] + low_rank_scale * contract(wide_q, up_q)
-    delta_k = contract(wide_k, up_kv)
-    delta_v = contract(wide_v, up_kv)
-    column = iota(delta_k.shape, 1)
-    delta = jnp.where(column < KF, delta_k, delta_v)
-    fresh = base_kv[...] + low_rank_scale * delta
+    wide_q = expand(shrunk[:RANK], used)
+    wide_k = expand(shrunk[RANK : 2 * RANK], used)
+    wide_v = expand(shrunk[2 * RANK :], used)
+    query = base_q[...] + low_rank_scale * contract(wide_q, up_q[...])
+    delta_k = contract(wide_k, up_kv[...])
+    delta_v = contract(wide_v, up_kv[...])
+    delta = jnp.where(iota(delta_k.shape, 1) % (2 * KF) < KF, delta_k, delta_v)
+    delta = jnp.where(iota(delta.shape, 1) // (2 * KF) == block[...], delta, 0.0)
+    folded = jnp.zeros((ALL_ROWS, 2 * KF), F32)
+    for j in range(SHARED):
+        folded = folded + delta[:, j * 2 * KF : (j + 1) * 2 * KF]
+    fresh = base_kv[...] + low_rank_scale * folded
     for t in range(N):
         lows = [s * ROWS + t * LOCAL for s in range(STEPS)]
         out[t, :, :QF] = jnp.concatenate([query[n : n + LOCAL] for n in lows], 0).astype(BF16)
         out[t, :, QF:] = jnp.concatenate([fresh[n : n + LOCAL] for n in lows], 0).astype(BF16)
 
 
-def split_kernel(place, weight, *rest):
-    outs, arrived = rest[:RING], rest[RING]
+def split_kernel(side, weight, out, arrived):
+    half = QF // 2
+    rows = pl.ds(aligned(side[0], half), half)
     copies = []
-    for k in range(RING):
-        other = lax.rem(place[0] + k, RING)
-        for n in range(PAIR):
-            block = (other // SIDE * PAIR + n) * SIDE + lax.rem(other, SIDE)
-            column = pl.multiple_of(block * OUT_PART, OUT_PART)
-            source = weight.at[:, pl.ds(column, OUT_PART)]
-            copies.append(pltpu.make_async_copy(source, outs[k].at[n], arrived.at[k, n]))
+    for t in range(N):
+        high, low, x = t // (PAIR * SIDE), t // SIDE % PAIR, t % SIDE
+        source = weight.at[rows, pl.ds(t * OUT_PART, OUT_PART)]
+        copies.append(
+            pltpu.make_async_copy(source, out.at[high * SIDE + x, low], arrived.at[t])
+        )
     for copy in copies:
         copy.start()
     for copy in copies:
@@ -186,6 +243,10 @@
     scale = 1.0 / math.sqrt(HD)
     dims = (((1,), (1,)), ((), ()))
     for i in range(LOCAL):
+        if i % GROUPED == 0:
+            for pair in loads[i : i + GROUPED]:
+                for copy in pair:
+                    copy.wait()
         asked = []
         for s in range(STEPS):
             low = (s * LOCAL + i) * N
@@ -194,7 +255,6 @@
         spread = jnp.where(own, jnp.concatenate([asked] * KH, axis=1), jnp.zeros((), BF16))
         new = lax.dot_general(spread, keys_new, dims, preferred_element_type=F32) * scale
         new = jnp.where(in_time & (new_row == i), new, -jnp.inf)
-        loads[i][0].wait()
         old = lax.dot_general(spread, key_rows[i], dims, preferred_element_type=F32) * scale
         old = jnp.where(place < lengths[i], old, -jnp.inf)
         highest = jnp.maximum(
@@ -202,7 +262,6 @@
         )
         old, new = jnp.exp(old - highest), jnp.exp(new - highest)
         totals = jnp.sum(old, axis=1, keepdims=True) + jnp.sum(new, axis=1, keepdims=True)
-        loads[i][1].wait()
         mixed = jnp.dot(old.astype(BF16), value_rows[i], preferred_element_type=F32)
         mixed = mixed + jnp.dot(new.astype(BF16), values_new, preferred_element_type=F32)
         mixed = jnp.where(own, mixed, 0.0)
@@ -260,28 +319,31 @@
         out[n] = shrunk
 
 
-def base_out_kernel(place, member, attended, *rest):
-    sources = rest[:RING]
-    out, columns, column_sem = rest[RING:]
-    copies = []
-    for k in range(RING):
-        copy = pltpu.make_async_copy(
-            sources[k].at[member[0]], columns.at[pl.ds(k * QF, QF)], column_sem.at[k]
-        )
-        copy.start()
-        copies.append(copy)
-    heads = []
-    for k in range(RING):
-        block = lax.rem(place[0] + RING - k, RING)
-        heads.append(attended[:, pl.ds(block, 1)].reshape(ALL_ROWS, QF))
-    total = jnp.zeros((ALL_ROWS, OUT_PART), F32)
-    for k in range(0, RING, PAIR):
-        for copy in copies[k : k + PAIR]:
-            copy.wait()
-        part = jnp.concatenate(heads[k : k + PAIR], axis=1)
-        rows = columns[k * QF : (k + PAIR) * QF]
-        total = total + jnp.dot(part, rows, preferred_element_type=F32)
-    out[...] = total.astype(out.dtype)
+def base_out_kernel(side, member, attended, mine, others, passed, kept, columns, sems):
+    half = QF // 2
+    near = aligned(side[0], half)
+    loads = []
+    for which in range(PAIR):
+        whose = (1 - member[0], member[0])[which]
+        for j in range(RING):
+            for n, (source, low) in enumerate(((mine, near), (others, half - near))):
+                rows = pl.ds(pl.multiple_of(j * QF + low, half), half)
+                copy = pltpu.make_async_copy(
+                    source.at[j, whose], columns.at[which, rows], sems.at[which, j, n]
+                )
+                copy.start()
+                loads.append(copy)
+    for which, out in enumerate((passed, kept)):
+        total = jnp.zeros((ALL_ROWS, OUT_PART), F32)
+        for j in range(0, RING, PAIR):
+            first = 2 * (which * RING + j)
+            for copy in loads[first : first + 2 * PAIR]:
+                copy.wait()
+            heads = [attended[:, n].reshape(ALL_ROWS, QF) for n in range(j, j + PAIR)]
+            part = jnp.concatenate(heads, axis=1)
+            rows = columns[which, j * QF : (j + PAIR) * QF]
+            total = total + jnp.dot(part, rows, preferred_element_type=F32)
+        out[...] = total.astype(out.dtype)
 
 
 def final_kernel(parts, entry, kept, arrived, up, out):
@@ -303,16 +365,31 @@
     part = lax.axis_index(TP)
     place = lax.axis_index(AROUND)[None]
     member = lax.axis_index("lo")[None]
+    side = (me % 2)[None]
 
     with jax.named_scope("gather_in_maps"):
-        whole_in = lax.all_gather(pool_a_in, "group").reshape(N * HELD, IN_RANK, IN_PART)
+        packed = pl.pallas_call(
+            pack_kernel,
+            out_shape=jax.ShapeDtypeStruct((PACKED, IN_PART), BF16),
+            in_specs=[hbm()] * 4,
+            out_specs=vmem(),
+            scratch_shapes=[
+                pltpu.VMEM((HELD, RANK, QF), BF16),
+                pltpu.VMEM((HELD, RANK, KF), BF16),
+                pltpu.VMEM((HELD, RANK, KF), BF16),
+                pltpu.SemaphoreType.DMA((HELD,)),
+                pltpu.SemaphoreType.DMA((3,)),
+            ],
+            compiler_params=params(58),
+            cost_estimate=cost(0, 2 << 20),
+            name="pack",
+        )(pool_a_in, pool_b_q, pool_b_k, pool_b_v)
+        pool = lax.all_gather(packed, "group")
 
     with jax.named_scope("positions"):
         position = jnp.sum(
             jnp.where(evict_adapter[..., None] == jnp.arange(N * HELD), owner, 0), axis=-1
         )
-        position = position.reshape(STEPS, N, LOADS)
-        wanted = position.transpose(1, 0, 2).reshape(N, STEPS * LOADS)
         targets = lax.dynamic_slice_in_dim(evict_slot, me * LOADS, LOADS, 1)
         survivor = SLOTS * (SLOTS - 1) // 2 - jnp.sum(targets[0])
         placed = targets[:, :, None] == jnp.arange(SLOTS)
@@ -327,25 +404,31 @@
             axis=-1,
         )
         by_step = entry.reshape(1, ALL_ROWS)
+        blocks = position % HELD % SHARED
+        blocks = lax.dynamic_slice_in_dim(blocks, me * LOADS, LOADS, 1).reshape(1, 1, -1)
+        load = jnp.arange(STEPS * LOADS) + 1
+        blocks = jnp.sum(jnp.where(entry[:, :, None] == load, blocks, 0), axis=-1)
+        blocks = blocks.reshape(ALL_ROWS, 1)
         by_owner = entry.reshape(STEPS, N, LOCAL).transpose(1, 0, 2)
         by_owner = by_owner.reshape(1, ALL_ROWS)
-        my_wanted = lax.dynamic_index_in_dim(position, me, 1, keepdims=False)
+        my_wanted = lax.dynamic_slice_in_dim(position, me * LOADS, LOADS, 1)
         my_wanted = my_wanted.reshape(STEPS * LOADS)
         index = jnp.concatenate([survivor[None], my_wanted]).astype(jnp.int32)
 
-    turns = [[(i, (i + k) % RING) for i in range(RING)] for k in range(1, RING)]
     with jax.named_scope("columns_of_w_out"):
-        block = jax.ShapeDtypeStruct((PAIR, QF, OUT_PART), BF16)
-        columns = pl.pallas_call(
+        w_out, packed = lax.optimization_barrier((w_out, packed))
+        half = pl.pallas_call(
             split_kernel,
-            out_shape=[block] * RING,
+            out_shape=jax.ShapeDtypeStruct((RING, PAIR, QF // 2, OUT_PART), BF16),
             in_specs=[smem(), hbm()],
-            out_specs=[vmem()] * RING,
-            scratch_shapes=[pltpu.SemaphoreType.DMA((RING, PAIR))],
+            out_specs=vmem(),
+            scratch_shapes=[pltpu.SemaphoreType.DMA((N,))],
             compiler_params=params(56),
             cost_estimate=cost(0, 8 << 20),
             name="split",
-        )(place, w_out)
+        )(side, w_out)
+        mine = lax.all_to_all(half, AROUND, split_axis=0, concat_axis=0, tiled=True)
+        others = lax.ppermute(mine, "group", [(i, i ^ 1) for i in range(N)])
 
     with jax.named_scope("base_projections"):
         tokens = hidden.reshape(ALL_ROWS, -1)
@@ -359,28 +442,10 @@
         )
         tokens_part = lax.dynamic_slice_in_dim(tokens, part * IN_PART, IN_PART, 1)
 
-    with jax.named_scope("exchange_up_maps"):
-        rest = jnp.concatenate([pool_b_q, pool_b_k, pool_b_v], axis=2)
-        rest, *columns = lax.optimization_barrier((rest, *columns))
-        by_rank = lax.all_to_all(
-            rest.transpose(1, 0, 2), "group", split_axis=0, concat_axis=0, tiled=True
-        ).reshape(N * HELD, QKV)
-        pick = (wanted.reshape(-1, 1) == jnp.arange(N * HELD)).astype(BF16)
-        sent = jnp.dot(pick, by_rank, preferred_element_type=F32).astype(BF16)
-        loaded = lax.all_to_all(
-            sent.reshape(N, STEPS * LOADS, QKV), "group", split_axis=0, concat_axis=0, tiled=True
-        ).reshape(RANK * STEPS * LOADS, QKV)
-        columns = columns[:1] + [
-            lax.ppermute(c, AROUND, turn) for c, turn in zip(columns[1:], turns)
-        ]
-        survived = lambda piece: lax.dynamic_index_in_dim(piece, survivor, 0, keepdims=False)
-        kept = jnp.concatenate([survived(p) for p in (slot_b_q, slot_b_k, slot_b_v)], axis=1)
-        up = jnp.concatenate([loaded, kept], axis=0)
-
     with jax.named_scope("gather_out_maps"):
         out_pool = jnp.concatenate([pool_a_o, pool_b_o], axis=2)
-        out_pool, index, up, base_q, base_kv, tokens_part, *columns = lax.optimization_barrier(
-            (out_pool, index, up, base_q, base_kv, tokens_part, *columns)
+        out_pool, index, base_q, base_kv, tokens_part, mine = lax.optimization_barrier(
+            (out_pool, index, base_q, base_kv, tokens_part, mine)
         )
         out_pool = lax.all_gather(out_pool, "group").reshape(N * HELD, RANK, QF + OUT_PART)
 
@@ -397,19 +462,34 @@
             compiler_params=params(56),
             cost_estimate=cost(2 * ENTRIES * IN_RANK * IN_PART * ALL_ROWS, 2 << 20),
             name="shrink",
-        )(index, whole_in, slot_a_in, tokens_part, by_step)
+        )(index, pool, slot_a_in, tokens_part, by_step)
+
+        partial_in, picks = lax.optimization_barrier((partial_in, index))
         partials = lax.all_to_all(partial_in, TP, split_axis=0, concat_axis=0, tiled=True)
 
     with jax.named_scope("project"):
+        up_q, up_kv = pl.pallas_call(
+            pick_up_kernel,
+            out_shape=[
+                jax.ShapeDtypeStruct((ENTRIES * RANK, QF), BF16),
+                jax.ShapeDtypeStruct((ENTRIES * RANK, IN_PART), BF16),
+            ],
+            in_specs=[smem(), hbm(), hbm(), vmem(), vmem()],
+            out_specs=[vmem()] * 2,
+            scratch_shapes=[pltpu.SemaphoreType.DMA((ENTRIES,))] * 2,
+            compiler_params=params(52),
+            cost_estimate=cost(0, 2 << 20),
+            name="pick_up",
+        )(picks, pool, slot_b_q, slot_b_k, slot_b_v)
         projected = pl.pallas_call(
             project_kernel,
             out_shape=jax.ShapeDtypeStruct((N, MINE, QF + 2 * KF), BF16),
-            in_specs=[vmem()] * 5,
+            in_specs=[vmem()] * 7,
             out_specs=vmem(),
             compiler_params=params(16),
             cost_estimate=cost(2 * 400 * 512 * ALL_ROWS, 1 << 20),
             name="project",
-        )(partials, by_step, base_q, base_kv, up)
+        )(partials, by_step, blocks, base_q, base_kv, up_q, up_kv)
 
     with jax.named_scope("attend"):
         received = lax.all_to_all(projected, TP, split_axis=0, concat_axis=0, tiled=True)
@@ -443,7 +523,7 @@
             in_specs=[smem()] + [hbm()] * 3,
             out_specs=[vmem()] * 2,
             scratch_shapes=[pltpu.SemaphoreType.DMA((ENTRIES,))] * 2,
-            compiler_params=params(56),
+            compiler_params=params(24),
             cost_estimate=cost(0, 3 << 20),
             name="pick",
         )(picks, slot_a_o, slot_b_o, out_pool)
@@ -461,23 +541,23 @@
         partial_out, member = lax.optimization_barrier((partial_out, member))
         partials_out = lax.all_to_all(partial_out, TP, split_axis=0, concat_axis=0, tiled=True)
 
-        def base_out(whose, dtype):
-            return pl.pallas_call(
-                base_out_kernel,
-                out_shape=jax.ShapeDtypeStruct((ALL_ROWS, OUT_PART), dtype),
-                in_specs=[smem()] * 2 + [vmem()] + [hbm()] * RING,
-                out_specs=vmem(),
-                scratch_shapes=[
-                    pltpu.VMEM((RING * QF, OUT_PART), BF16),
-                    pltpu.SemaphoreType.DMA((RING,)),
-                ],
-                compiler_params=params(56),
-                cost_estimate=cost(2 * ALL_ROWS * WIDE * OUT_PART, 3 << 20),
-                name="base_out",
-            )(place, whose, gathered, *columns)
-
-        passed = lax.ppermute(base_out(1 - member, BF16), "lo", [(0, 1), (1, 0)])
-        kept_out = base_out(member, F32)
+        passed, kept_out = pl.pallas_call(
+            base_out_kernel,
+            out_shape=[
+                jax.ShapeDtypeStruct((ALL_ROWS, OUT_PART), BF16),
+                jax.ShapeDtypeStruct((ALL_ROWS, OUT_PART), F32),
+            ],
+            in_specs=[smem()] * 2 + [vmem()] + [hbm()] * 2,
+            out_specs=[vmem()] * 2,
+            scratch_shapes=[
+                pltpu.VMEM((PAIR, RING * QF, OUT_PART), BF16),
+                pltpu.SemaphoreType.DMA((PAIR, RING, 2)),
+            ],
+            compiler_params=params(24),
+            cost_estimate=cost(4 * ALL_ROWS * WIDE * OUT_PART, 5 << 20),
+            name="base_out",
+        )(side, member, gathered, mine, others)
+        passed = lax.ppermute(passed, "lo", [(0, 1), (1, 0)])
         return pl.pallas_call(
             final_kernel,
             out_shape=jax.ShapeDtypeStruct((STEPS, ROWS, OUT_PART), BF16),

time: 177 us -> 169 us (0.955)
  waiting for transfers between devices: 40.1 us -> 65.2 us
  starting transfers between devices: 38.8 us -> 17.9 us
  local copies, waits for them, and re-layouts: 8.83 us -> 3.89 us
  Pallas kernels: 31.9 us -> 28.1 us
  blocking collectives: 26.9 us -> 23.6 us
    all_gather x1, waiting for transfers between devices: 0.01 us -> 31.9 us  [shard(): pool = lax.all_gather(packed, 'group')]
    ppermute x8 -> x2, waiting for transfers between devices: 22.9 us -> 0.01 us  [the longest x1 0.01 us: shard(): others = lax.ppermute(mine, 'group', [(i, i ^ 1) for i in range(N)])]
    all_to_all x3 -> x2, waiting for transfers between devices: 5.5 us -> 21.7 us  [the longest x1 14 us: shard(): mine = lax.all_to_all(half, AROUND, split_axis=0, concat_axis=0, tiled=True)]
    ppermute x8 -> x2, starting transfers between devices: 15.2 us -> 0.14 us  [the longest x1 0.09 us: shard(): passed = lax.ppermute(passed, 'lo', [(0, 1), (1, 0)])]
    all_to_all x3 -> x2, starting transfers between devices: 20 us -> 13.9 us  [the longest x1 7.07 us: shard(): mine = lax.all_to_all(half, AROUND, split_axis=0, concat_axis=0, tiled=True)]
    all_to_all x1, blocking collectives: 15.3 us -> 12 us  [shard(): lax.all_to_all(partial_out, TP, split_axis=0, concat_axis=0, tiled=True)]
    unnamed x37 -> x34, local copies, waits for them, and re-layouts: 4.81 us -> 2.41 us
    pallas_call x3 -> x4, Pallas kernels: 12.6 us -> 11.2 us  [the longest x1 3.29 us: shard(): pl.pallas_call(base_out_kernel, out_shape=[jax.ShapeDtypeStruct((ALL_ROWS...]
  transfers between devices with their start and end apart: 14 -> 7, of which waited for: 7 -> 4; matrix products, arithmetic and copies ran while one was open for 12% -> 9% of each run, Pallas kernels for 15% -> 13%
where the time goes in v5:
time: 169 us; the launch traced here: 167 us
  waiting for transfers between devices  65.2 us (39%)
  Pallas kernels  28.1 us (17%)
  blocking collectives  23.6 us (14%)
  starting transfers between devices  17.9 us (11%)
  between operations  14.4 us (9%)
  matrix products  10.3 us (6%)
  local copies, waits for them, and re-layouts  3.89 us (2%)
  other arithmetic  3.38 us (2%)
    all_gather x1, waiting for transfers between devices, shard(): pool = lax.all_gather(packed, 'group')  31.9 us
    all_to_all x1, waiting for transfers between devices, shard(): mine = lax.all_to_all(half, AROUND, split_axis=0, concat_axis=0, tiled=True)  14 us
    all_to_all x1, blocking collectives, shard(): lax.all_to_all(partial_out, TP, split_axis=0, concat_axis=0, tiled=True)  12 us
    all_to_all x1, blocking collectives, shard(): lax.all_to_all(projected, TP, split_axis=0, concat_axis=0, tiled=True)  11.6 us
    all_to_all x1, waiting for transfers between devices, shard(): lax.all_to_all(payload, TP, split_axis=0, concat_axis=0, tiled=True)  11.5 us
    pallas_call x1, Pallas kernels, shard(): pl.pallas_call(attend_kernel, out_shape=jax.ShapeDtypeStruct((N, RING, MI...  8.84 us
    all_to_all x1, waiting for transfers between devices, shard(): lax.all_to_all(partial_in, TP, split_axis=0, concat_axis=0, tiled=True)  7.7 us
    all_to_all x1, starting transfers between devices, shard(): mine = lax.all_to_all(half, AROUND, split_axis=0, concat_axis=0, tiled=True)  7.07 us
  transfers between devices with their start and end apart: 7, of which 4 were waited for; matrix products, arithmetic and copies ran while one was open for 9% of the time, Pallas kernels for 13%

profile of v5, /device:TPU:32, one launch (start us, length us, event | category | flops | bytes accessed | tf_op | source)
XLA Modules:
  0.0 166.7 jit_solution(12140596548945138294)
XLA Ops:
  6.5 2.3 %pack.1 = bf16[704,512]{1,0:T(8,128)(2,1)} custom-call(bf16[12,48,512]{2,1,0:T(8,128)(2,1)} %maps_in.1, bf16[12,16,256]{2,1,0:T(8,128)(2,1)} %maps_q.1, bf16[12,16,32]{2,1,0:T(8,128)(2,1)} %maps_k.1, bf16[12,16,32]{2,1,0:T(8,128)(2,1)} %maps_v.1), custom_call_target="tpu_custom_call" | custom-call | bytes 2097152 | tf_op jit(solution)/shard_map/gather_in_maps/pack/pallas_call | solution.py:371
  8.9 3.2 %split.1 = bf16[8,2,128,512]{3,2,1,0:T(8,128)(2,1)} custom-call(s32[1]{0:T(128)} %bitcast.3.side, bf16[256,8192]{1,0:T(8,128)(2,1)} %weight), custom_call_target="tpu_custom_call" | custom-call | bytes 8388608 | tf_op jit(solution)/shard_map/columns_of_w_out/split/pallas_call | solution.py:420
  12.1 7.1 %all-to-all-start = ((bf16[8,2,128,512]{3,2,1,0:T(8,128)(2,1)}), bf16[8,2,128,512]{3,2,1,0:T(8,128)(2,1)}, u32[]{:S(2)}, u32[]{:S(2)}) async-start(bf16[8,2,128,512]{3,2,1,0:T(8,128)(2,1)} %split.1), calls=%async_computation | async-start | bytes 4194304 | tf_op jit(solution)/shard_map/columns_of_w_out/all_to_all | solution.py:430
  19.3 0.2 select_reduce_fusion
  19.8 0.6 slice_reduce_fusion
  21.1 0.7 pad_add_fusion.1.index
  21.8 4.2 %fusion.5 = f32[256,32]{1,0:T(8,128)S(1)} fusion(bf16[256,8192]{1,0:T(8,128)(2,1)} %bitcast.20, bf16[8192,32]{0,1:T(8,128)(2,1)S(1)} %copy-done), kind=kOutput, calls=%fused_computation.27 | convolution fusion | flops 134217728 | bytes 4751360 | tf_op jit(solution)/shard_map/base_projections/dot_general | solution.py:438
  26.0 1.2 fusion.6
  27.2 0.1 pad_maximum_fusion.1.base_kv
  27.3 0.7 constant_dynamic-slice_fusion.1.tokens
  28.1 0.7 pad_maximum_fusion
  28.8 4.9 %fusion.4.base_q = f32[256,256]{1,0:T(8,128)S(1)} fusion(bf16[256,8192]{1,0:T(8,128)(2,1)} %bitcast.21, bf16[8192,256]{1,0:T(8,128)(2,1)} %param.25), kind=kOutput, calls=%fused_computation.26 | convolution fusion | flops 1073741824 | bytes 8650752 | tf_op jit(solution)/shard_map/base_projections/dot_general | solution.py:435
  33.7 14.0 %all-to-all-done.mine = bf16[8,2,128,512]{3,2,1,0:T(8,128)(2,1)} async-done(((bf16[8,2,128,512]{3,2,1,0:T(8,128)(2,1)}), bf16[8,2,128,512]{3,2,1,0:T(8,128)(2,1)}, u32[]{:S(2)}, u32[]{:S(2)}) %all-to-all-start) | async-done | bytes 2097184 | tf_op jit(solution)/shard_map/columns_of_w_out/all_to_all | solution.py:430
  47.9 0.1 fusion.1
  48.2 0.7 fusion
  48.8 31.9 %all-gather.5.cloned.1.call-done = bf16[11264,512]{1,0:T(8,128)(2,1)} async-done(((bf16[704,512]{1,0:T(8,128)(2,1)}), bf16[11264,512]{1,0:T(8,128)(2,1)}) %all-gather.5.cloned.1.call-update) | async-done | bytes 11534352 | tf_op jit(solution)/shard_map/gather_in_maps/all_gather | solution.py:387
  80.7 4.4 %shrink.1 = bf16[16,48,256]{2,1,0:T(8,128)(2,1)} custom-call(s32[25]{0:T(128)} %pad_add_fusion.1.index, bf16[16,704,512]{2,1,0:T(8,128)(2,1)} %bitcast.17, bf16[13,48,512]{2,1,0:T(8,128)(2,1)} %slot.1, bf16[256,512]{1,0:T(8,128)(2,1)} %constant_dynamic-slice_fusion.1.tokens, s32[1,256]{1,0:T(1,128)} %bitcast.15), custom_call_target="tpu_custom_call" | custom-call | flops 314572800 | bytes 2097152 | tf_op jit(solution)/shard_map/shrink/shrink/pallas_call | solution.py:453
  85.1 6.8 %all-to-all-start.1 = ((bf16[16,48,256]{2,1,0:T(8,128)(2,1)}), bf16[16,48,256]{2,1,0:T(8,128)(2,1)S(1)}, u32[]{:S(2)}, u32[]{:S(2)}) async-start(bf16[16,48,256]{2,1,0:T(8,128)(2,1)} %shrink.1), calls=%async_computation.1 | async-start | bytes 786432 | tf_op jit(solution)/shard_map/shrink/all_to_all | solution.py:468
  92.1 0.1 copy.39.block
  92.3 2.4 %pick_up.1 = (bf16[400,256]{1,0:T(8,128)(2,1)S(1)}, bf16[400,512]{1,0:T(8,128)(2,1)S(1)}) custom-call(s32[25]{0:T(128)S(1)} %copy-done.8, bf16[16,704,512]{2,1,0:T(8,128)(2,1)} %bitcast.18, bf16[13,16,256]{2,1,0:T(8,128)(2,1)S(1)} %copy-done.3, bf16[13,16,32]{2,1,0:T(8,128)(2,1)S(1)} %copy-done.5, bf16[13,16,32]{2,1,0:T(8,128)(2,1)S(1)} %copy-done.6), custom_call_target="tpu_custom_call" | custom-call | bytes 2097152 | tf_op jit(solution)/shard_map/project/pick_up/pallas_call | solution.py:471
  94.8 7.7 %all-to-all-done.1.parts = bf16[16,48,256]{2,1,0:T(8,128)(2,1)S(1)} async-done(((bf16[16,48,256]{2,1,0:T(8,128)(2,1)}), bf16[16,48,256]{2,1,0:T(8,128)(2,1)S(1)}, u32[]{:S(2)}, u32[]{:S(2)}) %all-to-all-start.1) | async-done | bytes 393248 | tf_op jit(solution)/shard_map/shrink/all_to_all | solution.py:468
  102.4 0.7 project.1
  103.2 11.6 %all_to_all.25.received = bf16[16,16,320]{2,1,0:T(8,128)(2,1)} all-to-all(bf16[16,16,320]{2,1,0:T(8,128)(2,1)S(1)} %project.1), channel_id=1, replica_groups=mesh['group'=16,'hi'=2,'lo'=2,'x'=4] {'hi','lo','x'}, dimensions={0} | all-to-all | bytes 327680 | tf_op jit(solution)/shard_map/attend/all_to_all | solution.py:495
  114.8 8.8 %attend.1 = bf16[16,8,16,256]{3,2,1,0:T(8,128)(2,1)} custom-call(s32[8]{0:T(128)} %lengths.1, bf16[16,16,320]{2,1,0:T(8,128)(2,1)} %all_to_all.25.received, bf16[8,512,512]{2,1,0:T(8,128)(2,1)} %keys.1, bf16[8,512,512]{2,1,0:T(8,128)(2,1)} %values.1), custom_call_target="tpu_custom_call" | custom-call | flops 536870912 | bytes 12582912 | tf_op jit(solution)/shard_map/attend/attend/pallas_call | solution.py:496
  123.7 3.8 %all-to-all-start.3 = ((bf16[16,8,16,256]{3,2,1,0:T(8,128)(2,1)}), bf16[16,8,16,256]{3,2,1,0:T(8,128)(2,1)S(1)}, u32[]{:S(2)}, u32[]{:S(2)}) async-start(bf16[16,8,16,256]{3,2,1,0:T(8,128)(2,1)} %attend.1), calls=%async_computation.3 | async-start | bytes 2097152 | tf_op jit(solution)/shard_map/attend/all_to_all | solution.py:514
  127.8 2.3 %copy-done.1 = bf16[192,16,768]{2,1,0:T(8,128)(2,1)S(1)} copy-done((bf16[192,16,768]{2,1,0:T(8,128)(2,1)S(1)}, bf16[192,16,768]{2,1,0:T(8,128)(2,1)}, u32[]{:S(2)}) %copy-start.1) | copy-done | bytes 4718616
  130.1 1.6 pick.1
  131.7 11.5 %all-to-all-done.3.attended = bf16[16,8,16,256]{3,2,1,0:T(8,128)(2,1)S(1)} async-done(((bf16[16,8,16,256]{3,2,1,0:T(8,128)(2,1)}), bf16[16,8,16,256]{3,2,1,0:T(8,128)(2,1)S(1)}, u32[]{:S(2)}, u32[]{:S(2)}) %all-to-all-start.3) | async-done | bytes 1048608 | tf_op jit(solution)/shard_map/attend/all_to_all | solution.py:514
  143.2 0.3 shrink_out.1
  143.5 3.3 %base_out.1 = (bf16[256,512]{1,0:T(8,128)(2,1)S(1)}, f32[256,512]{1,0:T(8,128)S(1)}) custom-call(s32[1]{0:T(128)} %bitcast.3.side, s32[1]{0:T(128)} %bitcast.8.member, bf16[16,8,16,256]{3,2,1,0:T(8,128)(2,1)S(1)} %all-to-all-done.3.attended, bf16[8,2,128,512]{3,2,1,0:T(8,128)(2,1)} %all-to-all-done.mine, bf16[8,2,128,512]{3,2,1,0:T(8,128)(2,1)} %collective-permute-done.others), custom_call_target="tpu_custom_call" | custom-call | flops 1073741824 | bytes 5242880 | tf_op jit(solution)/shard_map/output/base_out/pallas_call | solution.py:544
  146.9 12.0 %all_to_all.26.parts = bf16[16,16,256]{2,1,0:T(8,128)(2,1)S(1)} all-to-all(bf16[16,16,256]{2,1,0:T(8,128)(2,1)S(1)} %shrink_out.1), channel_id=1, replica_groups=mesh['group'=16,'hi'=2,'lo'=2,'x'=4] {'hi','lo','x'}, dimensions={0} | all-to-all | bytes 262144 | tf_op jit(solution)/shard_map/output/all_to_all | solution.py:542
  158.9 1.1 final.1
  (58 shorter events, 1.2 us)
Async XLA Ops:
  6.5 15.2 %copy-start = (bf16[8192,32]{0,1:T(8,128)(2,1)S(1)}, bf16[8192,32]{0,1:T(8,128)(2,1)}, u32[]{:S(2)}) copy-start(bf16[8192,32]{0,1:T(8,128)(2,1)} %param.26) | copy-start | bytes 1572868
  6.5 74.1 %all-gather.5.cloned.1.call-start = ((), (), s32[]{:S(2)}) async-start(), calls=%async_computation.5 | async-start | bytes 12255232 | tf_op jit(solution)/shard_map/gather_in_maps/all_gather | solution.py:387
  8.8 10.4 %copy-start.12 = (s32[2,192]{1,0:T(2,128)S(1)}, s32[2,192]{1,0:T(2,128)}, u32[]{:S(2)}) copy-start(s32[2,192]{1,0:T(2,128)} %param.34) | copy-start | bytes 4612
  8.9 10.4 %copy-start.13 = (s32[192]{0:T(256)S(1)}, s32[192]{0:T(256)}, u32[]{:S(2)}) copy-start(s32[192]{0:T(256)} %param.35) | copy-start | bytes 2308
  8.9 10.9 %copy-start.15 = (s32[2,192]{1,0:T(2,128)S(1)}, s32[2,192]{1,0:T(2,128)}, u32[]{:S(2)}) copy-start(s32[2,192]{1,0:T(2,128)} %param.33) | copy-start | bytes 4612
  12.1 13.9 %copy-start.16 = (bf16[8192,32]{0,1:T(8,128)(2,1)S(1)}, bf16[8192,32]{0,1:T(8,128)(2,1)}, u32[]{:S(2)}) copy-start(bf16[8192,32]{0,1:T(8,128)(2,1)} %param.27) | copy-start | bytes 1572868
  12.1 35.6 %all-to-all-start = ((bf16[8,2,128,512]{3,2,1,0:T(8,128)(2,1)}), bf16[8,2,128,512]{3,2,1,0:T(8,128)(2,1)}, u32[]{:S(2)}, u32[]{:S(2)}) async-start(bf16[8,2,128,512]{3,2,1,0:T(8,128)(2,1)} %split.1), calls=%async_computation | async-start | bytes 4194304 | tf_op jit(solution)/shard_map/columns_of_w_out/all_to_all | solution.py:430
  19.2 108.6 %all-gather.7.cloned.1.call-start = ((), (), s32[]{:S(2)}) async-start(), calls=%async_computation.6 | async-start | bytes 5013504 | tf_op jit(solution)/shard_map/gather_out_maps/all_gather | solution.py:450
  21.1 4.9 %copy-start.11 = (bf16[2,128,8192]{2,1,0:T(8,128)(2,1)S(1)}, bf16[2,128,8192]{2,1,0:T(8,128)(2,1)}, u32[]{:S(2)}) copy-start(bf16[2,128,8192]{2,1,0:T(8,128)(2,1)} %param.24) | copy-start | bytes 12582916
  26.0 2.1 %copy-start.9 = (bf16[12,16,512]{2,1,0:T(8,128)(2,1)S(1)}, bf16[12,16,512]{2,1,0:T(8,128)(2,1)}, u32[]{:S(2)}) copy-start(bf16[12,16,512]{2,1,0:T(8,128)(2,1)} %param.41) | copy-start | bytes 589828
  26.0 2.1 %copy-start.10 = (bf16[12,16,256]{2,1,0:T(8,128)(2,1)S(1)}, bf16[12,16,256]{2,1,0:T(8,128)(2,1)}, u32[]{:S(2)}) copy-start(bf16[12,16,256]{2,1,0:T(8,128)(2,1)} %param.40) | copy-start | bytes 294916
  28.8 19.3 %copy-start.14 = (s32[2,128]{1,0:T(2,128)S(1)}, s32[2,128]{1,0:T(2,128)}, u32[]{:S(2)}) copy-start(s32[2,128]{1,0:T(2,128)} %param.32) | copy-start | bytes 3076
  47.9 95.6 %collective-permute-start = (bf16[8,2,128,512]{3,2,1,0:T(8,128)(2,1)}, bf16[8,2,128,512]{3,2,1,0:T(8,128)(2,1)}, u32[]{:S(2)}, u32[]{:S(2)}) collective-permute-start(bf16[8,2,128,512]{3,2,1,0:T(8,128)(2,1)} %all-to-all-done.mine), channel_id=1, source_target_pairs={{0,16},{16,0},{32,48},{48,32},{64,80},{80,64},{96,112},{112,96},{1... | collective-permute-start | bytes 6291464 | tf_op jit(solution)/shard_map/columns_of_w_out/ppermute | solution.py:431
  80.7 11.4 %copy-start.7 = (s32[2,128]{1,0:T(2,128)S(1)}, s32[2,128]{1,0:T(2,128)}, u32[]{:S(2)}) copy-start(s32[2,128]{1,0:T(2,128)} %fusion) | copy-start | bytes 3076
  80.7 11.6 %copy-start.3 = (bf16[13,16,256]{2,1,0:T(8,128)(2,1)S(1)}, bf16[13,16,256]{2,1,0:T(8,128)(2,1)}, u32[]{:S(2)}) copy-start(bf16[13,16,256]{2,1,0:T(8,128)(2,1)} %slot_q.1) | copy-start | bytes 319492
  80.7 11.6 %copy-start.5 = (bf16[13,16,32]{2,1,0:T(8,128)(2,1)S(1)}, bf16[13,16,32]{2,1,0:T(8,128)(2,1)}, u32[]{:S(2)}) copy-start(bf16[13,16,32]{2,1,0:T(8,128)(2,1)} %slot_k.1) | copy-start | bytes 39940
  80.7 11.6 %copy-start.6 = (bf16[13,16,32]{2,1,0:T(8,128)(2,1)S(1)}, bf16[13,16,32]{2,1,0:T(8,128)(2,1)}, u32[]{:S(2)}) copy-start(bf16[13,16,32]{2,1,0:T(8,128)(2,1)} %slot_v.1) | copy-start | bytes 39940
  80.7 11.6 %copy-start.8 = (s32[25]{0:T(128)S(1)}, s32[25]{0:T(128)}, u32[]{:S(2)}) copy-start(s32[25]{0:T(128)} %pad_add_fusion.1.index) | copy-start | bytes 304
  85.1 17.3 %all-to-all-start.1 = ((bf16[16,48,256]{2,1,0:T(8,128)(2,1)}), bf16[16,48,256]{2,1,0:T(8,128)(2,1)S(1)}, u32[]{:S(2)}, u32[]{:S(2)}) async-start(bf16[16,48,256]{2,1,0:T(8,128)(2,1)} %shrink.1), calls=%async_computation.1 | async-start | bytes 786432 | tf_op jit(solution)/shard_map/shrink/all_to_all | solution.py:468
  114.8 12.9 %copy-start.2 = (bf16[13,16,512]{2,1,0:T(8,128)(2,1)S(1)}, bf16[13,16,512]{2,1,0:T(8,128)(2,1)}, u32[]{:S(2)}) copy-start(bf16[13,16,512]{2,1,0:T(8,128)(2,1)} %slot_up.1) | copy-start | bytes 638980
  114.8 13.0 %copy-start.4 = (bf16[13,16,256]{2,1,0:T(8,128)(2,1)S(1)}, bf16[13,16,256]{2,1,0:T(8,128)(2,1)}, u32[]{:S(2)}) copy-start(bf16[13,16,256]{2,1,0:T(8,128)(2,1)} %slot_in.1) | copy-start | bytes 319492
  123.7 19.5 %all-to-all-start.3 = ((bf16[16,8,16,256]{3,2,1,0:T(8,128)(2,1)}), bf16[16,8,16,256]{3,2,1,0:T(8,128)(2,1)S(1)}, u32[]{:S(2)}, u32[]{:S(2)}) async-start(bf16[16,8,16,256]{3,2,1,0:T(8,128)(2,1)} %attend.1), calls=%async_computation.3 | async-start | bytes 2097152 | tf_op jit(solution)/shard_map/attend/all_to_all | solution.py:514
  127.8 2.3 %copy-start.1 = (bf16[192,16,768]{2,1,0:T(8,128)(2,1)S(1)}, bf16[192,16,768]{2,1,0:T(8,128)(2,1)}, u32[]{:S(2)}) copy-start(bf16[192,16,768]{2,1,0:T(8,128)(2,1)} %all-gather.7.cloned.1.call-done.pool) | copy-start | bytes 14155780
  146.8 12.1 %collective-permute-start.1 = (bf16[256,512]{1,0:T(8,128)(2,1)S(1)}, bf16[256,512]{1,0:T(8,128)(2,1)S(1)}, u32[]{:S(2)}, u32[]{:S(2)}) collective-permute-start(bf16[256,512]{1,0:T(8,128)(2,1)S(1)} %get-tuple-element.39), channel_id=1, source_target_pairs={{0,4},{4,0},{1,5},{5,1},{2,6},{6,2},{3,7},{7,3},{8,12},{12,8},{9,1... | collective-permute-start | bytes 786440 | tf_op jit(solution)/shard_map/output/ppermute | solution.py:560
Sparse Core Ops, SparseCore 0:
  9.2 71.4 all-gather.4
  82.5 42.6 all-gather.6

commit v6 on v5

--- a/solution.py
+++ b/solution.py
@@ -18,9 +18,7 @@
 HELD = 12
 N = 16
 SIDE = 4
-RING = 8
 GROUPED = 2
-PAIR = 2
 ALL_ROWS = STEPS * ROWS
 LOCAL = ROWS // N
 MINE = STEPS * LOCAL
@@ -30,16 +28,14 @@
 KV_AT = Q_AT + HELD // 2 * RANK
 PACKED = KV_AT + 2 * RANK
 IN_RANK = 3 * RANK
-PER_DOT = 5
 QF = 256
 KF = 32
 IN_PART = 512
 OUT_PART = 512
 FEATURES = QH * HD
-WIDE = RING * QF
+WIDE = SIDE * QF
 QKV = QF + 2 * KF
-TP = ("hi", "lo", "x")
-AROUND = ("hi", "x")
+TP = ("y", "x")
 LENGTH = 512
 KW = KH * HD
 BF16 = jnp.bfloat16
@@ -113,18 +109,13 @@
         copy = pltpu.make_async_copy(origin, maps.at[pl.ds(i * IN_RANK, IN_RANK)], arrived.at[i])
         copy.start()
         copies.append(copy)
+    for copy in copies:
+        copy.wait()
     used = entry[...]
+    product = jnp.dot(maps[...], tokens[...], preferred_element_type=F32)
     total = jnp.zeros((IN_RANK, ALL_ROWS), F32)
-    for first in range(0, ENTRIES, PER_DOT):
-        for i in range(first, first + PER_DOT):
-            copies[i].wait()
-        block = maps[pl.ds(first * IN_RANK, PER_DOT * IN_RANK), :]
-        product = lax.dot_general(
-            block, tokens[...], (((1,), (1,)), ((), ())), preferred_element_type=F32
-        )
-        for k in range(PER_DOT):
-            piece = product[k * IN_RANK : (k + 1) * IN_RANK]
-            total = total + jnp.where(used == first + k, piece, 0.0)
+    for i in range(ENTRIES):
+        total = total + jnp.where(used == i, product[i * IN_RANK : (i + 1) * IN_RANK], 0.0)
     total = total.astype(BF16)
     for n in range(N):
         out[n] = total
@@ -183,15 +174,12 @@
         out[t, :, QF:] = jnp.concatenate([fresh[n : n + LOCAL] for n in lows], 0).astype(BF16)
 
 
-def split_kernel(side, weight, out, arrived):
-    half = QF // 2
-    rows = pl.ds(aligned(side[0], half), half)
+def split_kernel(weight, out, arrived):
     copies = []
     for t in range(N):
-        high, low, x = t // (PAIR * SIDE), t // SIDE % PAIR, t % SIDE
-        source = weight.at[rows, pl.ds(t * OUT_PART, OUT_PART)]
+        source = weight.at[:, pl.ds(t * OUT_PART, OUT_PART)]
         copies.append(
-            pltpu.make_async_copy(source, out.at[high * SIDE + x, low], arrived.at[t])
+            pltpu.make_async_copy(source, out.at[t % SIDE, t // SIDE], arrived.at[t])
         )
     for copy in copies:
         copy.start()
@@ -276,11 +264,9 @@
                 by_row[low : low + N, half * HD : (half + 1) * HD] = piece
 
     attended = jnp.dot(swap, by_row[...], preferred_element_type=F32).astype(BF16)
-    for t in range(N):
-        high, low, x = t // (PAIR * SIDE), t // SIDE % PAIR, t % SIDE
-        ready[low, high * SIDE + x] = attended[t * MINE : (t + 1) * MINE]
+    ready[...] = attended.reshape(SIDE, SIDE, MINE, QF)
     copies = [
-        pltpu.make_async_copy(ready.at[n // SIDE % PAIR], out.at[n], sent.at[n]) for n in range(N)
+        pltpu.make_async_copy(ready.at[n // SIDE], out.at[n], sent.at[n]) for n in range(N)
     ]
     for copy in copies:
         copy.start()
@@ -305,7 +291,19 @@
         copy.wait()
 
 
-def shrink_out_kernel(place, attended, entry, maps, out):
+def base_out_kernel(
+    place, member, attended, entry, maps, source, partial, first, second, third, kept, columns, sems
+):
+    loads = []
+    for n, k in enumerate((1, 2, 3, 0)):
+        whose = lax.rem(member[0] + k, SIDE)
+        for j in range(SIDE):
+            rows = pl.ds(j * QF, QF)
+            copy = pltpu.make_async_copy(
+                source.at[j, whose], columns.at[n, rows], sems.at[n, j]
+            )
+            copy.start()
+            loads.append(copy)
     heads = attended[:, pl.ds(place[0], 1)].reshape(ALL_ROWS, QF)
     product = lax.dot_general(
         maps[...], heads, (((1,), (1,)), ((), ())), preferred_element_type=F32
@@ -316,40 +314,26 @@
         shrunk = shrunk + jnp.where(used == i, product[i * RANK : (i + 1) * RANK], 0.0)
     shrunk = shrunk.astype(BF16)
     for n in range(N):
-        out[n] = shrunk
-
-
-def base_out_kernel(side, member, attended, mine, others, passed, kept, columns, sems):
-    half = QF // 2
-    near = aligned(side[0], half)
-    loads = []
-    for which in range(PAIR):
-        whose = (1 - member[0], member[0])[which]
-        for j in range(RING):
-            for n, (source, low) in enumerate(((mine, near), (others, half - near))):
-                rows = pl.ds(pl.multiple_of(j * QF + low, half), half)
-                copy = pltpu.make_async_copy(
-                    source.at[j, whose], columns.at[which, rows], sems.at[which, j, n]
-                )
-                copy.start()
-                loads.append(copy)
-    for which, out in enumerate((passed, kept)):
+        partial[n] = shrunk
+    for n, out in enumerate((first, second, third, kept)):
         total = jnp.zeros((ALL_ROWS, OUT_PART), F32)
-        for j in range(0, RING, PAIR):
-            first = 2 * (which * RING + j)
-            for copy in loads[first : first + 2 * PAIR]:
+        for j in range(0, SIDE, 2):
+            for copy in loads[n * SIDE + j : n * SIDE + j + 2]:
                 copy.wait()
-            heads = [attended[:, n].reshape(ALL_ROWS, QF) for n in range(j, j + PAIR)]
-            part = jnp.concatenate(heads, axis=1)
-            rows = columns[which, j * QF : (j + PAIR) * QF]
-            total = total + jnp.dot(part, rows, preferred_element_type=F32)
+            heads = [attended[:, t].reshape(ALL_ROWS, QF) for t in (j, j + 1)]
+            rows = columns[n, j * QF : (j + 2) * QF]
+            total = total + jnp.dot(
+                jnp.concatenate(heads, axis=1), rows, preferred_element_type=F32
+            )
         out[...] = total.astype(out.dtype)
 
 
-def final_kernel(parts, entry, kept, arrived, up, out):
+def final_kernel(parts, entry, kept, first, second, third, up, out):
     shrunk = jnp.sum(parts[...].astype(F32), axis=0).astype(BF16).astype(F32)
     wide = expand(shrunk, entry[...])
-    total = kept[...] + arrived[...].astype(F32)
+    total = kept[...]
+    for arrived in (first, second, third):
+        total = total + arrived[...].astype(F32)
     total = total + low_rank_scale * contract(wide, up[...])
     for s in range(STEPS):
         lows = [t * MINE + s * LOCAL for t in range(N)]
@@ -363,9 +347,8 @@
 ):
     me = lax.axis_index("group")
     part = lax.axis_index(TP)
-    place = lax.axis_index(AROUND)[None]
-    member = lax.axis_index("lo")[None]
-    side = (me % 2)[None]
+    place = lax.axis_index("x")[None]
+    member = lax.axis_index("y")[None]
 
     with jax.named_scope("gather_in_maps"):
         packed = pl.pallas_call(
@@ -419,16 +402,15 @@
         w_out, packed = lax.optimization_barrier((w_out, packed))
         half = pl.pallas_call(
             split_kernel,
-            out_shape=jax.ShapeDtypeStruct((RING, PAIR, QF // 2, OUT_PART), BF16),
-            in_specs=[smem(), hbm()],
+            out_shape=jax.ShapeDtypeStruct((SIDE, SIDE, QF, OUT_PART), BF16),
+            in_specs=[hbm()],
             out_specs=vmem(),
             scratch_shapes=[pltpu.SemaphoreType.DMA((N,))],
-            compiler_params=params(56),
+            compiler_params=params(60),
             cost_estimate=cost(0, 8 << 20),
             name="split",
-        )(side, w_out)
-        mine = lax.all_to_all(half, AROUND, split_axis=0, concat_axis=0, tiled=True)
-        others = lax.ppermute(mine, "group", [(i, i ^ 1) for i in range(N)])
+        )(w_out)
+        mine = lax.all_to_all(half, "x", split_axis=0, concat_axis=0, tiled=True)
 
     with jax.named_scope("base_projections"):
         tokens = hidden.reshape(ALL_ROWS, -1)
@@ -440,7 +422,7 @@
             ],
             axis=1,
         )
-        tokens_part = lax.dynamic_slice_in_dim(tokens, part * IN_PART, IN_PART, 1)
+        tokens_part = lax.dynamic_slice_in_dim(tokens, part * IN_PART, IN_PART, 1).T
 
     with jax.named_scope("gather_out_maps"):
         out_pool = jnp.concatenate([pool_a_o, pool_b_o], axis=2)
@@ -459,7 +441,7 @@
                 pltpu.VMEM((ENTRIES * IN_RANK, IN_PART), BF16),
                 pltpu.SemaphoreType.DMA((ENTRIES,)),
             ],
-            compiler_params=params(56),
+            compiler_params=params(60),
             cost_estimate=cost(2 * ENTRIES * IN_RANK * IN_PART * ALL_ROWS, 2 << 20),
             name="shrink",
         )(index, pool, slot_a_in, tokens_part, by_step)
@@ -495,19 +477,19 @@
         received = lax.all_to_all(projected, TP, split_axis=0, concat_axis=0, tiled=True)
         payload = pl.pallas_call(
             attend_kernel,
-            out_shape=jax.ShapeDtypeStruct((N, RING, MINE, QF), BF16),
+            out_shape=jax.ShapeDtypeStruct((N, SIDE, MINE, QF), BF16),
             in_specs=[smem(), vmem(), hbm(), hbm()],
             out_specs=hbm(),
             scratch_shapes=[
                 pltpu.VMEM((LOCAL, LENGTH, KW), BF16),
                 pltpu.VMEM((LOCAL, LENGTH, KW), BF16),
                 pltpu.VMEM((N * MINE, QF), BF16),
-                pltpu.VMEM((PAIR, RING, MINE, QF), BF16),
+                pltpu.VMEM((SIDE, SIDE, MINE, QF), BF16),
                 pltpu.SemaphoreType.DMA((LOCAL,)),
                 pltpu.SemaphoreType.DMA((LOCAL,)),
                 pltpu.SemaphoreType.DMA((N,)),
             ],
-            compiler_params=params(56),
+            compiler_params=params(60),
             cost_estimate=cost(4 * LOCAL * 64 * KW * LENGTH, 12 << 20),
             name="attend",
         )(lengths, received, key_cache, value_cache)
@@ -529,48 +511,38 @@
         )(picks, slot_a_o, slot_b_o, out_pool)
 
     with jax.named_scope("output"):
-        partial_out = pl.pallas_call(
-            shrink_out_kernel,
-            out_shape=jax.ShapeDtypeStruct((N, RANK, ALL_ROWS), BF16),
-            in_specs=[smem()] + [vmem()] * 3,
-            out_specs=vmem(),
-            compiler_params=params(16),
-            cost_estimate=cost(2 * 400 * QF * ALL_ROWS, 1 << 20),
-            name="shrink_out",
-        )(place, gathered, by_owner, maps)
-        partial_out, member = lax.optimization_barrier((partial_out, member))
+        block = (ALL_ROWS, OUT_PART)
+        partial_out, *passed, kept_out = pl.pallas_call(
+            base_out_kernel,
+            out_shape=[jax.ShapeDtypeStruct((N, RANK, ALL_ROWS), BF16)]
+            + [jax.ShapeDtypeStruct(block, BF16)] * 3
+            + [jax.ShapeDtypeStruct(block, F32)],
+            in_specs=[smem()] * 2 + [vmem()] * 3 + [hbm()],
+            out_specs=[vmem()] * 5,
+            scratch_shapes=[
+                pltpu.VMEM((SIDE, WIDE, OUT_PART), BF16),
+                pltpu.SemaphoreType.DMA((SIDE, SIDE)),
+            ],
+            compiler_params=params(24),
+            cost_estimate=cost(2 * ALL_ROWS * FEATURES * OUT_PART, 5 << 20),
+            name="base_out",
+        )(place, member, gathered, by_owner, maps, mine)
         partials_out = lax.all_to_all(partial_out, TP, split_axis=0, concat_axis=0, tiled=True)
-
-        passed, kept_out = pl.pallas_call(
-            base_out_kernel,
-            out_shape=[
-                jax.ShapeDtypeStruct((ALL_ROWS, OUT_PART), BF16),
-                jax.ShapeDtypeStruct((ALL_ROWS, OUT_PART), F32),
-            ],
-            in_specs=[smem()] * 2 + [vmem()] + [hbm()] * 2,
-            out_specs=[vmem()] * 2,
-            scratch_shapes=[
-                pltpu.VMEM((PAIR, RING * QF, OUT_PART), BF16),
-                pltpu.SemaphoreType.DMA((PAIR, RING, 2)),
-            ],
-            compiler_params=params(24),
-            cost_estimate=cost(4 * ALL_ROWS * WIDE * OUT_PART, 5 << 20),
-            name="base_out",
-        )(side, member, gathered, mine, others)
-        passed = lax.ppermute(passed, "lo", [(0, 1), (1, 0)])
+        turns = [[(i, (i + k) % SIDE) for i in range(SIDE)] for k in range(1, SIDE)]
+        passed = [lax.ppermute(p, "y", turn) for p, turn in zip(passed, turns)]
         return pl.pallas_call(
             final_kernel,
             out_shape=jax.ShapeDtypeStruct((STEPS, ROWS, OUT_PART), BF16),
-            in_specs=[vmem()] * 5,
+            in_specs=[vmem()] * 7,
             out_specs=vmem(),
             compiler_params=params(16),
             cost_estimate=cost(2 * 400 * OUT_PART * ALL_ROWS, 1 << 20),
             name="final",
-        )(partials_out, by_owner, kept_out, passed, up_o)
+        )(partials_out, by_owner, kept_out, *passed, up_o)
 
 
 def solution(mesh):
-    grid = jax.sharding.Mesh(mesh.devices.reshape(N, SIDE // PAIR, PAIR, SIDE), ("group",) + TP)
+    grid = jax.sharding.Mesh(mesh.devices.reshape(N, SIDE, SIDE), ("group",) + TP)
     pooled = P("group", None, TP)
     cached = P(("group",) + TP, None, None)
     placed = (

time: 169 us -> 166 us (0.982)
  waiting for transfers between devices: 65.2 us -> 59.2 us
    all_gather x1, waiting for transfers between devices: 31.9 us -> 12.3 us  [shard(): pool = lax.all_gather(packed, 'group')]
    all_to_all x1, waiting for transfers between devices: 14 us -> 33.4 us  [shard(): mine = lax.all_to_all(half, 'x', split_axis=0, concat_axis=0, tiled=True)]
    all_to_all x1, waiting for transfers between devices: 11.5 us -> 5.72 us  [shard(): lax.all_to_all(payload, TP, split_axis=0, concat_axis=0, tiled=True)]
    ppermute x2 -> x3, starting transfers between devices: 0.14 us -> 3.5 us  [shard(): passed = [lax.ppermute(p, 'y', turn) for p, turn in zip(passed, turns)]]
    all_to_all x1, starting transfers between devices: 7.07 us -> 5 us  [shard(): mine = lax.all_to_all(half, 'x', split_axis=0, concat_axis=0, tiled=True)]
    pallas_call x4 -> x3, Pallas kernels: 15.6 us -> 17.2 us  [the longest x1 8.66 us: shard(): pl.pallas_call(attend_kernel, out_shape=jax.ShapeDtypeStruct((N, SIDE, MI...]
  transfers between devices with their start and end apart: 7 -> 8, of which waited for: 4 -> 4; matrix products, arithmetic and copies ran while one was open for 9% -> 10% of each run, Pallas kernels for 13% -> 13%
where the time goes in v6:
time: 166 us; the launch traced here: 164 us
  waiting for transfers between devices  59.2 us (36%)
  Pallas kernels  29 us (17%)
  blocking collectives  23.8 us (14%)
  starting transfers between devices  19.2 us (12%)
  between operations  14.4 us (9%)
  matrix products  10.3 us (6%)
  local copies, waits for them, and re-layouts  4.96 us (3%)
  other arithmetic  3.47 us (2%)
    all_to_all x1, waiting for transfers between devices, shard(): mine = lax.all_to_all(half, 'x', split_axis=0, concat_axis=0, tiled=True)  33.4 us
    all_gather x1, waiting for transfers between devices, shard(): pool = lax.all_gather(packed, 'group')  12.3 us
    all_to_all x1, blocking collectives, shard(): lax.all_to_all(partial_out, TP, split_axis=0, concat_axis=0, tiled=True)  12.1 us
    all_to_all x1, blocking collectives, shard(): lax.all_to_all(projected, TP, split_axis=0, concat_axis=0, tiled=True)  11.6 us
    pallas_call x1, Pallas kernels, shard(): pl.pallas_call(attend_kernel, out_shape=jax.ShapeDtypeStruct((N, SIDE, MI...  8.66 us
    all_to_all x1, waiting for transfers between devices, shard(): lax.all_to_all(partial_in, TP, split_axis=0, concat_axis=0, tiled=True)  7.72 us
    all_to_all x1, starting transfers between devices, shard(): lax.all_to_all(partial_in, TP, split_axis=0, concat_axis=0, tiled=True)  6.93 us
    all_to_all x1, waiting for transfers between devices, shard(): lax.all_to_all(payload, TP, split_axis=0, concat_axis=0, tiled=True)  5.72 us
  transfers between devices with their start and end apart: 8, of which 4 were waited for; matrix products, arithmetic and copies ran while one was open for 10% of the time, Pallas kernels for 13%

profile of v6, /device:TPU:32, one launch (start us, length us, event | category | flops | bytes accessed | tf_op | source)
XLA Modules:
  0.0 164.4 jit_solution(17227579710024774323)
XLA Ops:
  6.5 2.3 %pack.1 = bf16[704,512]{1,0:T(8,128)(2,1)} custom-call(bf16[12,48,512]{2,1,0:T(8,128)(2,1)} %maps_in.1, bf16[12,16,256]{2,1,0:T(8,128)(2,1)} %maps_q.1, bf16[12,16,32]{2,1,0:T(8,128)(2,1)} %maps_k.1, bf16[12,16,32]{2,1,0:T(8,128)(2,1)} %maps_v.1), custom_call_target="tpu_custom_call" | custom-call | bytes 2097152 | tf_op jit(solution)/shard_map/gather_in_maps/pack/pallas_call | solution.py:354
  8.8 4.3 %split.1 = bf16[4,4,256,512]{3,2,1,0:T(8,128)(2,1)} custom-call(bf16[256,8192]{1,0:T(8,128)(2,1)} %weight), custom_call_target="tpu_custom_call" | custom-call | bytes 8388608 | tf_op jit(solution)/shard_map/columns_of_w_out/split/pallas_call | solution.py:403
  13.2 5.0 %all-to-all-start = ((bf16[4,4,256,512]{3,2,1,0:T(8,128)(2,1)}), bf16[4,4,256,512]{3,2,1,0:T(8,128)(2,1)}, u32[]{:S(2)}, u32[]{:S(2)}) async-start(bf16[4,4,256,512]{3,2,1,0:T(8,128)(2,1)} %split.1), calls=%async_computation | async-start | bytes 8388608 | tf_op jit(solution)/shard_map/columns_of_w_out/all_to_all | solution.py:413
  18.3 0.2 select_reduce_fusion
  18.8 1.0 constant_dynamic-slice_fusion.1
  19.7 0.8 copy.48
  20.7 0.7 slice_reduce_fusion
  22.0 0.7 pad_add_fusion.1.index
  22.7 4.2 %fusion.5 = f32[256,32]{1,0:T(8,128)S(1)} fusion(bf16[256,8192]{1,0:T(8,128)(2,1)} %bitcast.22, bf16[8192,32]{0,1:T(8,128)(2,1)S(1)} %copy-done), kind=kOutput, calls=%fused_computation.27 | convolution fusion | flops 134217728 | bytes 4751360 | tf_op jit(solution)/shard_map/base_projections/dot_general | solution.py:420
  26.9 1.2 fusion.6
  28.3 0.8 pad_maximum_fusion
  29.1 4.9 %fusion.4.base_q = f32[256,256]{1,0:T(8,128)S(1)} fusion(bf16[256,8192]{1,0:T(8,128)(2,1)} %bitcast.23, bf16[8192,256]{1,0:T(8,128)(2,1)} %param.25), kind=kOutput, calls=%fused_computation.26 | convolution fusion | flops 1073741824 | bytes 8650752 | tf_op jit(solution)/shard_map/base_projections/dot_general | solution.py:417
  34.0 33.4 %all-to-all-done.source = bf16[4,4,256,512]{3,2,1,0:T(8,128)(2,1)} async-done(((bf16[4,4,256,512]{3,2,1,0:T(8,128)(2,1)}), bf16[4,4,256,512]{3,2,1,0:T(8,128)(2,1)}, u32[]{:S(2)}, u32[]{:S(2)}) %all-to-all-start) | async-done | bytes 4194336 | tf_op jit(solution)/shard_map/columns_of_w_out/all_to_all | solution.py:413
  67.7 0.7 fusion
  68.4 12.3 %all-gather.5.cloned.1.call-done = bf16[11264,512]{1,0:T(8,128)(2,1)} async-done(((bf16[704,512]{1,0:T(8,128)(2,1)}), bf16[11264,512]{1,0:T(8,128)(2,1)}) %all-gather.5.cloned.1.call-update) | async-done | bytes 11534352 | tf_op jit(solution)/shard_map/gather_in_maps/all_gather | solution.py:370
  80.7 3.7 %shrink.1 = bf16[16,48,256]{2,1,0:T(8,128)(2,1)} custom-call(s32[25]{0:T(128)} %pad_add_fusion.1.index, bf16[16,704,512]{2,1,0:T(8,128)(2,1)} %bitcast.17, bf16[13,48,512]{2,1,0:T(8,128)(2,1)} %slot.1, bf16[512,256]{1,0:T(8,128)(2,1)} %bitcast.19, s32[1,256]{1,0:T(1,128)} %bitcast.15), custom_call_target="tpu_custom_call" | custom-call | flops 314572800 | bytes 2097152 | tf_op jit(solution)/shard_map/shrink/shrink/pallas_call | solution.py:435
  84.5 6.9 %all-to-all-start.1 = ((bf16[16,48,256]{2,1,0:T(8,128)(2,1)}), bf16[16,48,256]{2,1,0:T(8,128)(2,1)S(1)}, u32[]{:S(2)}, u32[]{:S(2)}) async-start(bf16[16,48,256]{2,1,0:T(8,128)(2,1)} %shrink.1), calls=%async_computation.1 | async-start | bytes 786432 | tf_op jit(solution)/shard_map/shrink/all_to_all | solution.py:450
  91.6 0.1 copy.43.block
  91.8 2.4 %pick_up.1 = (bf16[400,256]{1,0:T(8,128)(2,1)S(1)}, bf16[400,512]{1,0:T(8,128)(2,1)S(1)}) custom-call(s32[25]{0:T(128)S(1)} %copy-done.8, bf16[16,704,512]{2,1,0:T(8,128)(2,1)} %bitcast.18, bf16[13,16,256]{2,1,0:T(8,128)(2,1)S(1)} %copy-done.3, bf16[13,16,32]{2,1,0:T(8,128)(2,1)S(1)} %copy-done.5, bf16[13,16,32]{2,1,0:T(8,128)(2,1)S(1)} %copy-done.6), custom_call_target="tpu_custom_call" | custom-call | bytes 2097152 | tf_op jit(solution)/shard_map/project/pick_up/pallas_call | solution.py:453
  94.2 7.7 %all-to-all-done.1.parts = bf16[16,48,256]{2,1,0:T(8,128)(2,1)S(1)} async-done(((bf16[16,48,256]{2,1,0:T(8,128)(2,1)}), bf16[16,48,256]{2,1,0:T(8,128)(2,1)S(1)}, u32[]{:S(2)}, u32[]{:S(2)}) %all-to-all-start.1) | async-done | bytes 393248 | tf_op jit(solution)/shard_map/shrink/all_to_all | solution.py:450
  101.9 0.7 project.1
  102.6 11.6 %all_to_all.25.received = bf16[16,16,320]{2,1,0:T(8,128)(2,1)} all-to-all(bf16[16,16,320]{2,1,0:T(8,128)(2,1)S(1)} %project.1), channel_id=1, replica_groups=mesh['group'=16,'y'=4,'x'=4] {'y','x'}, dimensions={0} | all-to-all | bytes 327680 | tf_op jit(solution)/shard_map/attend/all_to_all | solution.py:477
  114.3 8.7 %attend.1 = bf16[16,4,16,256]{3,2,1,0:T(8,128)(2,1)} custom-call(s32[8]{0:T(128)} %lengths.1, bf16[16,16,320]{2,1,0:T(8,128)(2,1)} %all_to_all.25.received, bf16[8,512,512]{2,1,0:T(8,128)(2,1)} %keys.1, bf16[8,512,512]{2,1,0:T(8,128)(2,1)} %values.1), custom_call_target="tpu_custom_call" | custom-call | flops 536870912 | bytes 12582912 | tf_op jit(solution)/shard_map/attend/attend/pallas_call | solution.py:478
  122.9 3.8 %all-to-all-start.3 = ((bf16[16,4,16,256]{3,2,1,0:T(8,128)(2,1)}), bf16[16,4,16,256]{3,2,1,0:T(8,128)(2,1)S(1)}, u32[]{:S(2)}, u32[]{:S(2)}) async-start(bf16[16,4,16,256]{3,2,1,0:T(8,128)(2,1)} %attend.1), calls=%async_computation.3 | async-start | bytes 1048576 | tf_op jit(solution)/shard_map/attend/all_to_all | solution.py:496
  127.0 2.3 %copy-done.1 = bf16[192,16,768]{2,1,0:T(8,128)(2,1)S(1)} copy-done((bf16[192,16,768]{2,1,0:T(8,128)(2,1)S(1)}, bf16[192,16,768]{2,1,0:T(8,128)(2,1)}, u32[]{:S(2)}) %copy-start.1) | copy-done | bytes 4718616
  129.3 1.6 pick.1
  130.9 5.7 %all-to-all-done.3.attended = bf16[16,4,16,256]{3,2,1,0:T(8,128)(2,1)S(1)} async-done(((bf16[16,4,16,256]{3,2,1,0:T(8,128)(2,1)}), bf16[16,4,16,256]{3,2,1,0:T(8,128)(2,1)S(1)}, u32[]{:S(2)}, u32[]{:S(2)}) %all-to-all-start.3) | async-done | bytes 524320 | tf_op jit(solution)/shard_map/attend/all_to_all | solution.py:496
  136.6 4.2 %base_out.1 = (bf16[16,16,256]{2,1,0:T(8,128)(2,1)S(1)}, bf16[256,512]{1,0:T(8,128)(2,1)S(1)}, bf16[256,512]{1,0:T(8,128)(2,1)S(1)}, bf16[256,512]{1,0:T(8,128)(2,1)S(1)}, f32[256,512]{1,0:T(8,128)S(1)}) custom-call(s32[1]{0:T(128)} %bitcast.place, s32[1]{0:T(128)} %bitcast.1.member, bf16[16,4,16,256]{3,2,1,0:T(8,128)(2,1)S(1)} %all-to-all-done.3.attended, ...), custom_call_target="tpu_custom_call" | custom-call | flops 1073741824 | bytes 5242880 | tf_op jit(solution)/shard_map/output/base_out/pallas_call | solution.py:515
  140.9 2.3 %collective-permute-start.1 = (bf16[256,512]{1,0:T(8,128)(2,1)S(1)}, bf16[256,512]{1,0:T(8,128)(2,1)S(1)}, u32[]{:S(2)}, u32[]{:S(2)}) collective-permute-start(bf16[256,512]{1,0:T(8,128)(2,1)S(1)} %get-tuple-element.40), channel_id=1, source_target_pairs={{0,8},{4,12},{8,0},{12,4},{1,9},{5,13},{9,1},{13,5},{2,10},{6,14},... | collective-permute-start | bytes 786440 | tf_op jit(solution)/shard_map/output/ppermute | solution.py:532
  143.2 1.1 collective-permute-start.2
  144.3 12.1 %all_to_all.26.parts = bf16[16,16,256]{2,1,0:T(8,128)(2,1)S(1)} all-to-all(bf16[16,16,256]{2,1,0:T(8,128)(2,1)S(1)} %get-tuple-element.37), channel_id=1, replica_groups=mesh['group'=16,'y'=4,'x'=4] {'y','x'}, dimensions={0} | all-to-all | bytes 262144 | tf_op jit(solution)/shard_map/output/all_to_all | solution.py:530
  156.5 1.1 final.1
  (60 shorter events, 1.3 us)
Async XLA Ops:
  6.5 16.2 %copy-start = (bf16[8192,32]{0,1:T(8,128)(2,1)S(1)}, bf16[8192,32]{0,1:T(8,128)(2,1)}, u32[]{:S(2)}) copy-start(bf16[8192,32]{0,1:T(8,128)(2,1)} %param.26) | copy-start | bytes 1572868
  6.5 74.2 %all-gather.5.cloned.1.call-start = ((), (), s32[]{:S(2)}) async-start(), calls=%async_computation.5 | async-start | bytes 12255232 | tf_op jit(solution)/shard_map/gather_in_maps/all_gather | solution.py:370
  13.2 5.1 %copy-start.12 = (s32[2,192]{1,0:T(2,128)S(1)}, s32[2,192]{1,0:T(2,128)}, u32[]{:S(2)}) copy-start(s32[2,192]{1,0:T(2,128)} %param.34) | copy-start | bytes 4612
  13.2 5.1 %copy-start.13 = (s32[192]{0:T(256)S(1)}, s32[192]{0:T(256)}, u32[]{:S(2)}) copy-start(s32[192]{0:T(256)} %param.35) | copy-start | bytes 2308
  13.2 7.4 %copy-start.15 = (s32[2,192]{1,0:T(2,128)S(1)}, s32[2,192]{1,0:T(2,128)}, u32[]{:S(2)}) copy-start(s32[2,192]{1,0:T(2,128)} %param.33) | copy-start | bytes 4612
  13.2 54.1 %all-to-all-start = ((bf16[4,4,256,512]{3,2,1,0:T(8,128)(2,1)}), bf16[4,4,256,512]{3,2,1,0:T(8,128)(2,1)}, u32[]{:S(2)}, u32[]{:S(2)}) async-start(bf16[4,4,256,512]{3,2,1,0:T(8,128)(2,1)} %split.1), calls=%async_computation | async-start | bytes 8388608 | tf_op jit(solution)/shard_map/columns_of_w_out/all_to_all | solution.py:413
  18.2 8.7 %copy-start.16 = (bf16[8192,32]{0,1:T(8,128)(2,1)S(1)}, bf16[8192,32]{0,1:T(8,128)(2,1)}, u32[]{:S(2)}) copy-start(bf16[8192,32]{0,1:T(8,128)(2,1)} %param.27) | copy-start | bytes 1572868
  18.2 108.7 %all-gather.7.cloned.1.call-start = ((), (), s32[]{:S(2)}) async-start(), calls=%async_computation.6 | async-start | bytes 5013504 | tf_op jit(solution)/shard_map/gather_out_maps/all_gather | solution.py:432
  22.0 4.9 %copy-start.11 = (bf16[2,128,8192]{2,1,0:T(8,128)(2,1)S(1)}, bf16[2,128,8192]{2,1,0:T(8,128)(2,1)}, u32[]{:S(2)}) copy-start(bf16[2,128,8192]{2,1,0:T(8,128)(2,1)} %param.24) | copy-start | bytes 12582916
  22.7 5.6 %copy-start.9 = (bf16[12,16,512]{2,1,0:T(8,128)(2,1)S(1)}, bf16[12,16,512]{2,1,0:T(8,128)(2,1)}, u32[]{:S(2)}) copy-start(bf16[12,16,512]{2,1,0:T(8,128)(2,1)} %param.41) | copy-start | bytes 589828
  22.7 5.6 %copy-start.10 = (bf16[12,16,256]{2,1,0:T(8,128)(2,1)S(1)}, bf16[12,16,256]{2,1,0:T(8,128)(2,1)}, u32[]{:S(2)}) copy-start(bf16[12,16,256]{2,1,0:T(8,128)(2,1)} %param.40) | copy-start | bytes 294916
  29.0 38.7 %copy-start.14 = (s32[2,128]{1,0:T(2,128)S(1)}, s32[2,128]{1,0:T(2,128)}, u32[]{:S(2)}) copy-start(s32[2,128]{1,0:T(2,128)} %param.32) | copy-start | bytes 3076
  80.7 10.8 %copy-start.7 = (s32[2,128]{1,0:T(2,128)S(1)}, s32[2,128]{1,0:T(2,128)}, u32[]{:S(2)}) copy-start(s32[2,128]{1,0:T(2,128)} %fusion) | copy-start | bytes 3076
  80.7 11.0 %copy-start.3 = (bf16[13,16,256]{2,1,0:T(8,128)(2,1)S(1)}, bf16[13,16,256]{2,1,0:T(8,128)(2,1)}, u32[]{:S(2)}) copy-start(bf16[13,16,256]{2,1,0:T(8,128)(2,1)} %slot_q.1) | copy-start | bytes 319492
  80.7 11.0 %copy-start.5 = (bf16[13,16,32]{2,1,0:T(8,128)(2,1)S(1)}, bf16[13,16,32]{2,1,0:T(8,128)(2,1)}, u32[]{:S(2)}) copy-start(bf16[13,16,32]{2,1,0:T(8,128)(2,1)} %slot_k.1) | copy-start | bytes 39940
  80.7 11.0 %copy-start.6 = (bf16[13,16,32]{2,1,0:T(8,128)(2,1)S(1)}, bf16[13,16,32]{2,1,0:T(8,128)(2,1)}, u32[]{:S(2)}) copy-start(bf16[13,16,32]{2,1,0:T(8,128)(2,1)} %slot_v.1) | copy-start | bytes 39940
  80.7 11.1 %copy-start.8 = (s32[25]{0:T(128)S(1)}, s32[25]{0:T(128)}, u32[]{:S(2)}) copy-start(s32[25]{0:T(128)} %pad_add_fusion.1.index) | copy-start | bytes 304
  84.5 17.4 %all-to-all-start.1 = ((bf16[16,48,256]{2,1,0:T(8,128)(2,1)}), bf16[16,48,256]{2,1,0:T(8,128)(2,1)S(1)}, u32[]{:S(2)}, u32[]{:S(2)}) async-start(bf16[16,48,256]{2,1,0:T(8,128)(2,1)} %shrink.1), calls=%async_computation.1 | async-start | bytes 786432 | tf_op jit(solution)/shard_map/shrink/all_to_all | solution.py:450
  114.3 12.7 %copy-start.2 = (bf16[13,16,512]{2,1,0:T(8,128)(2,1)S(1)}, bf16[13,16,512]{2,1,0:T(8,128)(2,1)}, u32[]{:S(2)}) copy-start(bf16[13,16,512]{2,1,0:T(8,128)(2,1)} %slot_up.1) | copy-start | bytes 638980
  114.3 12.7 %copy-start.4 = (bf16[13,16,256]{2,1,0:T(8,128)(2,1)S(1)}, bf16[13,16,256]{2,1,0:T(8,128)(2,1)}, u32[]{:S(2)}) copy-start(bf16[13,16,256]{2,1,0:T(8,128)(2,1)} %slot_in.1) | copy-start | bytes 319492
  122.9 13.7 %all-to-all-start.3 = ((bf16[16,4,16,256]{3,2,1,0:T(8,128)(2,1)}), bf16[16,4,16,256]{3,2,1,0:T(8,128)(2,1)S(1)}, u32[]{:S(2)}, u32[]{:S(2)}) async-start(bf16[16,4,16,256]{3,2,1,0:T(8,128)(2,1)} %attend.1), calls=%async_computation.3 | async-start | bytes 1048576 | tf_op jit(solution)/shard_map/attend/all_to_all | solution.py:496
  126.9 2.3 %copy-start.1 = (bf16[192,16,768]{2,1,0:T(8,128)(2,1)S(1)}, bf16[192,16,768]{2,1,0:T(8,128)(2,1)}, u32[]{:S(2)}) copy-start(bf16[192,16,768]{2,1,0:T(8,128)(2,1)} %all-gather.7.cloned.1.call-done.pool) | copy-start | bytes 14155780
  140.8 15.7 %collective-permute-start = (bf16[256,512]{1,0:T(8,128)(2,1)S(1)}, bf16[256,512]{1,0:T(8,128)(2,1)S(1)}, u32[]{:S(2)}, u32[]{:S(2)}) collective-permute-start(bf16[256,512]{1,0:T(8,128)(2,1)S(1)} %get-tuple-element.39), channel_id=1, source_target_pairs={{0,4},{4,8},{8,12},{12,0},{1,5},{5,9},{9,13},{13,1},{2,6},{6,10},{... | collective-permute-start | bytes 786440 | tf_op jit(solution)/shard_map/output/ppermute | solution.py:532
  140.9 15.6 %collective-permute-start.1 = (bf16[256,512]{1,0:T(8,128)(2,1)S(1)}, bf16[256,512]{1,0:T(8,128)(2,1)S(1)}, u32[]{:S(2)}, u32[]{:S(2)}) collective-permute-start(bf16[256,512]{1,0:T(8,128)(2,1)S(1)} %get-tuple-element.40), channel_id=1, source_target_pairs={{0,8},{4,12},{8,0},{12,4},{1,9},{5,13},{9,1},{13,5},{2,10},{6,14},... | collective-permute-start | bytes 786440 | tf_op jit(solution)/shard_map/output/ppermute | solution.py:532
  143.2 13.3 %collective-permute-start.2 = (bf16[256,512]{1,0:T(8,128)(2,1)S(1)}, bf16[256,512]{1,0:T(8,128)(2,1)S(1)}, u32[]{:S(2)}, u32[]{:S(2)}) collective-permute-start(bf16[256,512]{1,0:T(8,128)(2,1)S(1)} %get-tuple-element.41), channel_id=1, source_target_pairs={{0,12},{4,0},{8,4},{12,8},{1,13},{5,1},{9,5},{13,9},{2,14},{6,2},{... | collective-permute-start | bytes 786440 | tf_op jit(solution)/shard_map/output/ppermute | solution.py:532
Sparse Core Ops, SparseCore 0:
  9.2 71.4 all-gather.4
  82.5 42.6 all-gather.6

commit v7 on v6

--- a/solution.py
+++ b/solution.py
@@ -33,7 +33,6 @@
 IN_PART = 512
 OUT_PART = 512
 FEATURES = QH * HD
-WIDE = SIDE * QF
 QKV = QF + 2 * KF
 TP = ("y", "x")
 LENGTH = 512
@@ -292,18 +291,8 @@
 
 
 def base_out_kernel(
-    place, member, attended, entry, maps, source, partial, first, second, third, kept, columns, sems
+    place, member, attended, entry, maps, source, partial, first, second, third, kept
 ):
-    loads = []
-    for n, k in enumerate((1, 2, 3, 0)):
-        whose = lax.rem(member[0] + k, SIDE)
-        for j in range(SIDE):
-            rows = pl.ds(j * QF, QF)
-            copy = pltpu.make_async_copy(
-                source.at[j, whose], columns.at[n, rows], sems.at[n, j]
-            )
-            copy.start()
-            loads.append(copy)
     heads = attended[:, pl.ds(place[0], 1)].reshape(ALL_ROWS, QF)
     product = lax.dot_general(
         maps[...], heads, (((1,), (1,)), ((), ())), preferred_element_type=F32
@@ -315,15 +304,14 @@
     shrunk = shrunk.astype(BF16)
     for n in range(N):
         partial[n] = shrunk
-    for n, out in enumerate((first, second, third, kept)):
+    heads = [attended[:, t].reshape(ALL_ROWS, QF) for t in range(SIDE)]
+    for k, out in ((1, first), (2, second), (3, third), (0, kept)):
+        whose = lax.rem(member[0] + k, SIDE)
         total = jnp.zeros((ALL_ROWS, OUT_PART), F32)
         for j in range(0, SIDE, 2):
-            for copy in loads[n * SIDE + j : n * SIDE + j + 2]:
-                copy.wait()
-            heads = [attended[:, t].reshape(ALL_ROWS, QF) for t in (j, j + 1)]
-            rows = columns[n, j * QF : (j + 2) * QF]
+            rows = jnp.concatenate([source[t, whose] for t in (j, j + 1)], axis=0)
             total = total + jnp.dot(
-                jnp.concatenate(heads, axis=1), rows, preferred_element_type=F32
+                jnp.concatenate(heads[j : j + 2], axis=1), rows, preferred_element_type=F32
             )
         out[...] = total.astype(out.dtype)
 
@@ -517,12 +505,8 @@
             out_shape=[jax.ShapeDtypeStruct((N, RANK, ALL_ROWS), BF16)]
             + [jax.ShapeDtypeStruct(block, BF16)] * 3
             + [jax.ShapeDtypeStruct(block, F32)],
-            in_specs=[smem()] * 2 + [vmem()] * 3 + [hbm()],
+            in_specs=[smem()] * 2 + [vmem()] * 4,
             out_specs=[vmem()] * 5,
-            scratch_shapes=[
-                pltpu.VMEM((SIDE, WIDE, OUT_PART), BF16),
-                pltpu.SemaphoreType.DMA((SIDE, SIDE)),
-            ],
             compiler_params=params(24),
             cost_estimate=cost(2 * ALL_ROWS * FEATURES * OUT_PART, 5 << 20),
             name="base_out",

time: 166 us -> 166 us (level)
  no operation moved by 1% of the time
where the time goes in v7:
time: 166 us; the launch traced here: 164 us
  waiting for transfers between devices  59.2 us (36%)
  Pallas kernels  28.3 us (17%)
  blocking collectives  23.8 us (14%)
  starting transfers between devices  19.2 us (12%)
  between operations  14.4 us (9%)
  matrix products  10.3 us (6%)
  local copies, waits for them, and re-layouts  4.96 us (3%)
  other arithmetic  3.47 us (2%)
    all_to_all x1, waiting for transfers between devices, shard(): mine = lax.all_to_all(half, 'x', split_axis=0, concat_axis=0, tiled=True)  33.4 us
    all_gather x1, waiting for transfers between devices, shard(): pool = lax.all_gather(packed, 'group')  12.3 us
    all_to_all x1, blocking collectives, shard(): lax.all_to_all(partial_out, TP, split_axis=0, concat_axis=0, tiled=True)  12.1 us
    all_to_all x1, blocking collectives, shard(): lax.all_to_all(projected, TP, split_axis=0, concat_axis=0, tiled=True)  11.6 us
    pallas_call x1, Pallas kernels, shard(): pl.pallas_call(attend_kernel, out_shape=jax.ShapeDtypeStruct((N, SIDE, MI...  8.66 us
    all_to_all x1, waiting for transfers between devices, shard(): lax.all_to_all(partial_in, TP, split_axis=0, concat_axis=0, tiled=True)  7.72 us
    all_to_all x1, starting transfers between devices, shard(): lax.all_to_all(partial_in, TP, split_axis=0, concat_axis=0, tiled=True)  6.93 us
    all_to_all x1, waiting for transfers between devices, shard(): lax.all_to_all(payload, TP, split_axis=0, concat_axis=0, tiled=True)  5.72 us
  transfers between devices with their start and end apart: 8, of which 4 were waited for; matrix products, arithmetic and copies ran while one was open for 10% of the time, Pallas kernels for 13%

profile of v7, /device:TPU:32, one launch (start us, length us, event | category | flops | bytes accessed | tf_op | source)
XLA Modules:
  0.0 163.6 jit_solution(6911065308392305798)
XLA Ops:
  6.5 2.3 %pack.1 = bf16[704,512]{1,0:T(8,128)(2,1)} custom-call(bf16[12,48,512]{2,1,0:T(8,128)(2,1)} %maps_in.1, bf16[12,16,256]{2,1,0:T(8,128)(2,1)} %maps_q.1, bf16[12,16,32]{2,1,0:T(8,128)(2,1)} %maps_k.1, bf16[12,16,32]{2,1,0:T(8,128)(2,1)} %maps_v.1), custom_call_target="tpu_custom_call" | custom-call | bytes 2097152 | tf_op jit(solution)/shard_map/gather_in_maps/pack/pallas_call | solution.py:342
  8.8 4.3 %split.1 = bf16[4,4,256,512]{3,2,1,0:T(8,128)(2,1)} custom-call(bf16[256,8192]{1,0:T(8,128)(2,1)} %weight), custom_call_target="tpu_custom_call" | custom-call | bytes 8388608 | tf_op jit(solution)/shard_map/columns_of_w_out/split/pallas_call | solution.py:391
  13.2 5.0 %all-to-all-start = ((bf16[4,4,256,512]{3,2,1,0:T(8,128)(2,1)}), bf16[4,4,256,512]{3,2,1,0:T(8,128)(2,1)}, u32[]{:S(2)}, u32[]{:S(2)}) async-start(bf16[4,4,256,512]{3,2,1,0:T(8,128)(2,1)} %split.1), calls=%async_computation | async-start | bytes 8388608 | tf_op jit(solution)/shard_map/columns_of_w_out/all_to_all | solution.py:401
  18.3 0.2 select_reduce_fusion
  18.8 1.0 constant_dynamic-slice_fusion.1
  19.7 0.8 copy.48
  20.7 0.7 slice_reduce_fusion
  22.0 0.7 pad_add_fusion.1.index
  22.7 4.2 %fusion.5 = f32[256,32]{1,0:T(8,128)S(1)} fusion(bf16[256,8192]{1,0:T(8,128)(2,1)} %bitcast.22, bf16[8192,32]{0,1:T(8,128)(2,1)S(1)} %copy-done), kind=kOutput, calls=%fused_computation.27 | convolution fusion | flops 134217728 | bytes 4751360 | tf_op jit(solution)/shard_map/base_projections/dot_general | solution.py:408
  26.9 1.2 fusion.6
  28.3 0.8 pad_maximum_fusion
  29.1 4.9 %fusion.4.base_q = f32[256,256]{1,0:T(8,128)S(1)} fusion(bf16[256,8192]{1,0:T(8,128)(2,1)} %bitcast.23, bf16[8192,256]{1,0:T(8,128)(2,1)} %param.25), kind=kOutput, calls=%fused_computation.26 | convolution fusion | flops 1073741824 | bytes 8650752 | tf_op jit(solution)/shard_map/base_projections/dot_general | solution.py:405
  34.0 33.4 %all-to-all-done.source = bf16[4,4,256,512]{3,2,1,0:T(8,128)(2,1)} async-done(((bf16[4,4,256,512]{3,2,1,0:T(8,128)(2,1)}), bf16[4,4,256,512]{3,2,1,0:T(8,128)(2,1)}, u32[]{:S(2)}, u32[]{:S(2)}) %all-to-all-start) | async-done | bytes 4194336 | tf_op jit(solution)/shard_map/columns_of_w_out/all_to_all | solution.py:401
  67.7 0.7 fusion
  68.4 12.3 %all-gather.5.cloned.1.call-done = bf16[11264,512]{1,0:T(8,128)(2,1)} async-done(((bf16[704,512]{1,0:T(8,128)(2,1)}), bf16[11264,512]{1,0:T(8,128)(2,1)}) %all-gather.5.cloned.1.call-update) | async-done | bytes 11534352 | tf_op jit(solution)/shard_map/gather_in_maps/all_gather | solution.py:358
  80.7 3.7 %shrink.1 = bf16[16,48,256]{2,1,0:T(8,128)(2,1)} custom-call(s32[25]{0:T(128)} %pad_add_fusion.1.index, bf16[16,704,512]{2,1,0:T(8,128)(2,1)} %bitcast.17, bf16[13,48,512]{2,1,0:T(8,128)(2,1)} %slot.1, bf16[512,256]{1,0:T(8,128)(2,1)} %bitcast.19, s32[1,256]{1,0:T(1,128)} %bitcast.15), custom_call_target="tpu_custom_call" | custom-call | flops 314572800 | bytes 2097152 | tf_op jit(solution)/shard_map/shrink/shrink/pallas_call | solution.py:423
  84.5 6.9 %all-to-all-start.1 = ((bf16[16,48,256]{2,1,0:T(8,128)(2,1)}), bf16[16,48,256]{2,1,0:T(8,128)(2,1)S(1)}, u32[]{:S(2)}, u32[]{:S(2)}) async-start(bf16[16,48,256]{2,1,0:T(8,128)(2,1)} %shrink.1), calls=%async_computation.1 | async-start | bytes 786432 | tf_op jit(solution)/shard_map/shrink/all_to_all | solution.py:438
  91.6 0.1 copy.43.block
  91.8 2.4 %pick_up.1 = (bf16[400,256]{1,0:T(8,128)(2,1)S(1)}, bf16[400,512]{1,0:T(8,128)(2,1)S(1)}) custom-call(s32[25]{0:T(128)S(1)} %copy-done.8, bf16[16,704,512]{2,1,0:T(8,128)(2,1)} %bitcast.18, bf16[13,16,256]{2,1,0:T(8,128)(2,1)S(1)} %copy-done.3, bf16[13,16,32]{2,1,0:T(8,128)(2,1)S(1)} %copy-done.5, bf16[13,16,32]{2,1,0:T(8,128)(2,1)S(1)} %copy-done.6), custom_call_target="tpu_custom_call" | custom-call | bytes 2097152 | tf_op jit(solution)/shard_map/project/pick_up/pallas_call | solution.py:441
  94.2 7.7 %all-to-all-done.1.parts = bf16[16,48,256]{2,1,0:T(8,128)(2,1)S(1)} async-done(((bf16[16,48,256]{2,1,0:T(8,128)(2,1)}), bf16[16,48,256]{2,1,0:T(8,128)(2,1)S(1)}, u32[]{:S(2)}, u32[]{:S(2)}) %all-to-all-start.1) | async-done | bytes 393248 | tf_op jit(solution)/shard_map/shrink/all_to_all | solution.py:438
  101.9 0.7 project.1
  102.6 11.6 %all_to_all.25.received = bf16[16,16,320]{2,1,0:T(8,128)(2,1)} all-to-all(bf16[16,16,320]{2,1,0:T(8,128)(2,1)S(1)} %project.1), channel_id=1, replica_groups=mesh['group'=16,'y'=4,'x'=4] {'y','x'}, dimensions={0} | all-to-all | bytes 327680 | tf_op jit(solution)/shard_map/attend/all_to_all | solution.py:465
  114.3 8.7 %attend.1 = bf16[16,4,16,256]{3,2,1,0:T(8,128)(2,1)} custom-call(s32[8]{0:T(128)} %lengths.1, bf16[16,16,320]{2,1,0:T(8,128)(2,1)} %all_to_all.25.received, bf16[8,512,512]{2,1,0:T(8,128)(2,1)} %keys.1, bf16[8,512,512]{2,1,0:T(8,128)(2,1)} %values.1), custom_call_target="tpu_custom_call" | custom-call | flops 536870912 | bytes 12582912 | tf_op jit(solution)/shard_map/attend/attend/pallas_call | solution.py:466
  122.9 3.8 %all-to-all-start.3 = ((bf16[16,4,16,256]{3,2,1,0:T(8,128)(2,1)}), bf16[16,4,16,256]{3,2,1,0:T(8,128)(2,1)S(1)}, u32[]{:S(2)}, u32[]{:S(2)}) async-start(bf16[16,4,16,256]{3,2,1,0:T(8,128)(2,1)} %attend.1), calls=%async_computation.3 | async-start | bytes 1048576 | tf_op jit(solution)/shard_map/attend/all_to_all | solution.py:484
  127.0 2.3 %copy-done.1 = bf16[192,16,768]{2,1,0:T(8,128)(2,1)S(1)} copy-done((bf16[192,16,768]{2,1,0:T(8,128)(2,1)S(1)}, bf16[192,16,768]{2,1,0:T(8,128)(2,1)}, u32[]{:S(2)}) %copy-start.1) | copy-done | bytes 4718616
  129.3 1.6 pick.1
  130.9 5.7 %all-to-all-done.3.attended = bf16[16,4,16,256]{3,2,1,0:T(8,128)(2,1)S(1)} async-done(((bf16[16,4,16,256]{3,2,1,0:T(8,128)(2,1)}), bf16[16,4,16,256]{3,2,1,0:T(8,128)(2,1)S(1)}, u32[]{:S(2)}, u32[]{:S(2)}) %all-to-all-start.3) | async-done | bytes 524320 | tf_op jit(solution)/shard_map/attend/all_to_all | solution.py:484
  136.6 3.5 %base_out.1 = (bf16[16,16,256]{2,1,0:T(8,128)(2,1)S(1)}, bf16[256,512]{1,0:T(8,128)(2,1)S(1)}, bf16[256,512]{1,0:T(8,128)(2,1)S(1)}, bf16[256,512]{1,0:T(8,128)(2,1)S(1)}, f32[256,512]{1,0:T(8,128)S(1)}) custom-call(s32[1]{0:T(128)} %bitcast.place, s32[1]{0:T(128)} %bitcast.1.member, bf16[16,4,16,256]{3,2,1,0:T(8,128)(2,1)S(1)} %all-to-all-done.3.attended, ...), custom_call_target="tpu_custom_call" | custom-call | flops 1073741824 | bytes 5242880 | tf_op jit(solution)/shard_map/output/base_out/pallas_call | solution.py:503
  140.2 2.3 %collective-permute-start.1 = (bf16[256,512]{1,0:T(8,128)(2,1)S(1)}, bf16[256,512]{1,0:T(8,128)(2,1)S(1)}, u32[]{:S(2)}, u32[]{:S(2)}) collective-permute-start(bf16[256,512]{1,0:T(8,128)(2,1)S(1)} %get-tuple-element.40), channel_id=1, source_target_pairs={{0,8},{4,12},{8,0},{12,4},{1,9},{5,13},{9,1},{13,5},{2,10},{6,14},... | collective-permute-start | bytes 786440 | tf_op jit(solution)/shard_map/output/ppermute | solution.py:516
  142.5 1.1 collective-permute-start.2
  143.6 12.1 %all_to_all.26.parts = bf16[16,16,256]{2,1,0:T(8,128)(2,1)S(1)} all-to-all(bf16[16,16,256]{2,1,0:T(8,128)(2,1)S(1)} %get-tuple-element.37), channel_id=1, replica_groups=mesh['group'=16,'y'=4,'x'=4] {'y','x'}, dimensions={0} | all-to-all | bytes 262144 | tf_op jit(solution)/shard_map/output/all_to_all | solution.py:514
  155.7 1.1 final.1
  (60 shorter events, 1.3 us)
Async XLA Ops:
  6.5 16.2 %copy-start = (bf16[8192,32]{0,1:T(8,128)(2,1)S(1)}, bf16[8192,32]{0,1:T(8,128)(2,1)}, u32[]{:S(2)}) copy-start(bf16[8192,32]{0,1:T(8,128)(2,1)} %param.26) | copy-start | bytes 1572868
  6.5 74.2 %all-gather.5.cloned.1.call-start = ((), (), s32[]{:S(2)}) async-start(), calls=%async_computation.5 | async-start | bytes 12255232 | tf_op jit(solution)/shard_map/gather_in_maps/all_gather | solution.py:358
  13.2 5.1 %copy-start.12 = (s32[2,192]{1,0:T(2,128)S(1)}, s32[2,192]{1,0:T(2,128)}, u32[]{:S(2)}) copy-start(s32[2,192]{1,0:T(2,128)} %param.34) | copy-start | bytes 4612
  13.2 5.1 %copy-start.13 = (s32[192]{0:T(256)S(1)}, s32[192]{0:T(256)}, u32[]{:S(2)}) copy-start(s32[192]{0:T(256)} %param.35) | copy-start | bytes 2308
  13.2 7.4 %copy-start.15 = (s32[2,192]{1,0:T(2,128)S(1)}, s32[2,192]{1,0:T(2,128)}, u32[]{:S(2)}) copy-start(s32[2,192]{1,0:T(2,128)} %param.33) | copy-start | bytes 4612
  13.2 54.1 %all-to-all-start = ((bf16[4,4,256,512]{3,2,1,0:T(8,128)(2,1)}), bf16[4,4,256,512]{3,2,1,0:T(8,128)(2,1)}, u32[]{:S(2)}, u32[]{:S(2)}) async-start(bf16[4,4,256,512]{3,2,1,0:T(8,128)(2,1)} %split.1), calls=%async_computation | async-start | bytes 8388608 | tf_op jit(solution)/shard_map/columns_of_w_out/all_to_all | solution.py:401
  18.2 8.7 %copy-start.16 = (bf16[8192,32]{0,1:T(8,128)(2,1)S(1)}, bf16[8192,32]{0,1:T(8,128)(2,1)}, u32[]{:S(2)}) copy-start(bf16[8192,32]{0,1:T(8,128)(2,1)} %param.27) | copy-start | bytes 1572868
  18.2 108.7 %all-gather.7.cloned.1.call-start = ((), (), s32[]{:S(2)}) async-start(), calls=%async_computation.6 | async-start | bytes 5013504 | tf_op jit(solution)/shard_map/gather_out_maps/all_gather | solution.py:420
  22.0 4.9 %copy-start.11 = (bf16[2,128,8192]{2,1,0:T(8,128)(2,1)S(1)}, bf16[2,128,8192]{2,1,0:T(8,128)(2,1)}, u32[]{:S(2)}) copy-start(bf16[2,128,8192]{2,1,0:T(8,128)(2,1)} %param.24) | copy-start | bytes 12582916
  22.7 5.6 %copy-start.9 = (bf16[12,16,512]{2,1,0:T(8,128)(2,1)S(1)}, bf16[12,16,512]{2,1,0:T(8,128)(2,1)}, u32[]{:S(2)}) copy-start(bf16[12,16,512]{2,1,0:T(8,128)(2,1)} %param.41) | copy-start | bytes 589828
  22.7 5.6 %copy-start.10 = (bf16[12,16,256]{2,1,0:T(8,128)(2,1)S(1)}, bf16[12,16,256]{2,1,0:T(8,128)(2,1)}, u32[]{:S(2)}) copy-start(bf16[12,16,256]{2,1,0:T(8,128)(2,1)} %param.40) | copy-start | bytes 294916
  29.0 38.7 %copy-start.14 = (s32[2,128]{1,0:T(2,128)S(1)}, s32[2,128]{1,0:T(2,128)}, u32[]{:S(2)}) copy-start(s32[2,128]{1,0:T(2,128)} %param.32) | copy-start | bytes 3076
  80.7 10.8 %copy-start.7 = (s32[2,128]{1,0:T(2,128)S(1)}, s32[2,128]{1,0:T(2,128)}, u32[]{:S(2)}) copy-start(s32[2,128]{1,0:T(2,128)} %fusion) | copy-start | bytes 3076
  80.7 11.0 %copy-start.3 = (bf16[13,16,256]{2,1,0:T(8,128)(2,1)S(1)}, bf16[13,16,256]{2,1,0:T(8,128)(2,1)}, u32[]{:S(2)}) copy-start(bf16[13,16,256]{2,1,0:T(8,128)(2,1)} %slot_q.1) | copy-start | bytes 319492
  80.7 11.0 %copy-start.5 = (bf16[13,16,32]{2,1,0:T(8,128)(2,1)S(1)}, bf16[13,16,32]{2,1,0:T(8,128)(2,1)}, u32[]{:S(2)}) copy-start(bf16[13,16,32]{2,1,0:T(8,128)(2,1)} %slot_k.1) | copy-start | bytes 39940
  80.7 11.0 %copy-start.6 = (bf16[13,16,32]{2,1,0:T(8,128)(2,1)S(1)}, bf16[13,16,32]{2,1,0:T(8,128)(2,1)}, u32[]{:S(2)}) copy-start(bf16[13,16,32]{2,1,0:T(8,128)(2,1)} %slot_v.1) | copy-start | bytes 39940
  80.7 11.1 %copy-start.8 = (s32[25]{0:T(128)S(1)}, s32[25]{0:T(128)}, u32[]{:S(2)}) copy-start(s32[25]{0:T(128)} %pad_add_fusion.1.index) | copy-start | bytes 304
  84.5 17.4 %all-to-all-start.1 = ((bf16[16,48,256]{2,1,0:T(8,128)(2,1)}), bf16[16,48,256]{2,1,0:T(8,128)(2,1)S(1)}, u32[]{:S(2)}, u32[]{:S(2)}) async-start(bf16[16,48,256]{2,1,0:T(8,128)(2,1)} %shrink.1), calls=%async_computation.1 | async-start | bytes 786432 | tf_op jit(solution)/shard_map/shrink/all_to_all | solution.py:438
  114.3 12.7 %copy-start.2 = (bf16[13,16,512]{2,1,0:T(8,128)(2,1)S(1)}, bf16[13,16,512]{2,1,0:T(8,128)(2,1)}, u32[]{:S(2)}) copy-start(bf16[13,16,512]{2,1,0:T(8,128)(2,1)} %slot_up.1) | copy-start | bytes 638980
  114.3 12.7 %copy-start.4 = (bf16[13,16,256]{2,1,0:T(8,128)(2,1)S(1)}, bf16[13,16,256]{2,1,0:T(8,128)(2,1)}, u32[]{:S(2)}) copy-start(bf16[13,16,256]{2,1,0:T(8,128)(2,1)} %slot_in.1) | copy-start | bytes 319492
  122.9 13.7 %all-to-all-start.3 = ((bf16[16,4,16,256]{3,2,1,0:T(8,128)(2,1)}), bf16[16,4,16,256]{3,2,1,0:T(8,128)(2,1)S(1)}, u32[]{:S(2)}, u32[]{:S(2)}) async-start(bf16[16,4,16,256]{3,2,1,0:T(8,128)(2,1)} %attend.1), calls=%async_computation.3 | async-start | bytes 1048576 | tf_op jit(solution)/shard_map/attend/all_to_all | solution.py:484
  126.9 2.3 %copy-start.1 = (bf16[192,16,768]{2,1,0:T(8,128)(2,1)S(1)}, bf16[192,16,768]{2,1,0:T(8,128)(2,1)}, u32[]{:S(2)}) copy-start(bf16[192,16,768]{2,1,0:T(8,128)(2,1)} %all-gather.7.cloned.1.call-done.pool) | copy-start | bytes 14155780
  140.1 15.7 %collective-permute-start = (bf16[256,512]{1,0:T(8,128)(2,1)S(1)}, bf16[256,512]{1,0:T(8,128)(2,1)S(1)}, u32[]{:S(2)}, u32[]{:S(2)}) collective-permute-start(bf16[256,512]{1,0:T(8,128)(2,1)S(1)} %get-tuple-element.39), channel_id=1, source_target_pairs={{0,4},{4,8},{8,12},{12,0},{1,5},{5,9},{9,13},{13,1},{2,6},{6,10},{... | collective-permute-start | bytes 786440 | tf_op jit(solution)/shard_map/output/ppermute | solution.py:516
  140.2 15.6 %collective-permute-start.1 = (bf16[256,512]{1,0:T(8,128)(2,1)S(1)}, bf16[256,512]{1,0:T(8,128)(2,1)S(1)}, u32[]{:S(2)}, u32[]{:S(2)}) collective-permute-start(bf16[256,512]{1,0:T(8,128)(2,1)S(1)} %get-tuple-element.40), channel_id=1, source_target_pairs={{0,8},{4,12},{8,0},{12,4},{1,9},{5,13},{9,1},{13,5},{2,10},{6,14},... | collective-permute-start | bytes 786440 | tf_op jit(solution)/shard_map/output/ppermute | solution.py:516
  142.5 13.3 %collective-permute-start.2 = (bf16[256,512]{1,0:T(8,128)(2,1)S(1)}, bf16[256,512]{1,0:T(8,128)(2,1)S(1)}, u32[]{:S(2)}, u32[]{:S(2)}) collective-permute-start(bf16[256,512]{1,0:T(8,128)(2,1)S(1)} %get-tuple-element.41), channel_id=1, source_target_pairs={{0,12},{4,0},{8,4},{12,8},{1,13},{5,1},{9,5},{13,9},{2,14},{6,2},{... | collective-permute-start | bytes 786440 | tf_op jit(solution)/shard_map/output/ppermute | solution.py:516
Sparse Core Ops, SparseCore 0:
  9.2 71.4 all-gather.4
  82.5 42.6 all-gather.6

commit v8 on v7

--- a/solution.py
+++ b/solution.py
@@ -229,18 +229,24 @@
     in_time = new_step <= iota(shape, 0) // QH
     scale = 1.0 / math.sqrt(HD)
     dims = (((1,), (1,)), ((), ()))
+    spreads = []
+    for i in range(LOCAL):
+        asked = []
+        for s in range(STEPS):
+            low = (s * LOCAL + i) * N
+            asked += [mine[low : low + N, :HD], mine[low : low + N, HD:QF]]
+        asked = jnp.concatenate(asked, axis=0)
+        spreads.append(jnp.where(own, jnp.concatenate([asked] * KH, axis=1), jnp.zeros((), BF16)))
+    fresh_scores = lax.dot_general(
+        jnp.concatenate(spreads, axis=0), keys_new, dims, preferred_element_type=F32
+    ) * scale
     for i in range(LOCAL):
         if i % GROUPED == 0:
             for pair in loads[i : i + GROUPED]:
                 for copy in pair:
                     copy.wait()
-        asked = []
-        for s in range(STEPS):
-            low = (s * LOCAL + i) * N
-            asked += [mine[low : low + N, :HD], mine[low : low + N, HD:QF]]
-        asked = jnp.concatenate(asked, axis=0)
-        spread = jnp.where(own, jnp.concatenate([asked] * KH, axis=1), jnp.zeros((), BF16))
-        new = lax.dot_general(spread, keys_new, dims, preferred_element_type=F32) * scale
+        spread = spreads[i]
+        new = fresh_scores[i * head_rows : (i + 1) * head_rows]
         new = jnp.where(in_time & (new_row == i), new, -jnp.inf)
         old = lax.dot_general(spread, key_rows[i], dims, preferred_element_type=F32) * scale
         old = jnp.where(place < lengths[i], old, -jnp.inf)

time: 166 us -> 166 us (level)
  no operation moved by 1% of the time
where the time goes in v8:
time: 166 us; the launch traced here: 164 us
  waiting for transfers between devices  59.4 us (36%)
  Pallas kernels  28 us (17%)
  blocking collectives  23.7 us (14%)
  starting transfers between devices  19.2 us (12%)
  between operations  14.4 us (9%)
  matrix products  10.3 us (6%)
  local copies, waits for them, and re-layouts  4.96 us (3%)
  other arithmetic  3.47 us (2%)
    all_to_all x1, waiting for transfers between devices, shard(): mine = lax.all_to_all(half, 'x', split_axis=0, concat_axis=0, tiled=True)  33.4 us
    all_gather x1, waiting for transfers between devices, shard(): pool = lax.all_gather(packed, 'group')  12.3 us
    all_to_all x1, blocking collectives, shard(): lax.all_to_all(partial_out, TP, split_axis=0, concat_axis=0, tiled=True)  12.1 us
    all_to_all x1, blocking collectives, shard(): lax.all_to_all(projected, TP, split_axis=0, concat_axis=0, tiled=True)  11.6 us
    pallas_call x1, Pallas kernels, shard(): pl.pallas_call(attend_kernel, out_shape=jax.ShapeDtypeStruct((N, SIDE, MI...  8.43 us
    all_to_all x1, waiting for transfers between devices, shard(): lax.all_to_all(partial_in, TP, split_axis=0, concat_axis=0, tiled=True)  7.72 us
    all_to_all x1, starting transfers between devices, shard(): lax.all_to_all(partial_in, TP, split_axis=0, concat_axis=0, tiled=True)  6.93 us
    all_to_all x1, waiting for transfers between devices, shard(): lax.all_to_all(payload, TP, split_axis=0, concat_axis=0, tiled=True)  5.9 us
  transfers between devices with their start and end apart: 8, of which 4 were waited for; matrix products, arithmetic and copies ran while one was open for 10% of the time, Pallas kernels for 13%

profile of v8, /device:TPU:32, one launch (start us, length us, event | category | flops | bytes accessed | tf_op | source)
XLA Modules:
  0.0 163.6 jit_solution(17678776163316204859)
XLA Ops:
  6.5 2.3 %pack.1 = bf16[704,512]{1,0:T(8,128)(2,1)} custom-call(bf16[12,48,512]{2,1,0:T(8,128)(2,1)} %maps_in.1, bf16[12,16,256]{2,1,0:T(8,128)(2,1)} %maps_q.1, bf16[12,16,32]{2,1,0:T(8,128)(2,1)} %maps_k.1, bf16[12,16,32]{2,1,0:T(8,128)(2,1)} %maps_v.1), custom_call_target="tpu_custom_call" | custom-call | bytes 2097152 | tf_op jit(solution)/shard_map/gather_in_maps/pack/pallas_call | solution.py:348
  8.8 4.3 %split.1 = bf16[4,4,256,512]{3,2,1,0:T(8,128)(2,1)} custom-call(bf16[256,8192]{1,0:T(8,128)(2,1)} %weight), custom_call_target="tpu_custom_call" | custom-call | bytes 8388608 | tf_op jit(solution)/shard_map/columns_of_w_out/split/pallas_call | solution.py:397
  13.2 5.0 %all-to-all-start = ((bf16[4,4,256,512]{3,2,1,0:T(8,128)(2,1)}), bf16[4,4,256,512]{3,2,1,0:T(8,128)(2,1)}, u32[]{:S(2)}, u32[]{:S(2)}) async-start(bf16[4,4,256,512]{3,2,1,0:T(8,128)(2,1)} %split.1), calls=%async_computation | async-start | bytes 8388608 | tf_op jit(solution)/shard_map/columns_of_w_out/all_to_all | solution.py:407
  18.3 0.2 select_reduce_fusion
  18.8 1.0 constant_dynamic-slice_fusion.1
  19.7 0.8 copy.48
  20.7 0.7 slice_reduce_fusion
  22.0 0.7 pad_add_fusion.1.index
  22.7 4.2 %fusion.5 = f32[256,32]{1,0:T(8,128)S(1)} fusion(bf16[256,8192]{1,0:T(8,128)(2,1)} %bitcast.22, bf16[8192,32]{0,1:T(8,128)(2,1)S(1)} %copy-done), kind=kOutput, calls=%fused_computation.27 | convolution fusion | flops 134217728 | bytes 4751360 | tf_op jit(solution)/shard_map/base_projections/dot_general | solution.py:414
  26.9 1.2 fusion.6
  28.3 0.8 pad_maximum_fusion
  29.1 4.9 %fusion.4.base_q = f32[256,256]{1,0:T(8,128)S(1)} fusion(bf16[256,8192]{1,0:T(8,128)(2,1)} %bitcast.23, bf16[8192,256]{1,0:T(8,128)(2,1)} %param.25), kind=kOutput, calls=%fused_computation.26 | convolution fusion | flops 1073741824 | bytes 8650752 | tf_op jit(solution)/shard_map/base_projections/dot_general | solution.py:411
  34.0 33.4 %all-to-all-done.source = bf16[4,4,256,512]{3,2,1,0:T(8,128)(2,1)} async-done(((bf16[4,4,256,512]{3,2,1,0:T(8,128)(2,1)}), bf16[4,4,256,512]{3,2,1,0:T(8,128)(2,1)}, u32[]{:S(2)}, u32[]{:S(2)}) %all-to-all-start) | async-done | bytes 4194336 | tf_op jit(solution)/shard_map/columns_of_w_out/all_to_all | solution.py:407
  67.7 0.7 fusion
  68.4 12.3 %all-gather.5.cloned.1.call-done = bf16[11264,512]{1,0:T(8,128)(2,1)} async-done(((bf16[704,512]{1,0:T(8,128)(2,1)}), bf16[11264,512]{1,0:T(8,128)(2,1)}) %all-gather.5.cloned.1.call-update) | async-done | bytes 11534352 | tf_op jit(solution)/shard_map/gather_in_maps/all_gather | solution.py:364
  80.7 3.7 %shrink.1 = bf16[16,48,256]{2,1,0:T(8,128)(2,1)} custom-call(s32[25]{0:T(128)} %pad_add_fusion.1.index, bf16[16,704,512]{2,1,0:T(8,128)(2,1)} %bitcast.17, bf16[13,48,512]{2,1,0:T(8,128)(2,1)} %slot.1, bf16[512,256]{1,0:T(8,128)(2,1)} %bitcast.19, s32[1,256]{1,0:T(1,128)} %bitcast.15), custom_call_target="tpu_custom_call" | custom-call | flops 314572800 | bytes 2097152 | tf_op jit(solution)/shard_map/shrink/shrink/pallas_call | solution.py:429
  84.5 6.9 %all-to-all-start.1 = ((bf16[16,48,256]{2,1,0:T(8,128)(2,1)}), bf16[16,48,256]{2,1,0:T(8,128)(2,1)S(1)}, u32[]{:S(2)}, u32[]{:S(2)}) async-start(bf16[16,48,256]{2,1,0:T(8,128)(2,1)} %shrink.1), calls=%async_computation.1 | async-start | bytes 786432 | tf_op jit(solution)/shard_map/shrink/all_to_all | solution.py:444
  91.8 2.4 %pick_up.1 = (bf16[400,256]{1,0:T(8,128)(2,1)S(1)}, bf16[400,512]{1,0:T(8,128)(2,1)S(1)}) custom-call(s32[25]{0:T(128)S(1)} %copy-done.8, bf16[16,704,512]{2,1,0:T(8,128)(2,1)} %bitcast.18, bf16[13,16,256]{2,1,0:T(8,128)(2,1)S(1)} %copy-done.3, bf16[13,16,32]{2,1,0:T(8,128)(2,1)S(1)} %copy-done.5, bf16[13,16,32]{2,1,0:T(8,128)(2,1)S(1)} %copy-done.6), custom_call_target="tpu_custom_call" | custom-call | bytes 2097152 | tf_op jit(solution)/shard_map/project/pick_up/pallas_call | solution.py:447
  94.2 7.7 %all-to-all-done.1.parts = bf16[16,48,256]{2,1,0:T(8,128)(2,1)S(1)} async-done(((bf16[16,48,256]{2,1,0:T(8,128)(2,1)}), bf16[16,48,256]{2,1,0:T(8,128)(2,1)S(1)}, u32[]{:S(2)}, u32[]{:S(2)}) %all-to-all-start.1) | async-done | bytes 393248 | tf_op jit(solution)/shard_map/shrink/all_to_all | solution.py:444
  101.9 0.7 project.1
  102.6 11.6 %all_to_all.25.received = bf16[16,16,320]{2,1,0:T(8,128)(2,1)} all-to-all(bf16[16,16,320]{2,1,0:T(8,128)(2,1)S(1)} %project.1), channel_id=1, replica_groups=mesh['group'=16,'y'=4,'x'=4] {'y','x'}, dimensions={0} | all-to-all | bytes 327680 | tf_op jit(solution)/shard_map/attend/all_to_all | solution.py:471
  114.3 8.4 %attend.1 = bf16[16,4,16,256]{3,2,1,0:T(8,128)(2,1)} custom-call(s32[8]{0:T(128)} %lengths.1, bf16[16,16,320]{2,1,0:T(8,128)(2,1)} %all_to_all.25.received, bf16[8,512,512]{2,1,0:T(8,128)(2,1)} %keys.1, bf16[8,512,512]{2,1,0:T(8,128)(2,1)} %values.1), custom_call_target="tpu_custom_call" | custom-call | flops 536870912 | bytes 12582912 | tf_op jit(solution)/shard_map/attend/attend/pallas_call | solution.py:472
  122.7 3.6 %all-to-all-start.3 = ((bf16[16,4,16,256]{3,2,1,0:T(8,128)(2,1)}), bf16[16,4,16,256]{3,2,1,0:T(8,128)(2,1)S(1)}, u32[]{:S(2)}, u32[]{:S(2)}) async-start(bf16[16,4,16,256]{3,2,1,0:T(8,128)(2,1)} %attend.1), calls=%async_computation.3 | async-start | bytes 1048576 | tf_op jit(solution)/shard_map/attend/all_to_all | solution.py:490
  126.5 2.3 %copy-done.1 = bf16[192,16,768]{2,1,0:T(8,128)(2,1)S(1)} copy-done((bf16[192,16,768]{2,1,0:T(8,128)(2,1)S(1)}, bf16[192,16,768]{2,1,0:T(8,128)(2,1)}, u32[]{:S(2)}) %copy-start.1) | copy-done | bytes 4718616
  128.9 1.6 pick.1
  130.4 5.9 %all-to-all-done.3.attended = bf16[16,4,16,256]{3,2,1,0:T(8,128)(2,1)S(1)} async-done(((bf16[16,4,16,256]{3,2,1,0:T(8,128)(2,1)}), bf16[16,4,16,256]{3,2,1,0:T(8,128)(2,1)S(1)}, u32[]{:S(2)}, u32[]{:S(2)}) %all-to-all-start.3) | async-done | bytes 524320 | tf_op jit(solution)/shard_map/attend/all_to_all | solution.py:490
  136.3 3.5 %base_out.1 = (bf16[16,16,256]{2,1,0:T(8,128)(2,1)S(1)}, bf16[256,512]{1,0:T(8,128)(2,1)S(1)}, bf16[256,512]{1,0:T(8,128)(2,1)S(1)}, bf16[256,512]{1,0:T(8,128)(2,1)S(1)}, f32[256,512]{1,0:T(8,128)S(1)}) custom-call(s32[1]{0:T(128)} %bitcast.place, s32[1]{0:T(128)} %bitcast.1.member, bf16[16,4,16,256]{3,2,1,0:T(8,128)(2,1)S(1)} %all-to-all-done.3.attended, ...), custom_call_target="tpu_custom_call" | custom-call | flops 1073741824 | bytes 5242880 | tf_op jit(solution)/shard_map/output/base_out/pallas_call | solution.py:509
  139.8 0.3 collective-permute-start
  140.1 2.3 %collective-permute-start.1 = (bf16[256,512]{1,0:T(8,128)(2,1)S(1)}, bf16[256,512]{1,0:T(8,128)(2,1)S(1)}, u32[]{:S(2)}, u32[]{:S(2)}) collective-permute-start(bf16[256,512]{1,0:T(8,128)(2,1)S(1)} %get-tuple-element.40), channel_id=1, source_target_pairs={{0,8},{4,12},{8,0},{12,4},{1,9},{5,13},{9,1},{13,5},{2,10},{6,14},... | collective-permute-start | bytes 786440 | tf_op jit(solution)/shard_map/output/ppermute | solution.py:522
  142.4 1.1 collective-permute-start.2
  143.5 12.1 %all_to_all.26.parts = bf16[16,16,256]{2,1,0:T(8,128)(2,1)S(1)} all-to-all(bf16[16,16,256]{2,1,0:T(8,128)(2,1)S(1)} %get-tuple-element.37), channel_id=1, replica_groups=mesh['group'=16,'y'=4,'x'=4] {'y','x'}, dimensions={0} | all-to-all | bytes 262144 | tf_op jit(solution)/shard_map/output/all_to_all | solution.py:520
  155.7 1.1 final.1
  (60 shorter events, 1.4 us)
Async XLA Ops:
  6.5 16.2 %copy-start = (bf16[8192,32]{0,1:T(8,128)(2,1)S(1)}, bf16[8192,32]{0,1:T(8,128)(2,1)}, u32[]{:S(2)}) copy-start(bf16[8192,32]{0,1:T(8,128)(2,1)} %param.26) | copy-start | bytes 1572868
  6.5 74.2 %all-gather.5.cloned.1.call-start = ((), (), s32[]{:S(2)}) async-start(), calls=%async_computation.5 | async-start | bytes 12255232 | tf_op jit(solution)/shard_map/gather_in_maps/all_gather | solution.py:364
  13.2 5.1 %copy-start.12 = (s32[2,192]{1,0:T(2,128)S(1)}, s32[2,192]{1,0:T(2,128)}, u32[]{:S(2)}) copy-start(s32[2,192]{1,0:T(2,128)} %param.34) | copy-start | bytes 4612
  13.2 5.1 %copy-start.13 = (s32[192]{0:T(256)S(1)}, s32[192]{0:T(256)}, u32[]{:S(2)}) copy-start(s32[192]{0:T(256)} %param.35) | copy-start | bytes 2308
  13.2 7.4 %copy-start.15 = (s32[2,192]{1,0:T(2,128)S(1)}, s32[2,192]{1,0:T(2,128)}, u32[]{:S(2)}) copy-start(s32[2,192]{1,0:T(2,128)} %param.33) | copy-start | bytes 4612
  13.2 54.1 %all-to-all-start = ((bf16[4,4,256,512]{3,2,1,0:T(8,128)(2,1)}), bf16[4,4,256,512]{3,2,1,0:T(8,128)(2,1)}, u32[]{:S(2)}, u32[]{:S(2)}) async-start(bf16[4,4,256,512]{3,2,1,0:T(8,128)(2,1)} %split.1), calls=%async_computation | async-start | bytes 8388608 | tf_op jit(solution)/shard_map/columns_of_w_out/all_to_all | solution.py:407
  18.2 8.7 %copy-start.16 = (bf16[8192,32]{0,1:T(8,128)(2,1)S(1)}, bf16[8192,32]{0,1:T(8,128)(2,1)}, u32[]{:S(2)}) copy-start(bf16[8192,32]{0,1:T(8,128)(2,1)} %param.27) | copy-start | bytes 1572868
  18.2 108.3 %all-gather.7.cloned.1.call-start = ((), (), s32[]{:S(2)}) async-start(), calls=%async_computation.6 | async-start | bytes 5013504 | tf_op jit(solution)/shard_map/gather_out_maps/all_gather | solution.py:426
  22.0 4.9 %copy-start.11 = (bf16[2,128,8192]{2,1,0:T(8,128)(2,1)S(1)}, bf16[2,128,8192]{2,1,0:T(8,128)(2,1)}, u32[]{:S(2)}) copy-start(bf16[2,128,8192]{2,1,0:T(8,128)(2,1)} %param.24) | copy-start | bytes 12582916
  22.7 5.6 %copy-start.9 = (bf16[12,16,512]{2,1,0:T(8,128)(2,1)S(1)}, bf16[12,16,512]{2,1,0:T(8,128)(2,1)}, u32[]{:S(2)}) copy-start(bf16[12,16,512]{2,1,0:T(8,128)(2,1)} %param.41) | copy-start | bytes 589828
  22.7 5.6 %copy-start.10 = (bf16[12,16,256]{2,1,0:T(8,128)(2,1)S(1)}, bf16[12,16,256]{2,1,0:T(8,128)(2,1)}, u32[]{:S(2)}) copy-start(bf16[12,16,256]{2,1,0:T(8,128)(2,1)} %param.40) | copy-start | bytes 294916
  29.0 38.7 %copy-start.14 = (s32[2,128]{1,0:T(2,128)S(1)}, s32[2,128]{1,0:T(2,128)}, u32[]{:S(2)}) copy-start(s32[2,128]{1,0:T(2,128)} %param.32) | copy-start | bytes 3076
  80.7 10.8 %copy-start.7 = (s32[2,128]{1,0:T(2,128)S(1)}, s32[2,128]{1,0:T(2,128)}, u32[]{:S(2)}) copy-start(s32[2,128]{1,0:T(2,128)} %fusion) | copy-start | bytes 3076
  80.7 11.0 %copy-start.3 = (bf16[13,16,256]{2,1,0:T(8,128)(2,1)S(1)}, bf16[13,16,256]{2,1,0:T(8,128)(2,1)}, u32[]{:S(2)}) copy-start(bf16[13,16,256]{2,1,0:T(8,128)(2,1)} %slot_q.1) | copy-start | bytes 319492
  80.7 11.0 %copy-start.5 = (bf16[13,16,32]{2,1,0:T(8,128)(2,1)S(1)}, bf16[13,16,32]{2,1,0:T(8,128)(2,1)}, u32[]{:S(2)}) copy-start(bf16[13,16,32]{2,1,0:T(8,128)(2,1)} %slot_k.1) | copy-start | bytes 39940
  80.7 11.0 %copy-start.6 = (bf16[13,16,32]{2,1,0:T(8,128)(2,1)S(1)}, bf16[13,16,32]{2,1,0:T(8,128)(2,1)}, u32[]{:S(2)}) copy-start(bf16[13,16,32]{2,1,0:T(8,128)(2,1)} %slot_v.1) | copy-start | bytes 39940
  80.7 11.1 %copy-start.8 = (s32[25]{0:T(128)S(1)}, s32[25]{0:T(128)}, u32[]{:S(2)}) copy-start(s32[25]{0:T(128)} %pad_add_fusion.1.index) | copy-start | bytes 304
  84.5 17.4 %all-to-all-start.1 = ((bf16[16,48,256]{2,1,0:T(8,128)(2,1)}), bf16[16,48,256]{2,1,0:T(8,128)(2,1)S(1)}, u32[]{:S(2)}, u32[]{:S(2)}) async-start(bf16[16,48,256]{2,1,0:T(8,128)(2,1)} %shrink.1), calls=%async_computation.1 | async-start | bytes 786432 | tf_op jit(solution)/shard_map/shrink/all_to_all | solution.py:444
  114.3 12.3 %copy-start.2 = (bf16[13,16,512]{2,1,0:T(8,128)(2,1)S(1)}, bf16[13,16,512]{2,1,0:T(8,128)(2,1)}, u32[]{:S(2)}) copy-start(bf16[13,16,512]{2,1,0:T(8,128)(2,1)} %slot_up.1) | copy-start | bytes 638980
  114.3 12.3 %copy-start.4 = (bf16[13,16,256]{2,1,0:T(8,128)(2,1)S(1)}, bf16[13,16,256]{2,1,0:T(8,128)(2,1)}, u32[]{:S(2)}) copy-start(bf16[13,16,256]{2,1,0:T(8,128)(2,1)} %slot_in.1) | copy-start | bytes 319492
  122.7 13.6 %all-to-all-start.3 = ((bf16[16,4,16,256]{3,2,1,0:T(8,128)(2,1)}), bf16[16,4,16,256]{3,2,1,0:T(8,128)(2,1)S(1)}, u32[]{:S(2)}, u32[]{:S(2)}) async-start(bf16[16,4,16,256]{3,2,1,0:T(8,128)(2,1)} %attend.1), calls=%async_computation.3 | async-start | bytes 1048576 | tf_op jit(solution)/shard_map/attend/all_to_all | solution.py:490
  126.5 2.3 %copy-start.1 = (bf16[192,16,768]{2,1,0:T(8,128)(2,1)S(1)}, bf16[192,16,768]{2,1,0:T(8,128)(2,1)}, u32[]{:S(2)}) copy-start(bf16[192,16,768]{2,1,0:T(8,128)(2,1)} %all-gather.7.cloned.1.call-done.pool) | copy-start | bytes 14155780
  139.8 15.8 %collective-permute-start = (bf16[256,512]{1,0:T(8,128)(2,1)S(1)}, bf16[256,512]{1,0:T(8,128)(2,1)S(1)}, u32[]{:S(2)}, u32[]{:S(2)}) collective-permute-start(bf16[256,512]{1,0:T(8,128)(2,1)S(1)} %get-tuple-element.39), channel_id=1, source_target_pairs={{0,4},{4,8},{8,12},{12,0},{1,5},{5,9},{9,13},{13,1},{2,6},{6,10},{... | collective-permute-start | bytes 786440 | tf_op jit(solution)/shard_map/output/ppermute | solution.py:522
  140.1 15.6 %collective-permute-start.1 = (bf16[256,512]{1,0:T(8,128)(2,1)S(1)}, bf16[256,512]{1,0:T(8,128)(2,1)S(1)}, u32[]{:S(2)}, u32[]{:S(2)}) collective-permute-start(bf16[256,512]{1,0:T(8,128)(2,1)S(1)} %get-tuple-element.40), channel_id=1, source_target_pairs={{0,8},{4,12},{8,0},{12,4},{1,9},{5,13},{9,1},{13,5},{2,10},{6,14},... | collective-permute-start | bytes 786440 | tf_op jit(solution)/shard_map/output/ppermute | solution.py:522
  142.4 13.3 %collective-permute-start.2 = (bf16[256,512]{1,0:T(8,128)(2,1)S(1)}, bf16[256,512]{1,0:T(8,128)(2,1)S(1)}, u32[]{:S(2)}, u32[]{:S(2)}) collective-permute-start(bf16[256,512]{1,0:T(8,128)(2,1)S(1)} %get-tuple-element.41), channel_id=1, source_target_pairs={{0,12},{4,0},{8,4},{12,8},{1,13},{5,1},{9,5},{13,9},{2,14},{6,2},{... | collective-permute-start | bytes 786440 | tf_op jit(solution)/shard_map/output/ppermute | solution.py:522
Sparse Core Ops, SparseCore 0:
  9.2 71.4 all-gather.4
  82.5 42.5 all-gather.6

commit v9 on v8

--- a/solution.py
+++ b/solution.py
@@ -18,7 +18,7 @@
 HELD = 12
 N = 16
 SIDE = 4
-GROUPED = 2
+GROUPED = 1
 ALL_ROWS = STEPS * ROWS
 LOCAL = ROWS // N
 MINE = STEPS * LOCAL

time: 166 us -> 166 us (level)
  no operation moved by 1% of the time
where the time goes in v9:
time: 166 us; the launch traced here: 164 us
  waiting for transfers between devices  59.2 us (36%)
  Pallas kernels  28.6 us (17%)
  blocking collectives  23.8 us (14%)
  starting transfers between devices  19.2 us (12%)
  between operations  14.4 us (9%)
  matrix products  10.3 us (6%)
  local copies, waits for them, and re-layouts  4.96 us (3%)
  other arithmetic  3.47 us (2%)
    all_to_all x1, waiting for transfers between devices, shard(): mine = lax.all_to_all(half, 'x', split_axis=0, concat_axis=0, tiled=True)  33.4 us
    all_gather x1, waiting for transfers between devices, shard(): pool = lax.all_gather(packed, 'group')  12.3 us
    all_to_all x1, blocking collectives, shard(): lax.all_to_all(partial_out, TP, split_axis=0, concat_axis=0, tiled=True)  12.1 us
    all_to_all x1, blocking collectives, shard(): lax.all_to_all(projected, TP, split_axis=0, concat_axis=0, tiled=True)  11.6 us
    pallas_call x1, Pallas kernels, shard(): pl.pallas_call(attend_kernel, out_shape=jax.ShapeDtypeStruct((N, SIDE, MI...  8.94 us
    all_to_all x1, waiting for transfers between devices, shard(): lax.all_to_all(partial_in, TP, split_axis=0, concat_axis=0, tiled=True)  7.69 us
    all_to_all x1, starting transfers between devices, shard(): lax.all_to_all(partial_in, TP, split_axis=0, concat_axis=0, tiled=True)  6.93 us
    all_to_all x1, waiting for transfers between devices, shard(): lax.all_to_all(payload, TP, split_axis=0, concat_axis=0, tiled=True)  5.72 us
  transfers between devices with their start and end apart: 8, of which 4 were waited for; matrix products, arithmetic and copies ran while one was open for 10% of the time, Pallas kernels for 13%

profile of v9, /device:TPU:32, one launch (start us, length us, event | category | flops | bytes accessed | tf_op | source)
XLA Modules:
  0.0 163.9 jit_solution(12304983535312215127)
XLA Ops:
  6.5 2.3 %pack.1 = bf16[704,512]{1,0:T(8,128)(2,1)} custom-call(bf16[12,48,512]{2,1,0:T(8,128)(2,1)} %maps_in.1, bf16[12,16,256]{2,1,0:T(8,128)(2,1)} %maps_q.1, bf16[12,16,32]{2,1,0:T(8,128)(2,1)} %maps_k.1, bf16[12,16,32]{2,1,0:T(8,128)(2,1)} %maps_v.1), custom_call_target="tpu_custom_call" | custom-call | bytes 2097152 | tf_op jit(solution)/shard_map/gather_in_maps/pack/pallas_call | solution.py:348
  8.8 4.3 %split.1 = bf16[4,4,256,512]{3,2,1,0:T(8,128)(2,1)} custom-call(bf16[256,8192]{1,0:T(8,128)(2,1)} %weight), custom_call_target="tpu_custom_call" | custom-call | bytes 8388608 | tf_op jit(solution)/shard_map/columns_of_w_out/split/pallas_call | solution.py:397
  13.2 5.0 %all-to-all-start = ((bf16[4,4,256,512]{3,2,1,0:T(8,128)(2,1)}), bf16[4,4,256,512]{3,2,1,0:T(8,128)(2,1)}, u32[]{:S(2)}, u32[]{:S(2)}) async-start(bf16[4,4,256,512]{3,2,1,0:T(8,128)(2,1)} %split.1), calls=%async_computation | async-start | bytes 8388608 | tf_op jit(solution)/shard_map/columns_of_w_out/all_to_all | solution.py:407
  18.3 0.2 select_reduce_fusion
  18.8 1.0 constant_dynamic-slice_fusion.1
  19.7 0.8 copy.48
  20.7 0.7 slice_reduce_fusion
  22.0 0.7 pad_add_fusion.1.index
  22.7 4.2 %fusion.5 = f32[256,32]{1,0:T(8,128)S(1)} fusion(bf16[256,8192]{1,0:T(8,128)(2,1)} %bitcast.22, bf16[8192,32]{0,1:T(8,128)(2,1)S(1)} %copy-done), kind=kOutput, calls=%fused_computation.27 | convolution fusion | flops 134217728 | bytes 4751360 | tf_op jit(solution)/shard_map/base_projections/dot_general | solution.py:414
  26.9 1.2 fusion.6
  28.3 0.8 pad_maximum_fusion
  29.1 4.9 %fusion.4.base_q = f32[256,256]{1,0:T(8,128)S(1)} fusion(bf16[256,8192]{1,0:T(8,128)(2,1)} %bitcast.23, bf16[8192,256]{1,0:T(8,128)(2,1)} %param.25), kind=kOutput, calls=%fused_computation.26 | convolution fusion | flops 1073741824 | bytes 8650752 | tf_op jit(solution)/shard_map/base_projections/dot_general | solution.py:411
  34.0 33.4 %all-to-all-done.source = bf16[4,4,256,512]{3,2,1,0:T(8,128)(2,1)} async-done(((bf16[4,4,256,512]{3,2,1,0:T(8,128)(2,1)}), bf16[4,4,256,512]{3,2,1,0:T(8,128)(2,1)}, u32[]{:S(2)}, u32[]{:S(2)}) %all-to-all-start) | async-done | bytes 4194336 | tf_op jit(solution)/shard_map/columns_of_w_out/all_to_all | solution.py:407
  67.7 0.7 fusion
  68.4 12.3 %all-gather.5.cloned.1.call-done = bf16[11264,512]{1,0:T(8,128)(2,1)} async-done(((bf16[704,512]{1,0:T(8,128)(2,1)}), bf16[11264,512]{1,0:T(8,128)(2,1)}) %all-gather.5.cloned.1.call-update) | async-done | bytes 11534352 | tf_op jit(solution)/shard_map/gather_in_maps/all_gather | solution.py:364
  80.7 3.7 %shrink.1 = bf16[16,48,256]{2,1,0:T(8,128)(2,1)} custom-call(s32[25]{0:T(128)} %pad_add_fusion.1.index, bf16[16,704,512]{2,1,0:T(8,128)(2,1)} %bitcast.17, bf16[13,48,512]{2,1,0:T(8,128)(2,1)} %slot.1, bf16[512,256]{1,0:T(8,128)(2,1)} %bitcast.19, s32[1,256]{1,0:T(1,128)} %bitcast.15), custom_call_target="tpu_custom_call" | custom-call | flops 314572800 | bytes 2097152 | tf_op jit(solution)/shard_map/shrink/shrink/pallas_call | solution.py:429
  84.5 6.9 %all-to-all-start.1 = ((bf16[16,48,256]{2,1,0:T(8,128)(2,1)}), bf16[16,48,256]{2,1,0:T(8,128)(2,1)S(1)}, u32[]{:S(2)}, u32[]{:S(2)}) async-start(bf16[16,48,256]{2,1,0:T(8,128)(2,1)} %shrink.1), calls=%async_computation.1 | async-start | bytes 786432 | tf_op jit(solution)/shard_map/shrink/all_to_all | solution.py:444
  91.6 0.1 copy.43.block
  91.8 2.4 %pick_up.1 = (bf16[400,256]{1,0:T(8,128)(2,1)S(1)}, bf16[400,512]{1,0:T(8,128)(2,1)S(1)}) custom-call(s32[25]{0:T(128)S(1)} %copy-done.8, bf16[16,704,512]{2,1,0:T(8,128)(2,1)} %bitcast.18, bf16[13,16,256]{2,1,0:T(8,128)(2,1)S(1)} %copy-done.3, bf16[13,16,32]{2,1,0:T(8,128)(2,1)S(1)} %copy-done.5, bf16[13,16,32]{2,1,0:T(8,128)(2,1)S(1)} %copy-done.6), custom_call_target="tpu_custom_call" | custom-call | bytes 2097152 | tf_op jit(solution)/shard_map/project/pick_up/pallas_call | solution.py:447
  94.2 7.7 %all-to-all-done.1.parts = bf16[16,48,256]{2,1,0:T(8,128)(2,1)S(1)} async-done(((bf16[16,48,256]{2,1,0:T(8,128)(2,1)}), bf16[16,48,256]{2,1,0:T(8,128)(2,1)S(1)}, u32[]{:S(2)}, u32[]{:S(2)}) %all-to-all-start.1) | async-done | bytes 393248 | tf_op jit(solution)/shard_map/shrink/all_to_all | solution.py:444
  101.9 0.7 project.1
  102.6 11.6 %all_to_all.25.received = bf16[16,16,320]{2,1,0:T(8,128)(2,1)} all-to-all(bf16[16,16,320]{2,1,0:T(8,128)(2,1)S(1)} %project.1), channel_id=1, replica_groups=mesh['group'=16,'y'=4,'x'=4] {'y','x'}, dimensions={0} | all-to-all | bytes 327680 | tf_op jit(solution)/shard_map/attend/all_to_all | solution.py:471
  114.3 8.9 %attend.1 = bf16[16,4,16,256]{3,2,1,0:T(8,128)(2,1)} custom-call(s32[8]{0:T(128)} %lengths.1, bf16[16,16,320]{2,1,0:T(8,128)(2,1)} %all_to_all.25.received, bf16[8,512,512]{2,1,0:T(8,128)(2,1)} %keys.1, bf16[8,512,512]{2,1,0:T(8,128)(2,1)} %values.1), custom_call_target="tpu_custom_call" | custom-call | flops 536870912 | bytes 12582912 | tf_op jit(solution)/shard_map/attend/attend/pallas_call | solution.py:472
  123.2 3.8 %all-to-all-start.3 = ((bf16[16,4,16,256]{3,2,1,0:T(8,128)(2,1)}), bf16[16,4,16,256]{3,2,1,0:T(8,128)(2,1)S(1)}, u32[]{:S(2)}, u32[]{:S(2)}) async-start(bf16[16,4,16,256]{3,2,1,0:T(8,128)(2,1)} %attend.1), calls=%async_computation.3 | async-start | bytes 1048576 | tf_op jit(solution)/shard_map/attend/all_to_all | solution.py:490
  127.2 2.3 %copy-done.1 = bf16[192,16,768]{2,1,0:T(8,128)(2,1)S(1)} copy-done((bf16[192,16,768]{2,1,0:T(8,128)(2,1)S(1)}, bf16[192,16,768]{2,1,0:T(8,128)(2,1)}, u32[]{:S(2)}) %copy-start.1) | copy-done | bytes 4718616
  129.6 1.6 pick.1
  131.1 5.7 %all-to-all-done.3.attended = bf16[16,4,16,256]{3,2,1,0:T(8,128)(2,1)S(1)} async-done(((bf16[16,4,16,256]{3,2,1,0:T(8,128)(2,1)}), bf16[16,4,16,256]{3,2,1,0:T(8,128)(2,1)S(1)}, u32[]{:S(2)}, u32[]{:S(2)}) %all-to-all-start.3) | async-done | bytes 524320 | tf_op jit(solution)/shard_map/attend/all_to_all | solution.py:490
  136.9 3.5 %base_out.1 = (bf16[16,16,256]{2,1,0:T(8,128)(2,1)S(1)}, bf16[256,512]{1,0:T(8,128)(2,1)S(1)}, bf16[256,512]{1,0:T(8,128)(2,1)S(1)}, bf16[256,512]{1,0:T(8,128)(2,1)S(1)}, f32[256,512]{1,0:T(8,128)S(1)}) custom-call(s32[1]{0:T(128)} %bitcast.place, s32[1]{0:T(128)} %bitcast.1.member, bf16[16,4,16,256]{3,2,1,0:T(8,128)(2,1)S(1)} %all-to-all-done.3.attended, ...), custom_call_target="tpu_custom_call" | custom-call | flops 1073741824 | bytes 5242880 | tf_op jit(solution)/shard_map/output/base_out/pallas_call | solution.py:509
  140.5 2.3 %collective-permute-start.1 = (bf16[256,512]{1,0:T(8,128)(2,1)S(1)}, bf16[256,512]{1,0:T(8,128)(2,1)S(1)}, u32[]{:S(2)}, u32[]{:S(2)}) collective-permute-start(bf16[256,512]{1,0:T(8,128)(2,1)S(1)} %get-tuple-element.40), channel_id=1, source_target_pairs={{0,8},{4,12},{8,0},{12,4},{1,9},{5,13},{9,1},{13,5},{2,10},{6,14},... | collective-permute-start | bytes 786440 | tf_op jit(solution)/shard_map/output/ppermute | solution.py:522
  142.7 1.1 collective-permute-start.2
  143.9 12.1 %all_to_all.26.parts = bf16[16,16,256]{2,1,0:T(8,128)(2,1)S(1)} all-to-all(bf16[16,16,256]{2,1,0:T(8,128)(2,1)S(1)} %get-tuple-element.37), channel_id=1, replica_groups=mesh['group'=16,'y'=4,'x'=4] {'y','x'}, dimensions={0} | all-to-all | bytes 262144 | tf_op jit(solution)/shard_map/output/all_to_all | solution.py:520
  156.0 1.1 final.1
  (60 shorter events, 1.3 us)
Async XLA Ops:
  6.5 16.2 %copy-start = (bf16[8192,32]{0,1:T(8,128)(2,1)S(1)}, bf16[8192,32]{0,1:T(8,128)(2,1)}, u32[]{:S(2)}) copy-start(bf16[8192,32]{0,1:T(8,128)(2,1)} %param.26) | copy-start | bytes 1572868
  6.5 74.2 %all-gather.5.cloned.1.call-start = ((), (), s32[]{:S(2)}) async-start(), calls=%async_computation.5 | async-start | bytes 12255232 | tf_op jit(solution)/shard_map/gather_in_maps/all_gather | solution.py:364
  13.2 5.1 %copy-start.12 = (s32[2,192]{1,0:T(2,128)S(1)}, s32[2,192]{1,0:T(2,128)}, u32[]{:S(2)}) copy-start(s32[2,192]{1,0:T(2,128)} %param.34) | copy-start | bytes 4612
  13.2 5.1 %copy-start.13 = (s32[192]{0:T(256)S(1)}, s32[192]{0:T(256)}, u32[]{:S(2)}) copy-start(s32[192]{0:T(256)} %param.35) | copy-start | bytes 2308
  13.2 7.4 %copy-start.15 = (s32[2,192]{1,0:T(2,128)S(1)}, s32[2,192]{1,0:T(2,128)}, u32[]{:S(2)}) copy-start(s32[2,192]{1,0:T(2,128)} %param.33) | copy-start | bytes 4612
  13.2 54.1 %all-to-all-start = ((bf16[4,4,256,512]{3,2,1,0:T(8,128)(2,1)}), bf16[4,4,256,512]{3,2,1,0:T(8,128)(2,1)}, u32[]{:S(2)}, u32[]{:S(2)}) async-start(bf16[4,4,256,512]{3,2,1,0:T(8,128)(2,1)} %split.1), calls=%async_computation | async-start | bytes 8388608 | tf_op jit(solution)/shard_map/columns_of_w_out/all_to_all | solution.py:407
  18.2 8.7 %copy-start.16 = (bf16[8192,32]{0,1:T(8,128)(2,1)S(1)}, bf16[8192,32]{0,1:T(8,128)(2,1)}, u32[]{:S(2)}) copy-start(bf16[8192,32]{0,1:T(8,128)(2,1)} %param.27) | copy-start | bytes 1572868
  18.2 109.0 %all-gather.7.cloned.1.call-start = ((), (), s32[]{:S(2)}) async-start(), calls=%async_computation.6 | async-start | bytes 5013504 | tf_op jit(solution)/shard_map/gather_out_maps/all_gather | solution.py:426
  22.0 4.9 %copy-start.11 = (bf16[2,128,8192]{2,1,0:T(8,128)(2,1)S(1)}, bf16[2,128,8192]{2,1,0:T(8,128)(2,1)}, u32[]{:S(2)}) copy-start(bf16[2,128,8192]{2,1,0:T(8,128)(2,1)} %param.24) | copy-start | bytes 12582916
  22.7 5.6 %copy-start.9 = (bf16[12,16,512]{2,1,0:T(8,128)(2,1)S(1)}, bf16[12,16,512]{2,1,0:T(8,128)(2,1)}, u32[]{:S(2)}) copy-start(bf16[12,16,512]{2,1,0:T(8,128)(2,1)} %param.41) | copy-start | bytes 589828
  22.7 5.6 %copy-start.10 = (bf16[12,16,256]{2,1,0:T(8,128)(2,1)S(1)}, bf16[12,16,256]{2,1,0:T(8,128)(2,1)}, u32[]{:S(2)}) copy-start(bf16[12,16,256]{2,1,0:T(8,128)(2,1)} %param.40) | copy-start | bytes 294916
  29.0 38.7 %copy-start.14 = (s32[2,128]{1,0:T(2,128)S(1)}, s32[2,128]{1,0:T(2,128)}, u32[]{:S(2)}) copy-start(s32[2,128]{1,0:T(2,128)} %param.32) | copy-start | bytes 3076
  80.7 10.8 %copy-start.7 = (s32[2,128]{1,0:T(2,128)S(1)}, s32[2,128]{1,0:T(2,128)}, u32[]{:S(2)}) copy-start(s32[2,128]{1,0:T(2,128)} %fusion) | copy-start | bytes 3076
  80.7 11.0 %copy-start.3 = (bf16[13,16,256]{2,1,0:T(8,128)(2,1)S(1)}, bf16[13,16,256]{2,1,0:T(8,128)(2,1)}, u32[]{:S(2)}) copy-start(bf16[13,16,256]{2,1,0:T(8,128)(2,1)} %slot_q.1) | copy-start | bytes 319492
  80.7 11.0 %copy-start.5 = (bf16[13,16,32]{2,1,0:T(8,128)(2,1)S(1)}, bf16[13,16,32]{2,1,0:T(8,128)(2,1)}, u32[]{:S(2)}) copy-start(bf16[13,16,32]{2,1,0:T(8,128)(2,1)} %slot_k.1) | copy-start | bytes 39940
  80.7 11.0 %copy-start.6 = (bf16[13,16,32]{2,1,0:T(8,128)(2,1)S(1)}, bf16[13,16,32]{2,1,0:T(8,128)(2,1)}, u32[]{:S(2)}) copy-start(bf16[13,16,32]{2,1,0:T(8,128)(2,1)} %slot_v.1) | copy-start | bytes 39940
  80.7 11.1 %copy-start.8 = (s32[25]{0:T(128)S(1)}, s32[25]{0:T(128)}, u32[]{:S(2)}) copy-start(s32[25]{0:T(128)} %pad_add_fusion.1.index) | copy-start | bytes 304
  84.5 17.4 %all-to-all-start.1 = ((bf16[16,48,256]{2,1,0:T(8,128)(2,1)}), bf16[16,48,256]{2,1,0:T(8,128)(2,1)S(1)}, u32[]{:S(2)}, u32[]{:S(2)}) async-start(bf16[16,48,256]{2,1,0:T(8,128)(2,1)} %shrink.1), calls=%async_computation.1 | async-start | bytes 786432 | tf_op jit(solution)/shard_map/shrink/all_to_all | solution.py:444
  114.3 13.0 %copy-start.2 = (bf16[13,16,512]{2,1,0:T(8,128)(2,1)S(1)}, bf16[13,16,512]{2,1,0:T(8,128)(2,1)}, u32[]{:S(2)}) copy-start(bf16[13,16,512]{2,1,0:T(8,128)(2,1)} %slot_up.1) | copy-start | bytes 638980
  114.3 13.0 %copy-start.4 = (bf16[13,16,256]{2,1,0:T(8,128)(2,1)S(1)}, bf16[13,16,256]{2,1,0:T(8,128)(2,1)}, u32[]{:S(2)}) copy-start(bf16[13,16,256]{2,1,0:T(8,128)(2,1)} %slot_in.1) | copy-start | bytes 319492
  123.2 13.7 %all-to-all-start.3 = ((bf16[16,4,16,256]{3,2,1,0:T(8,128)(2,1)}), bf16[16,4,16,256]{3,2,1,0:T(8,128)(2,1)S(1)}, u32[]{:S(2)}, u32[]{:S(2)}) async-start(bf16[16,4,16,256]{3,2,1,0:T(8,128)(2,1)} %attend.1), calls=%async_computation.3 | async-start | bytes 1048576 | tf_op jit(solution)/shard_map/attend/all_to_all | solution.py:490
  127.2 2.3 %copy-start.1 = (bf16[192,16,768]{2,1,0:T(8,128)(2,1)S(1)}, bf16[192,16,768]{2,1,0:T(8,128)(2,1)}, u32[]{:S(2)}) copy-start(bf16[192,16,768]{2,1,0:T(8,128)(2,1)} %all-gather.7.cloned.1.call-done.pool) | copy-start | bytes 14155780
  140.4 15.7 %collective-permute-start = (bf16[256,512]{1,0:T(8,128)(2,1)S(1)}, bf16[256,512]{1,0:T(8,128)(2,1)S(1)}, u32[]{:S(2)}, u32[]{:S(2)}) collective-permute-start(bf16[256,512]{1,0:T(8,128)(2,1)S(1)} %get-tuple-element.39), channel_id=1, source_target_pairs={{0,4},{4,8},{8,12},{12,0},{1,5},{5,9},{9,13},{13,1},{2,6},{6,10},{... | collective-permute-start | bytes 786440 | tf_op jit(solution)/shard_map/output/ppermute | solution.py:522
  140.5 15.6 %collective-permute-start.1 = (bf16[256,512]{1,0:T(8,128)(2,1)S(1)}, bf16[256,512]{1,0:T(8,128)(2,1)S(1)}, u32[]{:S(2)}, u32[]{:S(2)}) collective-permute-start(bf16[256,512]{1,0:T(8,128)(2,1)S(1)} %get-tuple-element.40), channel_id=1, source_target_pairs={{0,8},{4,12},{8,0},{12,4},{1,9},{5,13},{9,1},{13,5},{2,10},{6,14},... | collective-permute-start | bytes 786440 | tf_op jit(solution)/shard_map/output/ppermute | solution.py:522
  142.7 13.3 %collective-permute-start.2 = (bf16[256,512]{1,0:T(8,128)(2,1)S(1)}, bf16[256,512]{1,0:T(8,128)(2,1)S(1)}, u32[]{:S(2)}, u32[]{:S(2)}) collective-permute-start(bf16[256,512]{1,0:T(8,128)(2,1)S(1)} %get-tuple-element.41), channel_id=1, source_target_pairs={{0,12},{4,0},{8,4},{12,8},{1,13},{5,1},{9,5},{13,9},{2,14},{6,2},{... | collective-permute-start | bytes 786440 | tf_op jit(solution)/shard_map/output/ppermute | solution.py:522
Sparse Core Ops, SparseCore 0:
  9.2 71.4 all-gather.4
  82.5 42.5 all-gather.6
